TPU v7x, 32 devices: a whole 2x2x4 slice. The times are simulated.
32 devices in a mesh: row: 4 (over y, x), col: 8 (over z, core).
Axes of the slice: x: 2, y: 2, z: 4, core: 2. Of those that a mesh axis runs over, the one named last changes fastest.
Arguments:
- row_emb: float32 [16, 512, 256], P('row', 'col'), may hold values from -1.8 to 1.8
- col_emb: float32 [32, 512, 256], P('col', 'row'), may hold values from -1.8 to 1.8
- row_marg: bfloat16 [16, 512], P('row', 'col'), may hold values from 0.5 to 3
- col_marg: bfloat16 [32, 512], P('col', 'row'), may hold values from 0.5 to 3
- tile_list: int32 [4, 8, 8, 2], P('row', 'col'), may hold values from 0 to 31, as said below
- tile_count: int32 [4, 8], P('row', 'col'), may hold values from 1 to 8, as said below
- tile_data: int32 [4, 8, 8, 512, 512], P('row', 'col'), may hold values from 0 to 215
Outputs:
- row_new: float32 [16, 512, 256], P('row', 'col')
- col_new: float32 [32, 512, 256], P('col', 'row')
Inputs may be any that keep to these rules, and one draw needn't show every extreme that they name: `tile_list`: the slots of device (r, c) name distinct tiles with row block in r * 4 to (r + 1) * 4 - 1 and column block in c * 4 to (c + 1) * 4 - 1; slots at or past the device's tile_count are not used. `tile_count`: some device uses all 8 slots.
All inputs are finite; a program needn't handle non-finite values.
Results may differ from a plain program's by a relative error of at most 0.012.
Values may be sent and summed in bfloat16 or wider, within the bound.
No kernel may reach another device: no remote copies, remote signals or barrier semaphores. Data moves between devices by JAX's collectives and lax.ppermute only.
A program may use at most 64 MiB of HBM per device.

v0:
```python
import functools

import jax
import jax.numpy as jnp
from jax import lax
from jax.experimental import pallas as pl
from jax.experimental.pallas import tpu as pltpu
from jax.sharding import PartitionSpec as P

RATE = 0.0004
MARG_ROWS = 16
MARG_LANES = 128
ANY = pl.BlockSpec(memory_space=pl.ANY)
HBM = pl.BlockSpec(memory_space=pltpu.HBM)
VMEM = pl.BlockSpec(memory_space=pltpu.VMEM)
SMEM = pl.BlockSpec(memory_space=pltpu.SMEM)
SMALL = 12 << 20
LARGE = 32 << 20
LEVELS = 35 << 20
PACK = 62 << 20
f32, bf16 = jnp.float32, jnp.bfloat16
shape = jax.ShapeDtypeStruct


def cost(flops, moved):
    return pl.CostEstimate(flops=flops, bytes_accessed=moved, transcendentals=0)


def pack_kernel(row_emb, row_marg, col_emb, col_marg, row_out, col_out, *scratch):
    bufs, sem = scratch[:4], scratch[4]
    copies = [
        pltpu.make_async_copy(src, dst, sem.at[n])
        for n, (src, dst) in enumerate(zip((row_emb, row_marg, col_emb, col_marg), bufs))
    ]
    for copy in copies:
        copy.start()
    for n, out in enumerate((row_out, col_out)):
        copies[2 * n].wait()
        copies[2 * n + 1].wait()
        emb, marg = bufs[2 * n], bufs[2 * n + 1]
        blocks, part, width = emb.shape
        out[: blocks * part, :] = emb[...].astype(bf16).reshape(blocks * part, width)
        out[blocks * part :, :] = jnp.zeros((MARG_ROWS, width), bf16)
        for b in range(blocks):
            out[blocks * part + b : blocks * part + b + 1, :part] = marg[b : b + 1, :]


def pack(row_emb, row_marg, col_emb, col_marg):
    args = (row_emb, row_marg, col_emb, col_marg)
    return pl.pallas_call(
        pack_kernel,
        out_shape=[
            shape((e.shape[0] * e.shape[1] + MARG_ROWS, e.shape[2]), bf16) for e in args[::2]
        ],
        in_specs=[ANY] * 4,
        out_specs=[VMEM] * 2,
        scratch_shapes=[pltpu.VMEM(x.shape, x.dtype) for x in args]
        + [pltpu.SemaphoreType.DMA((4,))],
        compiler_params=pltpu.CompilerParams(vmem_limit_bytes=PACK),
        cost_estimate=cost(0, 1 << 20),
    )(*args)


def levels_kernel(used, tiles, logs, weights, token, tile_buf, sem):
    count = used[0]
    slots, size, _ = tile_buf.shape
    chunk = 64

    def load(slot):
        return pltpu.make_async_copy(tiles.at[slot], tile_buf.at[slot], sem.at[slot])

    for slot in range(slots):

        @pl.when(slot < count)
        def _():
            load(slot).start()

    token[...] = jnp.zeros_like(token)

    def one_tile(slot, carry):
        load(slot).wait()

        def one_chunk(n, carry):
            rows = pl.ds(pl.multiple_of(n * chunk, chunk), chunk)
            counts = tile_buf[slot, rows, :].astype(f32)
            level = jnp.maximum(counts, 1.0)
            logs[slot, rows, :] = jnp.log(level)
            weight = 0.1 + 0.25 * (level * lax.rsqrt(level))
            weights[slot, rows, :] = jnp.where(counts > 0.0, weight, 0.0)
            return carry

        lax.fori_loop(0, size // chunk, one_chunk, 0)
        return carry

    lax.fori_loop(0, count, one_tile, 0)


def levels(used, tiles):
    return pl.pallas_call(
        levels_kernel,
        out_shape=[shape(tiles.shape, f32)] * 2 + [shape((8, 128), f32)],
        in_specs=[SMEM, HBM],
        out_specs=[VMEM] * 3,
        scratch_shapes=[
            pltpu.VMEM(tiles.shape, jnp.int32),
            pltpu.SemaphoreType.DMA((tiles.shape[0],)),
        ],
        compiler_params=pltpu.CompilerParams(vmem_limit_bytes=LEVELS),
        cost_estimate=cost(0, 24 << 20),
    )(used, tiles)


def join_kernel(n_parts, *refs):
    out = refs[-1]
    for n in range(n_parts):
        out[n] = refs[n][...]


def join(parts, afters):
    return pl.pallas_call(
        functools.partial(join_kernel, len(parts)),
        out_shape=shape((len(parts), *parts[0].shape), parts[0].dtype),
        in_specs=[VMEM] * len(parts) + [ANY] * len(afters),
        out_specs=VMEM,
        compiler_params=pltpu.CompilerParams(vmem_limit_bytes=SMALL),
        cost_estimate=cost(0, 1 << 20),
    )(*parts, *afters)


def marg_table(pieces, owners, part, size):
    table = jnp.zeros((MARG_ROWS, size), f32)
    for piece, owner in zip(pieces, owners):
        tail = piece[piece.shape[0] - MARG_ROWS :, :MARG_LANES]
        k = lax.broadcasted_iota(jnp.int32, (MARG_LANES, size), 0)
        at = lax.broadcasted_iota(jnp.int32, (MARG_LANES, size), 1)
        place = ((at == k + owner * part) & (k < part)).astype(bf16)
        table += jnp.dot(tail, place, preferred_element_type=f32)
    return table


def work_kernel(first, n_row, n_col, row_owner, col_owner, *refs):
    refs = list(refs)

    def take(n):
        return [refs.pop(0) for _ in range(n)]

    listing, used, logs, weights, row_near, row_far = take(6)
    col_in = take(n_col)
    if not first:
        left, right = take(2)
    keep, swap = take(2)
    col_out = take(n_col)
    if first:
        left, right = take(2)
    row_panel, row_turned, col_panel, grad_row, grad_turned, grad_col, scores, signal = take(8)

    row_blocks, size, width = row_panel.shape
    col_blocks = col_panel.shape[0]
    row_part, col_part = size // n_row, size // n_col
    half = n_row // 2
    me_row, me_col = lax.axis_index("row"), lax.axis_index("col")
    row_owners = [me_col ^ k for k in row_owner]
    col_owners = [me_row ^ k for k in col_owner]
    row_zero, col_zero = me_row * row_blocks, me_col * col_blocks
    count = used[0]
    row_in = [side.at[n] for side in (row_near, row_far) for n in range(half)]

    for pieces, owners, panel, part in (
        (row_in, row_owners, row_panel, row_part),
        (col_in, col_owners, col_panel, col_part),
    ):
        for piece, owner in zip(pieces, owners):
            start = pl.multiple_of(owner * part, part)
            for b in range(panel.shape[0]):
                panel[b, pl.ds(start, part), :] = piece[b * part : (b + 1) * part, :]
    for b in range(row_blocks):
        row_turned[b] = row_panel[b].T
    grad_row[...] = jnp.zeros_like(grad_row)
    grad_turned[...] = jnp.zeros_like(grad_turned)

    if first:
        row_table = marg_table(row_in, row_owners, row_part, size).astype(bf16)
        for b in range(row_blocks):
            pick = (lax.broadcasted_iota(jnp.int32, (MARG_ROWS, 128), 0) == b).astype(bf16)
            left[b] = lax.dot_general(
                row_table, pick, (((0,), (0,)), ((), ())), preferred_element_type=f32
            )
        col_table = marg_table(col_in, col_owners, col_part, size)
        for b in range(col_blocks):
            right[b] = jnp.broadcast_to(col_table[b : b + 1, :], right.shape[1:])

    chunks = [slice(at, at + 256) for at in range(0, size, 256)]

    def place(slot):
        return listing[0, slot] - row_zero, listing[1, slot] - col_zero

    def make_scores(slot, rows):
        i, j = place(slot)
        scores[rows, :] = lax.dot_general(
            row_panel[i, rows, :], col_panel[j], (((1,), (1,)), ((), ())), preferred_element_type=f32
        )

    def make_signal(slot, rows):
        i, j = place(slot)
        marg_left = jnp.concatenate([left[i, rows, :]] * (size // 128), axis=1)
        diff = scores[rows, :] + marg_left + right[j, 0:1, :] - logs[slot, rows, :]
        weight = weights[slot, rows, :]
        flat = 0.5 * jnp.tanh(0.5 * diff) + 0.5
        signal[rows, :] = jnp.where(weight > 0.0, weight * diff, flat).astype(bf16)

    def add_grads(slot, rows):
        i, j = place(slot)
        piece = signal[rows, :]
        grad_row[i, rows, :] += jnp.dot(piece, col_panel[j], preferred_element_type=f32)
        grad_turned[j] += jnp.dot(row_turned[i, :, rows], piece, preferred_element_type=f32)

    def one_tile(slot, carry):
        for rows in chunks:
            add_grads(slot - 1, rows)
            make_signal(slot, rows)
            make_scores(jnp.minimum(slot + 1, count - 1), rows)
        return carry

    for rows in chunks:
        make_scores(0, rows)
    for rows in chunks:
        make_signal(0, rows)
        make_scores(jnp.minimum(1, count - 1), rows)
    lax.fori_loop(1, count, one_tile, 0)
    for rows in chunks:
        add_grads(count - 1, rows)

    for n in range(n_row):
        place, sibling = row_owner[n] >> 1, row_owner[n] & 1
        start = pl.multiple_of(row_owners[n] * row_part, row_part)
        piece = grad_row[:, pl.ds(start, row_part), :]
        if sibling:
            swap[place] = piece.astype(bf16)
        else:
            keep[place] = piece
    for b in range(col_blocks):
        grad_col[b] = grad_turned[b].astype(bf16).T
    for n in range(n_col):
        start = pl.multiple_of(col_owners[n] * col_part, col_part)
        col_out[n][...] = grad_col[:, pl.ds(start, col_part), :]


def work(listing, used, tabs, row_near, row_far, col_in, tables, row_owner, col_owner, dims):
    row_blocks, col_blocks, size, width = dims
    first = tables is None
    n_row, n_col = len(row_owner), len(col_owner)
    row_part, col_part = size // n_row, size // n_col
    half = n_row // 2
    outs = [
        shape((half, row_blocks, row_part, width), f32),
        shape((half, row_blocks, row_part, width), bf16),
    ] + [shape((col_blocks, col_part, width), bf16)] * n_col
    if first:
        outs += [shape((row_blocks, size, 128), f32), shape((col_blocks, 8, size), f32)]
    args = [listing, used, *tabs, row_near, row_far, *col_in] + ([] if first else list(tables))
    res = pl.pallas_call(
        functools.partial(work_kernel, first, n_row, n_col, row_owner, col_owner),
        out_shape=outs,
        in_specs=[SMEM, SMEM] + [VMEM] * (len(args) - 2),
        out_specs=[VMEM] * len(outs),
        scratch_shapes=[
            pltpu.VMEM((row_blocks, size, width), bf16),
            pltpu.VMEM((row_blocks, width, size), bf16),
            pltpu.VMEM((col_blocks, size, width), bf16),
            pltpu.VMEM((row_blocks, size, width), f32),
            pltpu.VMEM((col_blocks, width, size), f32),
            pltpu.VMEM((col_blocks, size, width), bf16),
            pltpu.VMEM((size, size), f32),
            pltpu.VMEM((size, size), bf16),
        ],
        compiler_params=pltpu.CompilerParams(vmem_limit_bytes=LARGE),
        cost_estimate=cost(8 * 6 * size * size * width, 16 << 20),
    )(*args)
    return res[0], res[1], res[2 : 2 + n_col], res[2 + n_col :]


def merge_kernel(kept, keep, got, *outs):
    for n, out in enumerate(outs):
        out[...] = (keep[n] + got[n].astype(f32)).astype(out.dtype)


def merge(keep, got, kept):
    n, *piece = keep.shape
    return pl.pallas_call(
        functools.partial(merge_kernel, kept),
        out_shape=[shape(tuple(piece), f32 if k in kept else bf16) for k in range(n)],
        in_specs=[VMEM] * 2,
        out_specs=[VMEM] * n,
        compiler_params=pltpu.CompilerParams(vmem_limit_bytes=SMALL),
        cost_estimate=cost(0, 2 << 20),
    )(keep, got)


def add_kernel(*refs):
    total = refs[0][...]
    for ref in refs[1:-1]:
        total += ref[...].astype(f32)
    refs[-1][...] = total.astype(bf16)


def add(own, parts):
    return pl.pallas_call(
        add_kernel,
        out_shape=shape(own.shape, bf16),
        in_specs=[VMEM] * (1 + len(parts)),
        out_specs=VMEM,
        compiler_params=pltpu.CompilerParams(vmem_limit_bytes=SMALL),
        cost_estimate=cost(0, 1 << 20),
    )(own, *parts)


def update_kernel(n_row, n_col, row_emb, col_emb, *refs):
    row_parts, col_parts, outs = refs[:n_row], refs[n_row : n_row + n_col], refs[n_row + n_col :]
    for n, (emb, parts) in enumerate(((row_emb, row_parts), (col_emb, col_parts))):
        total = parts[0][...].astype(f32)
        for part in parts[1:]:
            total += part[...].astype(f32)
        new = emb[...] - RATE * total
        outs[n][...] = new
        if len(outs) > 2:
            outs[2 + n][...] = new.astype(bf16).reshape(outs[2 + n].shape)


def update(row_emb, col_emb, row_parts, col_parts, last):
    embs = (row_emb, col_emb)
    outs = [shape(e.shape, f32) for e in embs]
    if not last:
        outs += [shape((e.shape[0] * e.shape[1], e.shape[2]), bf16) for e in embs]
    return pl.pallas_call(
        functools.partial(update_kernel, len(row_parts), len(col_parts)),
        out_shape=outs,
        in_specs=[VMEM] * (2 + len(row_parts) + len(col_parts)),
        out_specs=[VMEM] * len(outs),
        compiler_params=pltpu.CompilerParams(vmem_limit_bytes=SMALL),
        cost_estimate=cost(0, 2 << 20),
    )(row_emb, col_emb, *row_parts, *col_parts)


def send(x, axis, count, mask):
    return lax.ppermute(x, axis, [(k, k ^ mask) for k in range(count)])


def shards(n_row_dev, n_col_dev, row_emb, col_emb, row_marg, col_marg, tile_list, tile_count, tile_data):
    listing = tile_list[0, 0].T
    used = tile_count[0]
    tiles = tile_data[0, 0]
    dims = (row_emb.shape[0], col_emb.shape[0], tiles.shape[-1], row_emb.shape[-1])
    half = n_col_dev // 2
    far = half // 2
    near = range(1, far)
    row_owner = [2 * k for k in range(half)] + [2 * k + 1 for k in range(half)]
    col_owner = list(range(n_row_dev))

    def hop(x, distance):
        return send(x, "col", n_col_dev, 2 * distance)

    row_pay, col_pay = pack(row_emb, row_marg, col_emb, col_marg)
    *tabs, made_tabs = levels(used, tiles)
    tables = None
    for substep in range(2):
        crossed = hop(row_pay, far)
        row_near = [row_pay] + [hop(row_pay, k) for k in near] + [crossed] + [hop(crossed, k) for k in near]
        col_in = [col_pay] + [send(col_pay, "row", n_row_dev, k) for k in col_owner[1:]]
        row_near = join(row_near, col_in[1:] + ([made_tabs] if substep == 0 else []))
        row_far = send(row_near, "col", n_col_dev, 1)
        keep, swap, col_out, made = work(
            listing, used, tabs, row_near, row_far, col_in, tables, row_owner, col_owner, dims
        )
        tables = tables or made
        merged = merge(keep, send(swap, "col", n_col_dev, 1), (0, far))
        crossing = add(merged[far], [hop(merged[far + k], k) for k in near])
        col_parts = [col_out[0]] + [send(col_out[k], "row", n_row_dev, k) for k in col_owner[1:]]
        row_parts = [merged[0], hop(crossing, far)] + [hop(merged[k], k) for k in near]
        if substep == 0:
            row_emb, col_emb, row_pay, col_pay = update(row_emb, col_emb, row_parts, col_parts, False)
    return tuple(update(row_emb, col_emb, row_parts, col_parts, True))


def solution(mesh):
    placed = (
        P("row", "col", None),
        P("col", "row", None),
        P("row", "col"),
        P("col", "row"),
        P("row", "col", None, None),
        P("row", "col"),
        P("row", "col", None, None, None),
    )
    return jax.shard_map(
        functools.partial(shards, mesh.shape["row"], mesh.shape["col"]),
        mesh=mesh,
        in_specs=placed,
        out_specs=(P("row", "col", None), P("col", "row", None)),
        check_vma=False,
    )
```

profile of v0, /device:TPU:0, one launch (start us, length us, event | category | flops | bytes accessed | tf_op | source)
XLA Modules:
  0.0 87.2 jit_solution(5486123996780690552)
XLA Ops:
  0.6 1.9 %shard_map.87 = (bf16[272,256]{1,0:T(8,128)(2,1)}, bf16[528,256]{1,0:T(8,128)(2,1)}) custom-call(f32[4,64,256]{2,1,0:T(8,128)} %row_emb.3, bf16[4,64]{1,0:T(4,128)(2,1)} %row_marg.1, f32[4,128,256]{2,1,0:T(8,128)} %col_emb.3, bf16[4,128]{1,0:T(4,128)(2,1)} %col_marg.1), custom_call_target="tpu_custom_call" | custom-call | bytes 1048576 | tf_op jit(solution)/shard_map/pallas_call | solution.py:50
  2.6 4.1 %collective-permute-start.1 = (bf16[272,256]{1,0:T(8,128)(2,1)}, bf16[272,256]{1,0:T(8,128)(2,1)S(1)}, u32[]{:S(2)}, u32[]{:S(2)}) collective-permute-start(bf16[272,256]{1,0:T(8,128)(2,1)} %get-tuple-element.35.refs_0_), channel_id=1, source_target_pairs={{0,4},{1,5},{2,6},{3,7},{4,0},{5,1},{6,2},{7,3},{8,12},{9,13},{10,... | collective-permute-start | bytes 417800 | tf_op jit(solution)/shard_map/ppermute | solution.py:345
  6.7 2.4 %collective-permute-start.5 = (bf16[528,256]{1,0:T(8,128)(2,1)}, bf16[528,256]{1,0:T(8,128)(2,1)S(1)}, u32[]{:S(2)}, u32[]{:S(2)}) collective-permute-start(bf16[528,256]{1,0:T(8,128)(2,1)} %get-tuple-element.36.refs_6_), channel_id=1, source_target_pairs={{0,24},{8,16},{16,8},{24,0},{1,25},{9,17},{17,9},{25,1},{2,26},{10... | collective-permute-start | bytes 811016 | tf_op jit(solution)/shard_map/ppermute | solution.py:345
  11.8 1.9 %collective-permute-done.1.refs_2_ = bf16[272,256]{1,0:T(8,128)(2,1)S(1)} collective-permute-done((bf16[272,256]{1,0:T(8,128)(2,1)}, bf16[272,256]{1,0:T(8,128)(2,1)S(1)}, u32[]{:S(2)}, u32[]{:S(2)}) %collective-permute-start.1) | collective-permute-done | bytes 139296 | tf_op jit(solution)/shard_map/ppermute | solution.py:345
  17.3 4.3 %collective-permute-done.4.refs_5_.refs_8_ = bf16[528,256]{1,0:T(8,128)(2,1)S(1)} collective-permute-done((bf16[528,256]{1,0:T(8,128)(2,1)}, bf16[528,256]{1,0:T(8,128)(2,1)S(1)}, u32[]{:S(2)}, u32[]{:S(2)}) %collective-permute-start.4) | collective-permute-done | bytes 270368 | tf_op jit(solution)/shard_map/ppermute | solution.py:345
  21.8 1.9 %collective-permute-done.6.refs_5_ = bf16[4,272,256]{2,1,0:T(8,128)(2,1)S(1)} collective-permute-done((bf16[4,272,256]{2,1,0:T(8,128)(2,1)S(1)}, bf16[4,272,256]{2,1,0:T(8,128)(2,1)S(1)}, u32[]{:S(2)}, u32[]{:S(2)}) %collective-permute-start.6) | collective-permute-done | bytes 557088 | tf_op jit(solution)/shard_map/ppermute | solution.py:345
  23.7 2.8 %shard_map.89 = (f32[4,4,64,256]{3,2,1,0:T(8,128)S(1)}, bf16[4,4,64,256]{3,2,1,0:T(8,128)(2,1)S(1)}, bf16[4,128,256]{2,1,0:T(8,128)(2,1)S(1)}, bf16[4,128,256]{2...) custom-call(s32[2,8]{1,0:T(2,128)S(1)} %bitcast.8, ...), custom_call_target="tpu_custom_call" | custom-call | flops 3221225472 | bytes 16777216 | tf_op jit(solution)/shard_map/pallas_call | solution.py:261
  26.6 3.2 %collective-permute-start.7 = (bf16[4,4,64,256]{3,2,1,0:T(8,128)(2,1)S(1)}, bf16[4,4,64,256]{3,2,1,0:T(8,128)(2,1)S(1)}, u32[]{:S(2)}, u32[]{:S(2)}) collective-permute-start(bf16[4,4,64,256]{3,2,1,0:T(8,128)(2,1)S(1)} %get-tuple-element.39), channel_id=1, source_target_pairs={{0,1},{1,0},{2,3},{3,2},{4,5},{5,4},{6,7},{7,6},{8,9},{9,8},{10,11... | collective-permute-start | bytes 1572872 | tf_op jit(solution)/shard_map/ppermute | solution.py:345
  29.7 2.9 %collective-permute-start.12 = (bf16[4,128,256]{2,1,0:T(8,128)(2,1)S(1)}, bf16[4,128,256]{2,1,0:T(8,128)(2,1)S(1)}, u32[]{:S(2)}, u32[]{:S(2)}) collective-permute-start(bf16[4,128,256]{2,1,0:T(8,128)(2,1)S(1)} %get-tuple-element.46), channel_id=1, source_target_pairs={{0,16},{8,24},{16,0},{24,8},{1,17},{9,25},{17,1},{25,9},{2,18},{10... | collective-permute-start | bytes 786440 | tf_op jit(solution)/shard_map/ppermute | solution.py:345
  34.2 1.9 %collective-permute-start.10 = (bf16[4,64,256]{2,1,0:T(8,128)(2,1)S(1)}, bf16[4,64,256]{2,1,0:T(8,128)(2,1)S(1)}, u32[]{:S(2)}, u32[]{:S(2)}) collective-permute-start(bf16[4,64,256]{2,1,0:T(8,128)(2,1)S(1)} %get-tuple-element.43), channel_id=1, source_target_pairs={{0,2},{1,3},{2,0},{3,1},{4,6},{5,7},{6,4},{7,5},{8,10},{9,11},{10,... | collective-permute-start | bytes 393224 | tf_op jit(solution)/shard_map/ppermute | solution.py:345
  36.1 3.1 %collective-permute-done.8.refs_1_ = bf16[4,64,256]{2,1,0:T(8,128)(2,1)S(1)} collective-permute-done((bf16[4,64,256]{2,1,0:T(8,128)(2,1)S(1)}, bf16[4,64,256]{2,1,0:T(8,128)(2,1)S(1)}, u32[]{:S(2)}, u32[]{:S(2)}) %collective-permute-start.8) | collective-permute-done | bytes 131104 | tf_op jit(solution)/shard_map/ppermute | solution.py:345
  39.6 5.3 %collective-permute-done.12.refs_5_ = bf16[4,128,256]{2,1,0:T(8,128)(2,1)S(1)} collective-permute-done((bf16[4,128,256]{2,1,0:T(8,128)(2,1)S(1)}, bf16[4,128,256]{2,1,0:T(8,128)(2,1)S(1)}, u32[]{:S(2)}, u32[]{:S(2)}) %collective-permute-start.12) | collective-permute-done | bytes 262176 | tf_op jit(solution)/shard_map/ppermute | solution.py:345
  46.6 1.9 %collective-permute-start.19 = (bf16[512,256]{1,0:T(8,128)(2,1)S(1)}, bf16[512,256]{1,0:T(8,128)(2,1)S(1)}, u32[]{:S(2)}, u32[]{:S(2)}) collective-permute-start(bf16[512,256]{1,0:T(8,128)(2,1)S(1)} %get-tuple-element.51.refs_6_), channel_id=1, source_target_pairs={{0,24},{8,16},{16,8},{24,0},{1,25},{9,17},{17,9},{25,1},{2,26},{10... | collective-permute-start | bytes 786440 | tf_op jit(solution)/shard_map/ppermute | solution.py:345
  50.2 3.3 %collective-permute-start.14 = (bf16[256,256]{1,0:T(8,128)(2,1)S(1)}, bf16[256,256]{1,0:T(8,128)(2,1)S(1)}, u32[]{:S(2)}, u32[]{:S(2)}) collective-permute-start(bf16[256,256]{1,0:T(8,128)(2,1)S(1)} %get-tuple-element.50.refs_0_), channel_id=1, source_target_pairs={{0,2},{1,3},{2,0},{3,1},{4,6},{5,7},{6,4},{7,5},{8,10},{9,11},{10,... | collective-permute-start | bytes 393224 | tf_op jit(solution)/shard_map/ppermute | solution.py:345
  53.5 3.8 %collective-permute-done.15.refs_2_ = bf16[256,256]{1,0:T(8,128)(2,1)S(1)} collective-permute-done((bf16[256,256]{1,0:T(8,128)(2,1)S(1)}, bf16[256,256]{1,0:T(8,128)(2,1)S(1)}, u32[]{:S(2)}, u32[]{:S(2)}) %collective-permute-start.15) | collective-permute-done | bytes 131104 | tf_op jit(solution)/shard_map/ppermute | solution.py:345
  58.5 2.1 %collective-permute-done.18.refs_5_.refs_8_ = bf16[512,256]{1,0:T(8,128)(2,1)S(1)} collective-permute-done((bf16[512,256]{1,0:T(8,128)(2,1)S(1)}, bf16[512,256]{1,0:T(8,128)(2,1)S(1)}, u32[]{:S(2)}, u32[]{:S(2)}) %collective-permute-start.18) | collective-permute-done | bytes 262176 | tf_op jit(solution)/shard_map/ppermute | solution.py:345
  62.3 1.9 %collective-permute-done.20.refs_5_ = bf16[4,256,256]{2,1,0:T(8,128)(2,1)S(1)} collective-permute-done((bf16[4,256,256]{2,1,0:T(8,128)(2,1)S(1)}, bf16[4,256,256]{2,1,0:T(8,128)(2,1)S(1)}, u32[]{:S(2)}, u32[]{:S(2)}) %collective-permute-start.20) | collective-permute-done | bytes 524320 | tf_op jit(solution)/shard_map/ppermute | solution.py:345
  64.2 2.5 %shard_map.94 = (f32[4,4,64,256]{3,2,1,0:T(8,128)S(1)}, bf16[4,4,64,256]{3,2,1,0:T(8,128)(2,1)S(1)}, bf16[4,128,256]{2,1,0:T(8,128)(2,1)S(1)}, bf16[4,128,256]{2...) custom-call(s32[2,8]{1,0:T(2,128)S(1)} %bitcast.9, s32[1]{0:T(128)} %bitcast.7.refs_1_, ...), custom_call_target="tpu_custom_call" | custom-call | flops 3221225472 | bytes 16777216 | tf_op jit(solution)/shard_map/pallas_call | solution.py:261
  66.7 3.2 %collective-permute-start.21 = (bf16[4,4,64,256]{3,2,1,0:T(8,128)(2,1)S(1)}, bf16[4,4,64,256]{3,2,1,0:T(8,128)(2,1)S(1)}, u32[]{:S(2)}, u32[]{:S(2)}) collective-permute-start(bf16[4,4,64,256]{3,2,1,0:T(8,128)(2,1)S(1)} %get-tuple-element.55), channel_id=1, source_target_pairs={{0,1},{1,0},{2,3},{3,2},{4,5},{5,4},{6,7},{7,6},{8,9},{9,8},{10,11... | collective-permute-start | bytes 1572872 | tf_op jit(solution)/shard_map/ppermute | solution.py:345
  71.7 2.0 %collective-permute-start.27 = (bf16[4,128,256]{2,1,0:T(8,128)(2,1)S(1)}, bf16[4,128,256]{2,1,0:T(8,128)(2,1)S(1)}, u32[]{:S(2)}, u32[]{:S(2)}) collective-permute-start(bf16[4,128,256]{2,1,0:T(8,128)(2,1)S(1)} %get-tuple-element.63), channel_id=1, source_target_pairs={{0,24},{8,16},{16,8},{24,0},{1,25},{9,17},{17,9},{25,1},{2,26},{10... | collective-permute-start | bytes 786440 | tf_op jit(solution)/shard_map/ppermute | solution.py:345
  73.6 1.9 %collective-permute-start.24 = (bf16[4,64,256]{2,1,0:T(8,128)(2,1)S(1)}, bf16[4,64,256]{2,1,0:T(8,128)(2,1)S(1)}, u32[]{:S(2)}, u32[]{:S(2)}) collective-permute-start(bf16[4,64,256]{2,1,0:T(8,128)(2,1)S(1)} %get-tuple-element.59), channel_id=1, source_target_pairs={{0,2},{1,3},{2,0},{3,1},{4,6},{5,7},{6,4},{7,5},{8,10},{9,11},{10,... | collective-permute-start | bytes 393224 | tf_op jit(solution)/shard_map/ppermute | solution.py:345
  75.6 2.4 %collective-permute-done.22.refs_1_ = bf16[4,64,256]{2,1,0:T(8,128)(2,1)S(1)} collective-permute-done((bf16[4,64,256]{2,1,0:T(8,128)(2,1)S(1)}, bf16[4,64,256]{2,1,0:T(8,128)(2,1)S(1)}, u32[]{:S(2)}, u32[]{:S(2)}) %collective-permute-start.22) | collective-permute-done | bytes 131104 | tf_op jit(solution)/shard_map/ppermute | solution.py:345
  79.8 4.0 %collective-permute-done.26.refs_5_ = bf16[4,128,256]{2,1,0:T(8,128)(2,1)S(1)} collective-permute-done((bf16[4,128,256]{2,1,0:T(8,128)(2,1)S(1)}, bf16[4,128,256]{2,1,0:T(8,128)(2,1)S(1)}, u32[]{:S(2)}, u32[]{:S(2)}) %collective-permute-start.26) | collective-permute-done | bytes 262176 | tf_op jit(solution)/shard_map/ppermute | solution.py:345
  83.9 2.3 %collective-permute-done.23.refs_1_ = bf16[4,64,256]{2,1,0:T(8,128)(2,1)S(1)} collective-permute-done((bf16[4,64,256]{2,1,0:T(8,128)(2,1)S(1)}, bf16[4,64,256]{2,1,0:T(8,128)(2,1)S(1)}, u32[]{:S(2)}, u32[]{:S(2)}) %collective-permute-start.23) | collective-permute-done | bytes 131104 | tf_op jit(solution)/shard_map/ppermute | solution.py:345
  (54 shorter events, 18.6 us)
Async XLA Ops:
  2.6 11.1 %collective-permute-start.1 = (bf16[272,256]{1,0:T(8,128)(2,1)}, bf16[272,256]{1,0:T(8,128)(2,1)S(1)}, u32[]{:S(2)}, u32[]{:S(2)}) collective-permute-start(bf16[272,256]{1,0:T(8,128)(2,1)} %get-tuple-element.35.refs_0_), channel_id=1, source_target_pairs={{0,4},{1,5},{2,6},{3,7},{4,0},{5,1},{6,2},{7,3},{8,12},{9,13},{10,... | collective-permute-start | bytes 417800 | tf_op jit(solution)/shard_map/ppermute | solution.py:345
  6.7 10.6 %collective-permute-start.5 = (bf16[528,256]{1,0:T(8,128)(2,1)}, bf16[528,256]{1,0:T(8,128)(2,1)S(1)}, u32[]{:S(2)}, u32[]{:S(2)}) collective-permute-start(bf16[528,256]{1,0:T(8,128)(2,1)} %get-tuple-element.36.refs_6_), channel_id=1, source_target_pairs={{0,24},{8,16},{16,8},{24,0},{1,25},{9,17},{17,9},{25,1},{2,26},{10... | collective-permute-start | bytes 811016 | tf_op jit(solution)/shard_map/ppermute | solution.py:345
  9.2 12.4 %collective-permute-start.4 = (bf16[528,256]{1,0:T(8,128)(2,1)}, bf16[528,256]{1,0:T(8,128)(2,1)S(1)}, u32[]{:S(2)}, u32[]{:S(2)}) collective-permute-start(bf16[528,256]{1,0:T(8,128)(2,1)} %get-tuple-element.36.refs_6_), channel_id=1, source_target_pairs={{0,16},{8,24},{16,0},{24,8},{1,17},{9,25},{17,1},{25,9},{2,18},{10... | collective-permute-start | bytes 811016 | tf_op jit(solution)/shard_map/ppermute | solution.py:345
  9.7 12.0 %collective-permute-start.3 = (bf16[528,256]{1,0:T(8,128)(2,1)}, bf16[528,256]{1,0:T(8,128)(2,1)S(1)}, u32[]{:S(2)}, u32[]{:S(2)}) collective-permute-start(bf16[528,256]{1,0:T(8,128)(2,1)} %get-tuple-element.36.refs_6_), channel_id=1, source_target_pairs={{0,8},{8,0},{16,24},{24,16},{1,9},{9,1},{17,25},{25,17},{2,10},{10... | collective-permute-start | bytes 811016 | tf_op jit(solution)/shard_map/ppermute | solution.py:345
  10.2 6.8 %collective-permute-start = (bf16[272,256]{1,0:T(8,128)(2,1)}, bf16[272,256]{1,0:T(8,128)(2,1)S(1)}, u32[]{:S(2)}, u32[]{:S(2)}) collective-permute-start(bf16[272,256]{1,0:T(8,128)(2,1)} %get-tuple-element.35.refs_0_), channel_id=1, source_target_pairs={{0,2},{1,3},{2,0},{3,1},{4,6},{5,7},{6,4},{7,5},{8,10},{9,11},{10,... | collective-permute-start | bytes 417800 | tf_op jit(solution)/shard_map/ppermute | solution.py:345
  13.7 8.0 %collective-permute-start.2 = (bf16[272,256]{1,0:T(8,128)(2,1)S(1)}, bf16[272,256]{1,0:T(8,128)(2,1)S(1)}, u32[]{:S(2)}, u32[]{:S(2)}) collective-permute-start(bf16[272,256]{1,0:T(8,128)(2,1)S(1)} %collective-permute-done.1.refs_2_), channel_id=1, source_target_pairs={{0,2},{1,3},{2,0},{3,1},{4,6},{5,7},{6,4},{7,5},{8,10},{9,11},{10,... | collective-permute-start | bytes 417800 | tf_op jit(solution)/shard_map/ppermute | solution.py:345
  26.6 6.1 %collective-permute-start.7 = (bf16[4,4,64,256]{3,2,1,0:T(8,128)(2,1)S(1)}, bf16[4,4,64,256]{3,2,1,0:T(8,128)(2,1)S(1)}, u32[]{:S(2)}, u32[]{:S(2)}) collective-permute-start(bf16[4,4,64,256]{3,2,1,0:T(8,128)(2,1)S(1)} %get-tuple-element.39), channel_id=1, source_target_pairs={{0,1},{1,0},{2,3},{3,2},{4,5},{5,4},{6,7},{7,6},{8,9},{9,8},{10,11... | collective-permute-start | bytes 1572872 | tf_op jit(solution)/shard_map/ppermute | solution.py:345
  29.7 9.8 %collective-permute-start.11 = (bf16[4,128,256]{2,1,0:T(8,128)(2,1)S(1)}, bf16[4,128,256]{2,1,0:T(8,128)(2,1)S(1)}, u32[]{:S(2)}, u32[]{:S(2)}) collective-permute-start(bf16[4,128,256]{2,1,0:T(8,128)(2,1)S(1)} %get-tuple-element.45), channel_id=1, source_target_pairs={{0,8},{8,0},{16,24},{24,16},{1,9},{9,1},{17,25},{25,17},{2,10},{10... | collective-permute-start | bytes 786440 | tf_op jit(solution)/shard_map/ppermute | solution.py:345
  29.7 15.1 %collective-permute-start.12 = (bf16[4,128,256]{2,1,0:T(8,128)(2,1)S(1)}, bf16[4,128,256]{2,1,0:T(8,128)(2,1)S(1)}, u32[]{:S(2)}, u32[]{:S(2)}) collective-permute-start(bf16[4,128,256]{2,1,0:T(8,128)(2,1)S(1)} %get-tuple-element.46), channel_id=1, source_target_pairs={{0,16},{8,24},{16,0},{24,8},{1,17},{9,25},{17,1},{25,9},{2,18},{10... | collective-permute-start | bytes 786440 | tf_op jit(solution)/shard_map/ppermute | solution.py:345
  32.8 6.4 %collective-permute-start.8 = (bf16[4,64,256]{2,1,0:T(8,128)(2,1)S(1)}, bf16[4,64,256]{2,1,0:T(8,128)(2,1)S(1)}, u32[]{:S(2)}, u32[]{:S(2)}) collective-permute-start(bf16[4,64,256]{2,1,0:T(8,128)(2,1)S(1)} %get-tuple-element.42), channel_id=1, source_target_pairs={{0,2},{1,3},{2,0},{3,1},{4,6},{5,7},{6,4},{7,5},{8,10},{9,11},{10,... | collective-permute-start | bytes 393224 | tf_op jit(solution)/shard_map/ppermute | solution.py:345
  32.8 12.1 %collective-permute-start.13 = (bf16[4,128,256]{2,1,0:T(8,128)(2,1)S(1)}, bf16[4,128,256]{2,1,0:T(8,128)(2,1)S(1)}, u32[]{:S(2)}, u32[]{:S(2)}) collective-permute-start(bf16[4,128,256]{2,1,0:T(8,128)(2,1)S(1)} %get-tuple-element.47), channel_id=1, source_target_pairs={{0,24},{8,16},{16,8},{24,0},{1,25},{9,17},{17,9},{25,1},{2,26},{10... | collective-permute-start | bytes 786440 | tf_op jit(solution)/shard_map/ppermute | solution.py:345
  34.2 10.7 %collective-permute-start.10 = (bf16[4,64,256]{2,1,0:T(8,128)(2,1)S(1)}, bf16[4,64,256]{2,1,0:T(8,128)(2,1)S(1)}, u32[]{:S(2)}, u32[]{:S(2)}) collective-permute-start(bf16[4,64,256]{2,1,0:T(8,128)(2,1)S(1)} %get-tuple-element.43), channel_id=1, source_target_pairs={{0,2},{1,3},{2,0},{3,1},{4,6},{5,7},{6,4},{7,5},{8,10},{9,11},{10,... | collective-permute-start | bytes 393224 | tf_op jit(solution)/shard_map/ppermute | solution.py:345
  39.2 7.1 %collective-permute-start.9 = (bf16[4,64,256]{2,1,0:T(8,128)(2,1)S(1)}, bf16[4,64,256]{2,1,0:T(8,128)(2,1)S(1)}, u32[]{:S(2)}, u32[]{:S(2)}) collective-permute-start(bf16[4,64,256]{2,1,0:T(8,128)(2,1)S(1)} %shard_map.91), channel_id=1, source_target_pairs={{0,4},{1,5},{2,6},{3,7},{4,0},{5,1},{6,2},{7,3},{8,12},{9,13},{10,... | collective-permute-start | bytes 393224 | tf_op jit(solution)/shard_map/ppermute | solution.py:345
  46.6 11.8 %collective-permute-start.19 = (bf16[512,256]{1,0:T(8,128)(2,1)S(1)}, bf16[512,256]{1,0:T(8,128)(2,1)S(1)}, u32[]{:S(2)}, u32[]{:S(2)}) collective-permute-start(bf16[512,256]{1,0:T(8,128)(2,1)S(1)} %get-tuple-element.51.refs_6_), channel_id=1, source_target_pairs={{0,24},{8,16},{16,8},{24,0},{1,25},{9,17},{17,9},{25,1},{2,26},{10... | collective-permute-start | bytes 786440 | tf_op jit(solution)/shard_map/ppermute | solution.py:345
  48.5 12.1 %collective-permute-start.18 = (bf16[512,256]{1,0:T(8,128)(2,1)S(1)}, bf16[512,256]{1,0:T(8,128)(2,1)S(1)}, u32[]{:S(2)}, u32[]{:S(2)}) collective-permute-start(bf16[512,256]{1,0:T(8,128)(2,1)S(1)} %get-tuple-element.51.refs_6_), channel_id=1, source_target_pairs={{0,16},{8,24},{16,0},{24,8},{1,17},{9,25},{17,1},{25,9},{2,18},{10... | collective-permute-start | bytes 786440 | tf_op jit(solution)/shard_map/ppermute | solution.py:345
  49.1 8.1 %collective-permute-start.15 = (bf16[256,256]{1,0:T(8,128)(2,1)S(1)}, bf16[256,256]{1,0:T(8,128)(2,1)S(1)}, u32[]{:S(2)}, u32[]{:S(2)}) collective-permute-start(bf16[256,256]{1,0:T(8,128)(2,1)S(1)} %get-tuple-element.50.refs_0_), channel_id=1, source_target_pairs={{0,4},{1,5},{2,6},{3,7},{4,0},{5,1},{6,2},{7,3},{8,12},{9,13},{10,... | collective-permute-start | bytes 393224 | tf_op jit(solution)/shard_map/ppermute | solution.py:345
  49.1 11.5 %collective-permute-start.17 = (bf16[512,256]{1,0:T(8,128)(2,1)S(1)}, bf16[512,256]{1,0:T(8,128)(2,1)S(1)}, u32[]{:S(2)}, u32[]{:S(2)}) collective-permute-start(bf16[512,256]{1,0:T(8,128)(2,1)S(1)} %get-tuple-element.51.refs_6_), channel_id=1, source_target_pairs={{0,8},{8,0},{16,24},{24,16},{1,9},{9,1},{17,25},{25,17},{2,10},{10... | collective-permute-start | bytes 786440 | tf_op jit(solution)/shard_map/ppermute | solution.py:345
  50.2 8.3 %collective-permute-start.14 = (bf16[256,256]{1,0:T(8,128)(2,1)S(1)}, bf16[256,256]{1,0:T(8,128)(2,1)S(1)}, u32[]{:S(2)}, u32[]{:S(2)}) collective-permute-start(bf16[256,256]{1,0:T(8,128)(2,1)S(1)} %get-tuple-element.50.refs_0_), channel_id=1, source_target_pairs={{0,2},{1,3},{2,0},{3,1},{4,6},{5,7},{6,4},{7,5},{8,10},{9,11},{10,... | collective-permute-start | bytes 393224 | tf_op jit(solution)/shard_map/ppermute | solution.py:345
  69.9 9.9 %collective-permute-start.25 = (bf16[4,128,256]{2,1,0:T(8,128)(2,1)S(1)}, bf16[4,128,256]{2,1,0:T(8,128)(2,1)S(1)}, u32[]{:S(2)}, u32[]{:S(2)}) collective-permute-start(bf16[4,128,256]{2,1,0:T(8,128)(2,1)S(1)} %get-tuple-element.61), channel_id=1, source_target_pairs={{0,8},{8,0},{16,24},{24,16},{1,9},{9,1},{17,25},{25,17},{2,10},{10... | collective-permute-start | bytes 786440 | tf_op jit(solution)/shard_map/ppermute | solution.py:345
  69.9 14.0 %collective-permute-start.26 = (bf16[4,128,256]{2,1,0:T(8,128)(2,1)S(1)}, bf16[4,128,256]{2,1,0:T(8,128)(2,1)S(1)}, u32[]{:S(2)}, u32[]{:S(2)}) collective-permute-start(bf16[4,128,256]{2,1,0:T(8,128)(2,1)S(1)} %get-tuple-element.62), channel_id=1, source_target_pairs={{0,16},{8,24},{16,0},{24,8},{1,17},{9,25},{17,1},{25,9},{2,18},{10... | collective-permute-start | bytes 786440 | tf_op jit(solution)/shard_map/ppermute | solution.py:345
  71.6 6.4 %collective-permute-start.22 = (bf16[4,64,256]{2,1,0:T(8,128)(2,1)S(1)}, bf16[4,64,256]{2,1,0:T(8,128)(2,1)S(1)}, u32[]{:S(2)}, u32[]{:S(2)}) collective-permute-start(bf16[4,64,256]{2,1,0:T(8,128)(2,1)S(1)} %get-tuple-element.58), channel_id=1, source_target_pairs={{0,2},{1,3},{2,0},{3,1},{4,6},{5,7},{6,4},{7,5},{8,10},{9,11},{10,... | collective-permute-start | bytes 393224 | tf_op jit(solution)/shard_map/ppermute | solution.py:345
  71.7 12.2 %collective-permute-start.27 = (bf16[4,128,256]{2,1,0:T(8,128)(2,1)S(1)}, bf16[4,128,256]{2,1,0:T(8,128)(2,1)S(1)}, u32[]{:S(2)}, u32[]{:S(2)}) collective-permute-start(bf16[4,128,256]{2,1,0:T(8,128)(2,1)S(1)} %get-tuple-element.63), channel_id=1, source_target_pairs={{0,24},{8,16},{16,8},{24,0},{1,25},{9,17},{17,9},{25,1},{2,26},{10... | collective-permute-start | bytes 786440 | tf_op jit(solution)/shard_map/ppermute | solution.py:345
  73.6 10.2 %collective-permute-start.24 = (bf16[4,64,256]{2,1,0:T(8,128)(2,1)S(1)}, bf16[4,64,256]{2,1,0:T(8,128)(2,1)S(1)}, u32[]{:S(2)}, u32[]{:S(2)}) collective-permute-start(bf16[4,64,256]{2,1,0:T(8,128)(2,1)S(1)} %get-tuple-element.59), channel_id=1, source_target_pairs={{0,2},{1,3},{2,0},{3,1},{4,6},{5,7},{6,4},{7,5},{8,10},{9,11},{10,... | collective-permute-start | bytes 393224 | tf_op jit(solution)/shard_map/ppermute | solution.py:345
  78.0 8.2 %collective-permute-start.23 = (bf16[4,64,256]{2,1,0:T(8,128)(2,1)S(1)}, bf16[4,64,256]{2,1,0:T(8,128)(2,1)S(1)}, u32[]{:S(2)}, u32[]{:S(2)}) collective-permute-start(bf16[4,64,256]{2,1,0:T(8,128)(2,1)S(1)} %shard_map.96), channel_id=1, source_target_pairs={{0,4},{1,5},{2,6},{3,7},{4,0},{5,1},{6,2},{7,3},{8,12},{9,13},{10,... | collective-permute-start | bytes 393224 | tf_op jit(solution)/shard_map/ppermute | solution.py:345
  (9 other events, 122.2 us)
where the time goes:
time: 88.3 us; the launch traced here: 87.2 us
  starting transfers between devices  37.6 us (43%)
  waiting for transfers between devices  37.5 us (42%)
  Pallas kernels  10.6 us (12%)
  between operations  1.43 us (2%)
    ppermute x28, starting transfers between devices, send(): return lax.ppermute(x, axis, [(k, k ^ mask) for k in range(count)])  37.6 us
    ppermute x28, waiting for transfers between devices, send(): return lax.ppermute(x, axis, [(k, k ^ mask) for k in range(count)])  37.5 us
    pallas_call x2, Pallas kernels, work(): pl.pallas_call(functools.partial(work_kernel, first, n_row, n_col, row_ow...  5.35 us
    pallas_call x1, Pallas kernels, pack(): pl.pallas_call(pack_kernel, out_shape=[shape((e.shape[0] * e.shape[1] + M...  1.93 us
  transfers between devices with their start and end apart: 28, of which 17 were waited for; matrix products, arithmetic and copies ran while one was open for 0% of the time, Pallas kernels for 2%

commit v1 on v0

--- a/solution.py
+++ b/solution.py
@@ -15,8 +15,8 @@
 VMEM = pl.BlockSpec(memory_space=pltpu.VMEM)
 SMEM = pl.BlockSpec(memory_space=pltpu.SMEM)
 SMALL = 12 << 20
-LARGE = 32 << 20
-LEVELS = 35 << 20
+LARGE = 16 << 20
+LEVELS = 31 << 20
 PACK = 62 << 20
 f32, bf16 = jnp.float32, jnp.bfloat16
 shape = jax.ShapeDtypeStruct
@@ -62,8 +62,8 @@
 
 
 def levels_kernel(used, tiles, logs, weights, token, tile_buf, sem):
+    slots, size, _ = tile_buf.shape
     count = used[0]
-    slots, size, _ = tile_buf.shape
     chunk = 64
 
     def load(slot):
@@ -106,7 +106,7 @@
             pltpu.SemaphoreType.DMA((tiles.shape[0],)),
         ],
         compiler_params=pltpu.CompilerParams(vmem_limit_bytes=LEVELS),
-        cost_estimate=cost(0, 24 << 20),
+        cost_estimate=cost(0, 12 << 20),
     )(used, tiles)
 
 
@@ -152,7 +152,7 @@
     col_out = take(n_col)
     if first:
         left, right = take(2)
-    row_panel, row_turned, col_panel, grad_row, grad_turned, grad_col, scores, signal = take(8)
+    row_panel, row_turned, col_panel, grad_row, grad_turned, grad_col, even, odd = take(8)
 
     row_blocks, size, width = row_panel.shape
     col_blocks = col_panel.shape[0]
@@ -194,41 +194,53 @@
     def place(slot):
         return listing[0, slot] - row_zero, listing[1, slot] - col_zero
 
-    def make_scores(slot, rows):
+    def make_signal(slot, rows, signal):
         i, j = place(slot)
-        scores[rows, :] = lax.dot_general(
+        scores = lax.dot_general(
             row_panel[i, rows, :], col_panel[j], (((1,), (1,)), ((), ())), preferred_element_type=f32
         )
-
-    def make_signal(slot, rows):
-        i, j = place(slot)
         marg_left = jnp.concatenate([left[i, rows, :]] * (size // 128), axis=1)
-        diff = scores[rows, :] + marg_left + right[j, 0:1, :] - logs[slot, rows, :]
+        diff = scores + marg_left + right[j, 0:1, :] - logs[slot, rows, :]
         weight = weights[slot, rows, :]
         flat = 0.5 * jnp.tanh(0.5 * diff) + 0.5
         signal[rows, :] = jnp.where(weight > 0.0, weight * diff, flat).astype(bf16)
 
-    def add_grads(slot, rows):
+    def add_row(slot, rows, signal):
         i, j = place(slot)
-        piece = signal[rows, :]
-        grad_row[i, rows, :] += jnp.dot(piece, col_panel[j], preferred_element_type=f32)
-        grad_turned[j] += jnp.dot(row_turned[i, :, rows], piece, preferred_element_type=f32)
-
-    def one_tile(slot, carry):
+        grad_row[i, rows, :] += jnp.dot(signal[rows, :], col_panel[j], preferred_element_type=f32)
+
+    def add_col(slot, signal):
+        i, j = place(slot)
+        grad_turned[j] += jnp.dot(row_turned[i], signal[...], preferred_element_type=f32)
+
+    def step(slot, before, now):
         for rows in chunks:
-            add_grads(slot - 1, rows)
-            make_signal(slot, rows)
-            make_scores(jnp.minimum(slot + 1, count - 1), rows)
+            make_signal(slot, rows, now)
+            add_row(slot - 1, rows, before)
+        add_col(slot - 1, before)
+
+    pairs = (count - 1) // 2
+
+    def pair(n, carry):
+        step(2 * n + 1, even, odd)
+        step(2 * n + 2, odd, even)
         return carry
 
     for rows in chunks:
-        make_scores(0, rows)
-    for rows in chunks:
-        make_signal(0, rows)
-        make_scores(jnp.minimum(1, count - 1), rows)
-    lax.fori_loop(1, count, one_tile, 0)
-    for rows in chunks:
-        add_grads(count - 1, rows)
+        make_signal(0, rows, even)
+    lax.fori_loop(0, pairs, pair, 0)
+
+    @pl.when(2 * pairs + 1 < count)
+    def _():
+        step(2 * pairs + 1, even, odd)
+
+    for parity, signal in enumerate((even, odd)):
+
+        @pl.when(lax.rem(count - 1, 2) == parity)
+        def _():
+            for rows in chunks:
+                add_row(count - 1, rows, signal)
+            add_col(count - 1, signal)
 
     for n in range(n_row):
         place, sibling = row_owner[n] >> 1, row_owner[n] & 1
@@ -270,7 +282,7 @@
             pltpu.VMEM((row_blocks, size, width), f32),
             pltpu.VMEM((col_blocks, width, size), f32),
             pltpu.VMEM((col_blocks, size, width), bf16),
-            pltpu.VMEM((size, size), f32),
+            pltpu.VMEM((size, size), bf16),
             pltpu.VMEM((size, size), bf16),
         ],
         compiler_params=pltpu.CompilerParams(vmem_limit_bytes=LARGE),
@@ -360,13 +372,15 @@
         return send(x, "col", n_col_dev, 2 * distance)
 
     row_pay, col_pay = pack(row_emb, row_marg, col_emb, col_marg)
-    *tabs, made_tabs = levels(used, tiles)
+    *tabs, tabs_made = levels(used, tiles)
     tables = None
     for substep in range(2):
         crossed = hop(row_pay, far)
+        if substep == 0:
+            (crossed,) = join([crossed], [tabs_made])
         row_near = [row_pay] + [hop(row_pay, k) for k in near] + [crossed] + [hop(crossed, k) for k in near]
         col_in = [col_pay] + [send(col_pay, "row", n_row_dev, k) for k in col_owner[1:]]
-        row_near = join(row_near, col_in[1:] + ([made_tabs] if substep == 0 else []))
+        row_near = join(row_near, col_in[1:])
         row_far = send(row_near, "col", n_col_dev, 1)
         keep, swap, col_out, made = work(
             listing, used, tabs, row_near, row_far, col_in, tables, row_owner, col_owner, dims

time: 88.3 us -> 87.1 us (0.986)
  starting transfers between devices: 37.6 us -> 35.9 us
  waiting for transfers between devices: 37.5 us -> 38.6 us
    ppermute x28, starting transfers between devices: 37.6 us -> 35.9 us  [send(): return lax.ppermute(x, axis, [(k, k ^ mask) for k in range(count)])]
    ppermute x28, waiting for transfers between devices: 37.5 us -> 38.6 us  [send(): return lax.ppermute(x, axis, [(k, k ^ mask) for k in range(count)])]
  transfers between devices with their start and end apart: 28 -> 28, of which waited for: 17 -> 16; matrix products, arithmetic and copies ran while one was open for 0% -> 0% of each run, Pallas kernels for 2% -> 2%
where the time goes in v1:
time: 87.1 us; the launch traced here: 86.6 us
  waiting for transfers between devices  38.6 us (44%)
  starting transfers between devices  35.9 us (41%)
  Pallas kernels  10.6 us (12%)
  between operations  1.43 us (2%)
    ppermute x28, waiting for transfers between devices, send(): return lax.ppermute(x, axis, [(k, k ^ mask) for k in range(count)])  38.6 us
    ppermute x28, starting transfers between devices, send(): return lax.ppermute(x, axis, [(k, k ^ mask) for k in range(count)])  35.9 us
    pallas_call x2, Pallas kernels, work(): pl.pallas_call(functools.partial(work_kernel, first, n_row, n_col, row_ow...  5.33 us
    pallas_call x1, Pallas kernels, pack(): pl.pallas_call(pack_kernel, out_shape=[shape((e.shape[0] * e.shape[1] + M...  1.93 us
  transfers between devices with their start and end apart: 28, of which 16 were waited for; matrix products, arithmetic and copies ran while one was open for 0% of the time, Pallas kernels for 2%

profile of v1, /device:TPU:0, one launch (start us, length us, event | category | flops | bytes accessed | tf_op | source)
XLA Modules:
  0.0 86.6 jit_solution(5578194384028007658)
XLA Ops:
  0.6 1.9 %shard_map.87 = (bf16[272,256]{1,0:T(8,128)(2,1)}, bf16[528,256]{1,0:T(8,128)(2,1)}) custom-call(f32[4,64,256]{2,1,0:T(8,128)} %row_emb.3, bf16[4,64]{1,0:T(4,128)(2,1)} %row_marg.1, f32[4,128,256]{2,1,0:T(8,128)} %col_emb.3, bf16[4,128]{1,0:T(4,128)(2,1)} %col_marg.1), custom_call_target="tpu_custom_call" | custom-call | bytes 1048576 | tf_op jit(solution)/shard_map/pallas_call | solution.py:50
  2.6 4.1 %collective-permute-start.1 = (bf16[272,256]{1,0:T(8,128)(2,1)}, bf16[272,256]{1,0:T(8,128)(2,1)S(1)}, u32[]{:S(2)}, u32[]{:S(2)}) collective-permute-start(bf16[272,256]{1,0:T(8,128)(2,1)} %get-tuple-element.35.refs_0_), channel_id=1, source_target_pairs={{0,4},{1,5},{2,6},{3,7},{4,0},{5,1},{6,2},{7,3},{8,12},{9,13},{10,... | collective-permute-start | bytes 417800 | tf_op jit(solution)/shard_map/ppermute | solution.py:357
  6.7 2.4 %collective-permute-start.5 = (bf16[528,256]{1,0:T(8,128)(2,1)}, bf16[528,256]{1,0:T(8,128)(2,1)S(1)}, u32[]{:S(2)}, u32[]{:S(2)}) collective-permute-start(bf16[528,256]{1,0:T(8,128)(2,1)} %get-tuple-element.37.refs_6_), channel_id=1, source_target_pairs={{0,24},{8,16},{16,8},{24,0},{1,25},{9,17},{17,9},{25,1},{2,26},{10... | collective-permute-start | bytes 811016 | tf_op jit(solution)/shard_map/ppermute | solution.py:357
  14.7 2.3 %collective-permute-done.refs_1_ = bf16[272,256]{1,0:T(8,128)(2,1)S(1)} collective-permute-done((bf16[272,256]{1,0:T(8,128)(2,1)}, bf16[272,256]{1,0:T(8,128)(2,1)S(1)}, u32[]{:S(2)}, u32[]{:S(2)}) %collective-permute-start) | collective-permute-done | bytes 139296 | tf_op jit(solution)/shard_map/ppermute | solution.py:357
  17.3 4.3 %collective-permute-done.4.refs_5_.refs_8_ = bf16[528,256]{1,0:T(8,128)(2,1)S(1)} collective-permute-done((bf16[528,256]{1,0:T(8,128)(2,1)}, bf16[528,256]{1,0:T(8,128)(2,1)S(1)}, u32[]{:S(2)}, u32[]{:S(2)}) %collective-permute-start.4) | collective-permute-done | bytes 270368 | tf_op jit(solution)/shard_map/ppermute | solution.py:357
  21.8 1.9 %collective-permute-done.6.refs_5_ = bf16[4,272,256]{2,1,0:T(8,128)(2,1)S(1)} collective-permute-done((bf16[4,272,256]{2,1,0:T(8,128)(2,1)S(1)}, bf16[4,272,256]{2,1,0:T(8,128)(2,1)S(1)}, u32[]{:S(2)}, u32[]{:S(2)}) %collective-permute-start.6) | collective-permute-done | bytes 557088 | tf_op jit(solution)/shard_map/ppermute | solution.py:357
  23.7 2.8 %shard_map.90 = (f32[4,4,64,256]{3,2,1,0:T(8,128)S(1)}, bf16[4,4,64,256]{3,2,1,0:T(8,128)(2,1)S(1)}, bf16[4,128,256]{2,1,0:T(8,128)(2,1)S(1)}, bf16[4,128,256]{2...) custom-call(s32[2,8]{1,0:T(2,128)S(1)} %bitcast.11, ...), custom_call_target="tpu_custom_call" | custom-call | flops 3221225472 | bytes 16777216 | tf_op jit(solution)/shard_map/pallas_call | solution.py:273
  26.8 4.0 %collective-permute-start.11 = (bf16[4,128,256]{2,1,0:T(8,128)(2,1)S(1)}, bf16[4,128,256]{2,1,0:T(8,128)(2,1)S(1)}, u32[]{:S(2)}, u32[]{:S(2)}) collective-permute-start(bf16[4,128,256]{2,1,0:T(8,128)(2,1)S(1)} %get-tuple-element.45), channel_id=1, source_target_pairs={{0,8},{8,0},{16,24},{24,16},{1,9},{9,1},{17,25},{25,17},{2,10},{10... | collective-permute-start | bytes 786440 | tf_op jit(solution)/shard_map/ppermute | solution.py:357
  31.7 2.9 %collective-permute-start.8 = (bf16[4,64,256]{2,1,0:T(8,128)(2,1)S(1)}, bf16[4,64,256]{2,1,0:T(8,128)(2,1)S(1)}, u32[]{:S(2)}, u32[]{:S(2)}) collective-permute-start(bf16[4,64,256]{2,1,0:T(8,128)(2,1)S(1)} %get-tuple-element.42), channel_id=1, source_target_pairs={{0,2},{1,3},{2,0},{3,1},{4,6},{5,7},{6,4},{7,5},{8,10},{9,11},{10,... | collective-permute-start | bytes 393224 | tf_op jit(solution)/shard_map/ppermute | solution.py:357
  36.2 2.4 %collective-permute-done.8.refs_1_ = bf16[4,64,256]{2,1,0:T(8,128)(2,1)S(1)} collective-permute-done((bf16[4,64,256]{2,1,0:T(8,128)(2,1)S(1)}, bf16[4,64,256]{2,1,0:T(8,128)(2,1)S(1)}, u32[]{:S(2)}, u32[]{:S(2)}) %collective-permute-start.8) | collective-permute-done | bytes 131104 | tf_op jit(solution)/shard_map/ppermute | solution.py:357
  39.1 5.6 %collective-permute-done.12.refs_5_ = bf16[4,128,256]{2,1,0:T(8,128)(2,1)S(1)} collective-permute-done((bf16[4,128,256]{2,1,0:T(8,128)(2,1)S(1)}, bf16[4,128,256]{2,1,0:T(8,128)(2,1)S(1)}, u32[]{:S(2)}, u32[]{:S(2)}) %collective-permute-start.12) | collective-permute-done | bytes 262176 | tf_op jit(solution)/shard_map/ppermute | solution.py:357
  48.5 2.5 %collective-permute-start.18 = (bf16[512,256]{1,0:T(8,128)(2,1)S(1)}, bf16[512,256]{1,0:T(8,128)(2,1)S(1)}, u32[]{:S(2)}, u32[]{:S(2)}) collective-permute-start(bf16[512,256]{1,0:T(8,128)(2,1)S(1)} %get-tuple-element.51.refs_6_), channel_id=1, source_target_pairs={{0,16},{8,24},{16,0},{24,8},{1,17},{9,25},{17,1},{25,9},{2,18},{10... | collective-permute-start | bytes 786440 | tf_op jit(solution)/shard_map/ppermute | solution.py:357
  51.0 1.8 %collective-permute-start.14 = (bf16[256,256]{1,0:T(8,128)(2,1)S(1)}, bf16[256,256]{1,0:T(8,128)(2,1)S(1)}, u32[]{:S(2)}, u32[]{:S(2)}) collective-permute-start(bf16[256,256]{1,0:T(8,128)(2,1)S(1)} %get-tuple-element.50.refs_0_), channel_id=1, source_target_pairs={{0,2},{1,3},{2,0},{3,1},{4,6},{5,7},{6,4},{7,5},{8,10},{9,11},{10,... | collective-permute-start | bytes 393224 | tf_op jit(solution)/shard_map/ppermute | solution.py:357
  52.8 4.9 %collective-permute-done.15.refs_2_ = bf16[256,256]{1,0:T(8,128)(2,1)S(1)} collective-permute-done((bf16[256,256]{1,0:T(8,128)(2,1)S(1)}, bf16[256,256]{1,0:T(8,128)(2,1)S(1)}, u32[]{:S(2)}, u32[]{:S(2)}) %collective-permute-start.15) | collective-permute-done | bytes 131104 | tf_op jit(solution)/shard_map/ppermute | solution.py:357
  57.7 1.9 %collective-permute-done.18.refs_5_.refs_8_ = bf16[512,256]{1,0:T(8,128)(2,1)S(1)} collective-permute-done((bf16[512,256]{1,0:T(8,128)(2,1)S(1)}, bf16[512,256]{1,0:T(8,128)(2,1)S(1)}, u32[]{:S(2)}, u32[]{:S(2)}) %collective-permute-start.18) | collective-permute-done | bytes 262176 | tf_op jit(solution)/shard_map/ppermute | solution.py:357
  60.7 2.0 %collective-permute-done.16.refs_3_ = bf16[256,256]{1,0:T(8,128)(2,1)S(1)} collective-permute-done((bf16[256,256]{1,0:T(8,128)(2,1)S(1)}, bf16[256,256]{1,0:T(8,128)(2,1)S(1)}, u32[]{:S(2)}, u32[]{:S(2)}) %collective-permute-start.16) | collective-permute-done | bytes 131104 | tf_op jit(solution)/shard_map/ppermute | solution.py:357
  62.8 1.9 %collective-permute-done.20.refs_5_ = bf16[4,256,256]{2,1,0:T(8,128)(2,1)S(1)} collective-permute-done((bf16[4,256,256]{2,1,0:T(8,128)(2,1)S(1)}, bf16[4,256,256]{2,1,0:T(8,128)(2,1)S(1)}, u32[]{:S(2)}, u32[]{:S(2)}) %collective-permute-start.20) | collective-permute-done | bytes 524320 | tf_op jit(solution)/shard_map/ppermute | solution.py:357
  64.7 2.5 %shard_map.95 = (f32[4,4,64,256]{3,2,1,0:T(8,128)S(1)}, bf16[4,4,64,256]{3,2,1,0:T(8,128)(2,1)S(1)}, bf16[4,128,256]{2,1,0:T(8,128)(2,1)S(1)}, bf16[4,128,256]{2...) custom-call(s32[2,8]{1,0:T(2,128)S(1)} %bitcast.12, s32[1]{0:T(128)} %bitcast.8.refs_1_, ...), custom_call_target="tpu_custom_call" | custom-call | flops 3221225472 | bytes 16777216 | tf_op jit(solution)/shard_map/pallas_call | solution.py:273
  67.4 2.3 %collective-permute-start.25 = (bf16[4,128,256]{2,1,0:T(8,128)(2,1)S(1)}, bf16[4,128,256]{2,1,0:T(8,128)(2,1)S(1)}, u32[]{:S(2)}, u32[]{:S(2)}) collective-permute-start(bf16[4,128,256]{2,1,0:T(8,128)(2,1)S(1)} %get-tuple-element.61), channel_id=1, source_target_pairs={{0,8},{8,0},{16,24},{24,16},{1,9},{9,1},{17,25},{25,17},{2,10},{10... | collective-permute-start | bytes 786440 | tf_op jit(solution)/shard_map/ppermute | solution.py:357
  69.7 2.1 %collective-permute-start.26 = (bf16[4,128,256]{2,1,0:T(8,128)(2,1)S(1)}, bf16[4,128,256]{2,1,0:T(8,128)(2,1)S(1)}, u32[]{:S(2)}, u32[]{:S(2)}) collective-permute-start(bf16[4,128,256]{2,1,0:T(8,128)(2,1)S(1)} %get-tuple-element.62), channel_id=1, source_target_pairs={{0,16},{8,24},{16,0},{24,8},{1,17},{9,25},{17,1},{25,9},{2,18},{10... | collective-permute-start | bytes 786440 | tf_op jit(solution)/shard_map/ppermute | solution.py:357
  75.2 2.4 %collective-permute-done.22.refs_1_ = bf16[4,64,256]{2,1,0:T(8,128)(2,1)S(1)} collective-permute-done((bf16[4,64,256]{2,1,0:T(8,128)(2,1)S(1)}, bf16[4,64,256]{2,1,0:T(8,128)(2,1)S(1)}, u32[]{:S(2)}, u32[]{:S(2)}) %collective-permute-start.22) | collective-permute-done | bytes 131104 | tf_op jit(solution)/shard_map/ppermute | solution.py:357
  77.6 2.2 %collective-permute-start.23 = (bf16[4,64,256]{2,1,0:T(8,128)(2,1)S(1)}, bf16[4,64,256]{2,1,0:T(8,128)(2,1)S(1)}, u32[]{:S(2)}, u32[]{:S(2)}) collective-permute-start(bf16[4,64,256]{2,1,0:T(8,128)(2,1)S(1)} %shard_map.97), channel_id=1, source_target_pairs={{0,4},{1,5},{2,6},{3,7},{4,0},{5,1},{6,2},{7,3},{8,12},{9,13},{10,... | collective-permute-start | bytes 393224 | tf_op jit(solution)/shard_map/ppermute | solution.py:357
  79.7 4.0 %collective-permute-done.26.refs_5_ = bf16[4,128,256]{2,1,0:T(8,128)(2,1)S(1)} collective-permute-done((bf16[4,128,256]{2,1,0:T(8,128)(2,1)S(1)}, bf16[4,128,256]{2,1,0:T(8,128)(2,1)S(1)}, u32[]{:S(2)}, u32[]{:S(2)}) %collective-permute-start.26) | collective-permute-done | bytes 262176 | tf_op jit(solution)/shard_map/ppermute | solution.py:357
  83.7 1.8 %collective-permute-done.23.refs_1_ = bf16[4,64,256]{2,1,0:T(8,128)(2,1)S(1)} collective-permute-done((bf16[4,64,256]{2,1,0:T(8,128)(2,1)S(1)}, bf16[4,64,256]{2,1,0:T(8,128)(2,1)S(1)}, u32[]{:S(2)}, u32[]{:S(2)}) %collective-permute-start.23) | collective-permute-done | bytes 131104 | tf_op jit(solution)/shard_map/ppermute | solution.py:357
  (55 shorter events, 18.0 us)
Async XLA Ops:
  2.6 11.5 %collective-permute-start.1 = (bf16[272,256]{1,0:T(8,128)(2,1)}, bf16[272,256]{1,0:T(8,128)(2,1)S(1)}, u32[]{:S(2)}, u32[]{:S(2)}) collective-permute-start(bf16[272,256]{1,0:T(8,128)(2,1)} %get-tuple-element.35.refs_0_), channel_id=1, source_target_pairs={{0,4},{1,5},{2,6},{3,7},{4,0},{5,1},{6,2},{7,3},{8,12},{9,13},{10,... | collective-permute-start | bytes 417800 | tf_op jit(solution)/shard_map/ppermute | solution.py:357
  6.7 10.6 %collective-permute-start.5 = (bf16[528,256]{1,0:T(8,128)(2,1)}, bf16[528,256]{1,0:T(8,128)(2,1)S(1)}, u32[]{:S(2)}, u32[]{:S(2)}) collective-permute-start(bf16[528,256]{1,0:T(8,128)(2,1)} %get-tuple-element.37.refs_6_), channel_id=1, source_target_pairs={{0,24},{8,16},{16,8},{24,0},{1,25},{9,17},{17,9},{25,1},{2,26},{10... | collective-permute-start | bytes 811016 | tf_op jit(solution)/shard_map/ppermute | solution.py:357
  9.2 12.4 %collective-permute-start.4 = (bf16[528,256]{1,0:T(8,128)(2,1)}, bf16[528,256]{1,0:T(8,128)(2,1)S(1)}, u32[]{:S(2)}, u32[]{:S(2)}) collective-permute-start(bf16[528,256]{1,0:T(8,128)(2,1)} %get-tuple-element.37.refs_6_), channel_id=1, source_target_pairs={{0,16},{8,24},{16,0},{24,8},{1,17},{9,25},{17,1},{25,9},{2,18},{10... | collective-permute-start | bytes 811016 | tf_op jit(solution)/shard_map/ppermute | solution.py:357
  9.7 12.0 %collective-permute-start.3 = (bf16[528,256]{1,0:T(8,128)(2,1)}, bf16[528,256]{1,0:T(8,128)(2,1)S(1)}, u32[]{:S(2)}, u32[]{:S(2)}) collective-permute-start(bf16[528,256]{1,0:T(8,128)(2,1)} %get-tuple-element.37.refs_6_), channel_id=1, source_target_pairs={{0,8},{8,0},{16,24},{24,16},{1,9},{9,1},{17,25},{25,17},{2,10},{10... | collective-permute-start | bytes 811016 | tf_op jit(solution)/shard_map/ppermute | solution.py:357
  10.2 6.8 %collective-permute-start = (bf16[272,256]{1,0:T(8,128)(2,1)}, bf16[272,256]{1,0:T(8,128)(2,1)S(1)}, u32[]{:S(2)}, u32[]{:S(2)}) collective-permute-start(bf16[272,256]{1,0:T(8,128)(2,1)} %get-tuple-element.35.refs_0_), channel_id=1, source_target_pairs={{0,2},{1,3},{2,0},{3,1},{4,6},{5,7},{6,4},{7,5},{8,10},{9,11},{10,... | collective-permute-start | bytes 417800 | tf_op jit(solution)/shard_map/ppermute | solution.py:357
  14.2 7.5 %collective-permute-start.2 = (bf16[272,256]{1,0:T(8,128)(2,1)S(1)}, bf16[272,256]{1,0:T(8,128)(2,1)S(1)}, u32[]{:S(2)}, u32[]{:S(2)}) collective-permute-start(bf16[272,256]{1,0:T(8,128)(2,1)S(1)} %bitcast.9), channel_id=1, source_target_pairs={{0,2},{1,3},{2,0},{3,1},{4,6},{5,7},{6,4},{7,5},{8,10},{9,11},{10,... | collective-permute-start | bytes 417800 | tf_op jit(solution)/shard_map/ppermute | solution.py:357
  26.5 5.0 %collective-permute-start.7 = (bf16[4,4,64,256]{3,2,1,0:T(8,128)(2,1)S(1)}, bf16[4,4,64,256]{3,2,1,0:T(8,128)(2,1)S(1)}, u32[]{:S(2)}, u32[]{:S(2)}) collective-permute-start(bf16[4,4,64,256]{3,2,1,0:T(8,128)(2,1)S(1)} %get-tuple-element.39), channel_id=1, source_target_pairs={{0,1},{1,0},{2,3},{3,2},{4,5},{5,4},{6,7},{7,6},{8,9},{9,8},{10,11... | collective-permute-start | bytes 1572872 | tf_op jit(solution)/shard_map/ppermute | solution.py:357
  26.8 12.4 %collective-permute-start.11 = (bf16[4,128,256]{2,1,0:T(8,128)(2,1)S(1)}, bf16[4,128,256]{2,1,0:T(8,128)(2,1)S(1)}, u32[]{:S(2)}, u32[]{:S(2)}) collective-permute-start(bf16[4,128,256]{2,1,0:T(8,128)(2,1)S(1)} %get-tuple-element.45), channel_id=1, source_target_pairs={{0,8},{8,0},{16,24},{24,16},{1,9},{9,1},{17,25},{25,17},{2,10},{10... | collective-permute-start | bytes 786440 | tf_op jit(solution)/shard_map/ppermute | solution.py:357
  30.8 14.0 %collective-permute-start.12 = (bf16[4,128,256]{2,1,0:T(8,128)(2,1)S(1)}, bf16[4,128,256]{2,1,0:T(8,128)(2,1)S(1)}, u32[]{:S(2)}, u32[]{:S(2)}) collective-permute-start(bf16[4,128,256]{2,1,0:T(8,128)(2,1)S(1)} %get-tuple-element.46), channel_id=1, source_target_pairs={{0,16},{8,24},{16,0},{24,8},{1,17},{9,25},{17,1},{25,9},{2,18},{10... | collective-permute-start | bytes 786440 | tf_op jit(solution)/shard_map/ppermute | solution.py:357
  31.7 6.8 %collective-permute-start.8 = (bf16[4,64,256]{2,1,0:T(8,128)(2,1)S(1)}, bf16[4,64,256]{2,1,0:T(8,128)(2,1)S(1)}, u32[]{:S(2)}, u32[]{:S(2)}) collective-permute-start(bf16[4,64,256]{2,1,0:T(8,128)(2,1)S(1)} %get-tuple-element.42), channel_id=1, source_target_pairs={{0,2},{1,3},{2,0},{3,1},{4,6},{5,7},{6,4},{7,5},{8,10},{9,11},{10,... | collective-permute-start | bytes 393224 | tf_op jit(solution)/shard_map/ppermute | solution.py:357
  34.6 10.2 %collective-permute-start.13 = (bf16[4,128,256]{2,1,0:T(8,128)(2,1)S(1)}, bf16[4,128,256]{2,1,0:T(8,128)(2,1)S(1)}, u32[]{:S(2)}, u32[]{:S(2)}) collective-permute-start(bf16[4,128,256]{2,1,0:T(8,128)(2,1)S(1)} %get-tuple-element.47), channel_id=1, source_target_pairs={{0,24},{8,16},{16,8},{24,0},{1,25},{9,17},{17,9},{25,1},{2,26},{10... | collective-permute-start | bytes 786440 | tf_op jit(solution)/shard_map/ppermute | solution.py:357
  36.1 8.7 %collective-permute-start.10 = (bf16[4,64,256]{2,1,0:T(8,128)(2,1)S(1)}, bf16[4,64,256]{2,1,0:T(8,128)(2,1)S(1)}, u32[]{:S(2)}, u32[]{:S(2)}) collective-permute-start(bf16[4,64,256]{2,1,0:T(8,128)(2,1)S(1)} %get-tuple-element.43), channel_id=1, source_target_pairs={{0,2},{1,3},{2,0},{3,1},{4,6},{5,7},{6,4},{7,5},{8,10},{9,11},{10,... | collective-permute-start | bytes 393224 | tf_op jit(solution)/shard_map/ppermute | solution.py:357
  38.6 8.0 %collective-permute-start.9 = (bf16[4,64,256]{2,1,0:T(8,128)(2,1)S(1)}, bf16[4,64,256]{2,1,0:T(8,128)(2,1)S(1)}, u32[]{:S(2)}, u32[]{:S(2)}) collective-permute-start(bf16[4,64,256]{2,1,0:T(8,128)(2,1)S(1)} %shard_map.92), channel_id=1, source_target_pairs={{0,4},{1,5},{2,6},{3,7},{4,0},{5,1},{6,2},{7,3},{8,12},{9,13},{10,... | collective-permute-start | bytes 393224 | tf_op jit(solution)/shard_map/ppermute | solution.py:357
  46.8 10.9 %collective-permute-start.19 = (bf16[512,256]{1,0:T(8,128)(2,1)S(1)}, bf16[512,256]{1,0:T(8,128)(2,1)S(1)}, u32[]{:S(2)}, u32[]{:S(2)}) collective-permute-start(bf16[512,256]{1,0:T(8,128)(2,1)S(1)} %get-tuple-element.51.refs_6_), channel_id=1, source_target_pairs={{0,24},{8,16},{16,8},{24,0},{1,25},{9,17},{17,9},{25,1},{2,26},{10... | collective-permute-start | bytes 786440 | tf_op jit(solution)/shard_map/ppermute | solution.py:357
  48.5 11.1 %collective-permute-start.18 = (bf16[512,256]{1,0:T(8,128)(2,1)S(1)}, bf16[512,256]{1,0:T(8,128)(2,1)S(1)}, u32[]{:S(2)}, u32[]{:S(2)}) collective-permute-start(bf16[512,256]{1,0:T(8,128)(2,1)S(1)} %get-tuple-element.51.refs_6_), channel_id=1, source_target_pairs={{0,16},{8,24},{16,0},{24,8},{1,17},{9,25},{17,1},{25,9},{2,18},{10... | collective-permute-start | bytes 786440 | tf_op jit(solution)/shard_map/ppermute | solution.py:357
  51.0 6.7 %collective-permute-start.15 = (bf16[256,256]{1,0:T(8,128)(2,1)S(1)}, bf16[256,256]{1,0:T(8,128)(2,1)S(1)}, u32[]{:S(2)}, u32[]{:S(2)}) collective-permute-start(bf16[256,256]{1,0:T(8,128)(2,1)S(1)} %get-tuple-element.50.refs_0_), channel_id=1, source_target_pairs={{0,4},{1,5},{2,6},{3,7},{4,0},{5,1},{6,2},{7,3},{8,12},{9,13},{10,... | collective-permute-start | bytes 393224 | tf_op jit(solution)/shard_map/ppermute | solution.py:357
  51.0 9.7 %collective-permute-start.17 = (bf16[512,256]{1,0:T(8,128)(2,1)S(1)}, bf16[512,256]{1,0:T(8,128)(2,1)S(1)}, u32[]{:S(2)}, u32[]{:S(2)}) collective-permute-start(bf16[512,256]{1,0:T(8,128)(2,1)S(1)} %get-tuple-element.51.refs_6_), channel_id=1, source_target_pairs={{0,8},{8,0},{16,24},{24,16},{1,9},{9,1},{17,25},{25,17},{2,10},{10... | collective-permute-start | bytes 786440 | tf_op jit(solution)/shard_map/ppermute | solution.py:357
  51.0 6.7 %collective-permute-start.14 = (bf16[256,256]{1,0:T(8,128)(2,1)S(1)}, bf16[256,256]{1,0:T(8,128)(2,1)S(1)}, u32[]{:S(2)}, u32[]{:S(2)}) collective-permute-start(bf16[256,256]{1,0:T(8,128)(2,1)S(1)} %get-tuple-element.50.refs_0_), channel_id=1, source_target_pairs={{0,2},{1,3},{2,0},{3,1},{4,6},{5,7},{6,4},{7,5},{8,10},{9,11},{10,... | collective-permute-start | bytes 393224 | tf_op jit(solution)/shard_map/ppermute | solution.py:357
  67.4 12.3 %collective-permute-start.25 = (bf16[4,128,256]{2,1,0:T(8,128)(2,1)S(1)}, bf16[4,128,256]{2,1,0:T(8,128)(2,1)S(1)}, u32[]{:S(2)}, u32[]{:S(2)}) collective-permute-start(bf16[4,128,256]{2,1,0:T(8,128)(2,1)S(1)} %get-tuple-element.61), channel_id=1, source_target_pairs={{0,8},{8,0},{16,24},{24,16},{1,9},{9,1},{17,25},{25,17},{2,10},{10... | collective-permute-start | bytes 786440 | tf_op jit(solution)/shard_map/ppermute | solution.py:357
  69.7 14.0 %collective-permute-start.26 = (bf16[4,128,256]{2,1,0:T(8,128)(2,1)S(1)}, bf16[4,128,256]{2,1,0:T(8,128)(2,1)S(1)}, u32[]{:S(2)}, u32[]{:S(2)}) collective-permute-start(bf16[4,128,256]{2,1,0:T(8,128)(2,1)S(1)} %get-tuple-element.62), channel_id=1, source_target_pairs={{0,16},{8,24},{16,0},{24,8},{1,17},{9,25},{17,1},{25,9},{2,18},{10... | collective-permute-start | bytes 786440 | tf_op jit(solution)/shard_map/ppermute | solution.py:357
  72.0 5.6 %collective-permute-start.22 = (bf16[4,64,256]{2,1,0:T(8,128)(2,1)S(1)}, bf16[4,64,256]{2,1,0:T(8,128)(2,1)S(1)}, u32[]{:S(2)}, u32[]{:S(2)}) collective-permute-start(bf16[4,64,256]{2,1,0:T(8,128)(2,1)S(1)} %get-tuple-element.58), channel_id=1, source_target_pairs={{0,2},{1,3},{2,0},{3,1},{4,6},{5,7},{6,4},{7,5},{8,10},{9,11},{10,... | collective-permute-start | bytes 393224 | tf_op jit(solution)/shard_map/ppermute | solution.py:357
  73.6 10.1 %collective-permute-start.27 = (bf16[4,128,256]{2,1,0:T(8,128)(2,1)S(1)}, bf16[4,128,256]{2,1,0:T(8,128)(2,1)S(1)}, u32[]{:S(2)}, u32[]{:S(2)}) collective-permute-start(bf16[4,128,256]{2,1,0:T(8,128)(2,1)S(1)} %get-tuple-element.63), channel_id=1, source_target_pairs={{0,24},{8,16},{16,8},{24,0},{1,25},{9,17},{17,9},{25,1},{2,26},{10... | collective-permute-start | bytes 786440 | tf_op jit(solution)/shard_map/ppermute | solution.py:357
  75.1 8.6 %collective-permute-start.24 = (bf16[4,64,256]{2,1,0:T(8,128)(2,1)S(1)}, bf16[4,64,256]{2,1,0:T(8,128)(2,1)S(1)}, u32[]{:S(2)}, u32[]{:S(2)}) collective-permute-start(bf16[4,64,256]{2,1,0:T(8,128)(2,1)S(1)} %get-tuple-element.59), channel_id=1, source_target_pairs={{0,2},{1,3},{2,0},{3,1},{4,6},{5,7},{6,4},{7,5},{8,10},{9,11},{10,... | collective-permute-start | bytes 393224 | tf_op jit(solution)/shard_map/ppermute | solution.py:357
  77.6 8.0 %collective-permute-start.23 = (bf16[4,64,256]{2,1,0:T(8,128)(2,1)S(1)}, bf16[4,64,256]{2,1,0:T(8,128)(2,1)S(1)}, u32[]{:S(2)}, u32[]{:S(2)}) collective-permute-start(bf16[4,64,256]{2,1,0:T(8,128)(2,1)S(1)} %shard_map.97), channel_id=1, source_target_pairs={{0,4},{1,5},{2,6},{3,7},{4,0},{5,1},{6,2},{7,3},{8,12},{9,13},{10,... | collective-permute-start | bytes 393224 | tf_op jit(solution)/shard_map/ppermute | solution.py:357
  (9 other events, 122.5 us)

commit v2 on v1

--- a/solution.py
+++ b/solution.py
@@ -16,7 +16,7 @@
 SMEM = pl.BlockSpec(memory_space=pltpu.SMEM)
 SMALL = 12 << 20
 LARGE = 16 << 20
-LEVELS = 31 << 20
+LEVELS = 35 << 20
 PACK = 62 << 20
 f32, bf16 = jnp.float32, jnp.bfloat16
 shape = jax.ShapeDtypeStruct
@@ -86,7 +86,7 @@
             level = jnp.maximum(counts, 1.0)
             logs[slot, rows, :] = jnp.log(level)
             weight = 0.1 + 0.25 * (level * lax.rsqrt(level))
-            weights[slot, rows, :] = jnp.where(counts > 0.0, weight, 0.0)
+            weights[slot, rows, :] = jnp.where(counts > 0.0, weight, 0.0).astype(bf16)
             return carry
 
         lax.fori_loop(0, size // chunk, one_chunk, 0)
@@ -98,7 +98,7 @@
 def levels(used, tiles):
     return pl.pallas_call(
         levels_kernel,
-        out_shape=[shape(tiles.shape, f32)] * 2 + [shape((8, 128), f32)],
+        out_shape=[shape(tiles.shape, f32), shape(tiles.shape, bf16), shape((8, 128), f32)],
         in_specs=[SMEM, HBM],
         out_specs=[VMEM] * 3,
         scratch_shapes=[
@@ -138,13 +138,14 @@
     return table
 
 
-def work_kernel(first, n_row, n_col, row_owner, col_owner, *refs):
+def work_kernel(first, n_sides, n_row, n_col, row_owner, col_owner, *refs):
     refs = list(refs)
 
     def take(n):
         return [refs.pop(0) for _ in range(n)]
 
-    listing, used, logs, weights, row_near, row_far = take(6)
+    listing, used, logs, weights = take(4)
+    sides = take(n_sides)
     col_in = take(n_col)
     if not first:
         left, right = take(2)
@@ -163,7 +164,7 @@
     col_owners = [me_row ^ k for k in col_owner]
     row_zero, col_zero = me_row * row_blocks, me_col * col_blocks
     count = used[0]
-    row_in = [side.at[n] for side in (row_near, row_far) for n in range(half)]
+    row_in = [side.at[n] for side in sides for n in range(side.shape[0])]
 
     for pieces, owners, panel, part in (
         (row_in, row_owners, row_panel, row_part),
@@ -200,10 +201,11 @@
             row_panel[i, rows, :], col_panel[j], (((1,), (1,)), ((), ())), preferred_element_type=f32
         )
         marg_left = jnp.concatenate([left[i, rows, :]] * (size // 128), axis=1)
-        diff = scores + marg_left + right[j, 0:1, :] - logs[slot, rows, :]
+        diff = (scores + marg_left + right[j, 0:1, :] - logs[slot, rows, :]).astype(bf16)
         weight = weights[slot, rows, :]
-        flat = 0.5 * jnp.tanh(0.5 * diff) + 0.5
-        signal[rows, :] = jnp.where(weight > 0.0, weight * diff, flat).astype(bf16)
+        half_one = jnp.asarray(0.5, bf16)
+        flat = half_one * jnp.tanh(half_one * diff) + half_one
+        signal[rows, :] = jnp.where(weight > 0, weight * diff, flat)
 
     def add_row(slot, rows, signal):
         i, j = place(slot)
@@ -257,7 +259,7 @@
         col_out[n][...] = grad_col[:, pl.ds(start, col_part), :]
 
 
-def work(listing, used, tabs, row_near, row_far, col_in, tables, row_owner, col_owner, dims):
+def work(listing, used, tabs, row_in, col_in, tables, row_owner, col_owner, dims):
     row_blocks, col_blocks, size, width = dims
     first = tables is None
     n_row, n_col = len(row_owner), len(col_owner)
@@ -269,9 +271,9 @@
     ] + [shape((col_blocks, col_part, width), bf16)] * n_col
     if first:
         outs += [shape((row_blocks, size, 128), f32), shape((col_blocks, 8, size), f32)]
-    args = [listing, used, *tabs, row_near, row_far, *col_in] + ([] if first else list(tables))
+    args = [listing, used, *tabs, *row_in, *col_in] + ([] if first else list(tables))
     res = pl.pallas_call(
-        functools.partial(work_kernel, first, n_row, n_col, row_owner, col_owner),
+        functools.partial(work_kernel, first, len(row_in), n_row, n_col, row_owner, col_owner),
         out_shape=outs,
         in_specs=[SMEM, SMEM] + [VMEM] * (len(args) - 2),
         out_specs=[VMEM] * len(outs),
@@ -326,31 +328,31 @@
     )(own, *parts)
 
 
-def update_kernel(n_row, n_col, row_emb, col_emb, *refs):
-    row_parts, col_parts, outs = refs[:n_row], refs[n_row : n_row + n_col], refs[n_row + n_col :]
-    for n, (emb, parts) in enumerate(((row_emb, row_parts), (col_emb, col_parts))):
-        total = parts[0][...].astype(f32)
-        for part in parts[1:]:
-            total += part[...].astype(f32)
-        new = emb[...] - RATE * total
-        outs[n][...] = new
-        if len(outs) > 2:
-            outs[2 + n][...] = new.astype(bf16).reshape(outs[2 + n].shape)
-
-
-def update(row_emb, col_emb, row_parts, col_parts, last):
-    embs = (row_emb, col_emb)
-    outs = [shape(e.shape, f32) for e in embs]
+def update_kernel(n_parts, emb, *refs):
+    parts, outs = refs[:n_parts], refs[n_parts + 1 :]
+    total = parts[0][...].astype(f32)
+    for part in parts[1:]:
+        total += part[...].astype(f32)
+    new = emb[...] - RATE * total
+    outs[0][...] = new
+    if len(outs) > 1:
+        outs[1][...] = new.astype(bf16).reshape(outs[1].shape)
+
+
+def update(emb, parts, after, last):
+    blocks, part, width = emb.shape
+    outs = [shape(emb.shape, f32)]
     if not last:
-        outs += [shape((e.shape[0] * e.shape[1], e.shape[2]), bf16) for e in embs]
-    return pl.pallas_call(
-        functools.partial(update_kernel, len(row_parts), len(col_parts)),
+        outs.append(shape((blocks * part, width), bf16))
+    res = pl.pallas_call(
+        functools.partial(update_kernel, len(parts)),
         out_shape=outs,
-        in_specs=[VMEM] * (2 + len(row_parts) + len(col_parts)),
+        in_specs=[VMEM] * (1 + len(parts)) + [ANY],
         out_specs=[VMEM] * len(outs),
         compiler_params=pltpu.CompilerParams(vmem_limit_bytes=SMALL),
-        cost_estimate=cost(0, 2 << 20),
-    )(row_emb, col_emb, *row_parts, *col_parts)
+        cost_estimate=cost(0, 1 << 20),
+    )(emb, *parts, after)
+    return res if not last else (res[0], None)
 
 
 def send(x, axis, count, mask):
@@ -376,23 +378,22 @@
     tables = None
     for substep in range(2):
         crossed = hop(row_pay, far)
-        if substep == 0:
-            (crossed,) = join([crossed], [tabs_made])
-        row_near = [row_pay] + [hop(row_pay, k) for k in near] + [crossed] + [hop(crossed, k) for k in near]
         col_in = [col_pay] + [send(col_pay, "row", n_row_dev, k) for k in col_owner[1:]]
-        row_near = join(row_near, col_in[1:])
-        row_far = send(row_near, "col", n_col_dev, 1)
+        (crossed,) = join([crossed], [tabs_made if substep == 0 else col_in[-1]])
+        row_in = [row_pay] + [hop(row_pay, k) for k in near] + [crossed] + [hop(crossed, k) for k in near]
+        row_in = [join(row_in, col_in[1:])]
+        row_in += [send(pieces, "col", n_col_dev, 1) for pieces in row_in]
         keep, swap, col_out, made = work(
-            listing, used, tabs, row_near, row_far, col_in, tables, row_owner, col_owner, dims
+            listing, used, tabs, row_in, col_in, tables, row_owner, col_owner, dims
         )
         tables = tables or made
         merged = merge(keep, send(swap, "col", n_col_dev, 1), (0, far))
         crossing = add(merged[far], [hop(merged[far + k], k) for k in near])
         col_parts = [col_out[0]] + [send(col_out[k], "row", n_row_dev, k) for k in col_owner[1:]]
         row_parts = [merged[0], hop(crossing, far)] + [hop(merged[k], k) for k in near]
-        if substep == 0:
-            row_emb, col_emb, row_pay, col_pay = update(row_emb, col_emb, row_parts, col_parts, False)
-    return tuple(update(row_emb, col_emb, row_parts, col_parts, True))
+        col_emb, col_pay = update(col_emb, col_parts, crossing, substep == 1)
+        row_emb, row_pay = update(row_emb, row_parts, col_pay if substep == 0 else crossing, substep == 1)
+    return (row_emb, col_emb)
 
 
 def solution(mesh):

time: 87.1 us -> 85.7 us (0.984)
  waiting for transfers between devices: 38.6 us -> 35 us
  Pallas kernels: 10.6 us -> 14 us
  starting transfers between devices: 35.9 us -> 34.1 us
    ppermute x28, waiting for transfers between devices: 38.6 us -> 35 us  [send(): return lax.ppermute(x, axis, [(k, k ^ mask) for k in range(count)])]
    pallas_call x5 -> x7, Pallas kernels: 8.29 us -> 11.7 us  [the longest x2 7.22 us: work(): pl.pallas_call(functools.partial(work_kernel, first, len(row_in), n_row,...]
    ppermute x28, starting transfers between devices: 35.9 us -> 34.1 us  [send(): return lax.ppermute(x, axis, [(k, k ^ mask) for k in range(count)])]
  transfers between devices with their start and end apart: 28 -> 28, of which waited for: 16 -> 15; matrix products, arithmetic and copies ran while one was open for 0% -> 0% of each run, Pallas kernels for 2% -> 5%
where the time goes in v2:
time: 85.7 us; the launch traced here: 84.6 us
  waiting for transfers between devices  35 us (41%)
  starting transfers between devices  34.1 us (40%)
  Pallas kernels  14 us (16%)
  between operations  1.48 us (2%)
    ppermute x28, waiting for transfers between devices, send(): return lax.ppermute(x, axis, [(k, k ^ mask) for k in range(count)])  35 us
    ppermute x28, starting transfers between devices, send(): return lax.ppermute(x, axis, [(k, k ^ mask) for k in range(count)])  34.1 us
    pallas_call x2, Pallas kernels, work(): pl.pallas_call(functools.partial(work_kernel, first, len(row_in), n_row,...  7.22 us
    pallas_call x1, Pallas kernels, levels(): pl.pallas_call(levels_kernel, out_shape=[shape(tiles.shape, f32), shape(t...  2.54 us
    pallas_call x4, Pallas kernels, update(): pl.pallas_call(functools.partial(update_kernel, len(parts)), out_shape=ou...  1.98 us
    pallas_call x1, Pallas kernels, pack(): pl.pallas_call(pack_kernel, out_shape=[shape((e.shape[0] * e.shape[1] + M...  1.93 us
  transfers between devices with their start and end apart: 28, of which 15 were waited for; matrix products, arithmetic and copies ran while one was open for 0% of the time, Pallas kernels for 5%

profile of v2, /device:TPU:0, one launch (start us, length us, event | category | flops | bytes accessed | tf_op | source)
XLA Modules:
  0.0 84.6 jit_solution(7444941228230689322)
XLA Ops:
  0.6 1.9 %shard_map.87 = (bf16[272,256]{1,0:T(8,128)(2,1)}, bf16[528,256]{1,0:T(8,128)(2,1)}) custom-call(f32[4,64,256]{2,1,0:T(8,128)} %emb.3, bf16[4,64]{1,0:T(4,128)(2,1)} %row_marg.1, f32[4,128,256]{2,1,0:T(8,128)} %emb.2, bf16[4,128]{1,0:T(4,128)(2,1)} %col_marg.1), custom_call_target="tpu_custom_call" | custom-call | bytes 1048576 | tf_op jit(solution)/shard_map/pallas_call | solution.py:50
  2.6 4.1 %collective-permute-start.1 = (bf16[272,256]{1,0:T(8,128)(2,1)}, bf16[272,256]{1,0:T(8,128)(2,1)S(1)}, u32[]{:S(2)}, u32[]{:S(2)}) collective-permute-start(bf16[272,256]{1,0:T(8,128)(2,1)} %get-tuple-element.35.refs_0_), channel_id=1, source_target_pairs={{0,4},{1,5},{2,6},{3,7},{4,0},{5,1},{6,2},{7,3},{8,12},{9,13},{10,... | collective-permute-start | bytes 417800 | tf_op jit(solution)/shard_map/ppermute | solution.py:359
  6.7 2.4 %collective-permute-start.5 = (bf16[528,256]{1,0:T(8,128)(2,1)}, bf16[528,256]{1,0:T(8,128)(2,1)S(1)}, u32[]{:S(2)}, u32[]{:S(2)}) collective-permute-start(bf16[528,256]{1,0:T(8,128)(2,1)} %get-tuple-element.37.refs_6_), channel_id=1, source_target_pairs={{0,24},{8,16},{16,8},{24,0},{1,25},{9,17},{17,9},{25,1},{2,26},{10... | collective-permute-start | bytes 811016 | tf_op jit(solution)/shard_map/ppermute | solution.py:359
  10.2 1.6 %collective-permute-start = (bf16[272,256]{1,0:T(8,128)(2,1)}, bf16[272,256]{1,0:T(8,128)(2,1)S(1)}, u32[]{:S(2)}, u32[]{:S(2)}) collective-permute-start(bf16[272,256]{1,0:T(8,128)(2,1)} %get-tuple-element.35.refs_0_), channel_id=1, source_target_pairs={{0,2},{1,3},{2,0},{3,1},{4,6},{5,7},{6,4},{7,5},{8,10},{9,11},{10,... | collective-permute-start | bytes 417800 | tf_op jit(solution)/shard_map/ppermute | solution.py:359
  12.4 2.5 %shard_map.86 = (f32[8,512,512]{2,1,0:T(8,128)S(1)}, bf16[8,512,512]{2,1,0:T(8,128)(2,1)S(1)}, f32[8,128]{1,0:T(8,128)S(1)}) custom-call(s32[1]{0:T(128)} %bitcast.7.used, s32[8,512,512]{2,1,0:T(8,128)} %bitcast.16), custom_call_target="tpu_custom_call" | custom-call | bytes 12582912 | tf_op jit(solution)/shard_map/pallas_call | solution.py:99
  17.3 4.3 %collective-permute-done.4.refs_5_.refs_8_ = bf16[528,256]{1,0:T(8,128)(2,1)S(1)} collective-permute-done((bf16[528,256]{1,0:T(8,128)(2,1)}, bf16[528,256]{1,0:T(8,128)(2,1)S(1)}, u32[]{:S(2)}, u32[]{:S(2)}) %collective-permute-start.4) | collective-permute-done | bytes 270368 | tf_op jit(solution)/shard_map/ppermute | solution.py:359
  21.8 1.9 %collective-permute-done.6.refs_5_ = bf16[4,272,256]{2,1,0:T(8,128)(2,1)S(1)} collective-permute-done((bf16[4,272,256]{2,1,0:T(8,128)(2,1)S(1)}, bf16[4,272,256]{2,1,0:T(8,128)(2,1)S(1)}, u32[]{:S(2)}, u32[]{:S(2)}) %collective-permute-start.6) | collective-permute-done | bytes 557088 | tf_op jit(solution)/shard_map/ppermute | solution.py:359
  23.7 3.8 %shard_map.90 = (f32[4,4,64,256]{3,2,1,0:T(8,128)S(1)}, bf16[4,4,64,256]{3,2,1,0:T(8,128)(2,1)S(1)}, bf16[4,128,256]{2,1,0:T(8,128)(2,1)S(1)}, bf16[4,128,256]{2...) custom-call(s32[2,8]{1,0:T(2,128)S(1)} %bitcast.14, ...), custom_call_target="tpu_custom_call" | custom-call | flops 3221225472 | bytes 16777216 | tf_op jit(solution)/shard_map/pallas_call | solution.py:275
  27.6 3.2 %collective-permute-start.11 = (bf16[4,128,256]{2,1,0:T(8,128)(2,1)S(1)}, bf16[4,128,256]{2,1,0:T(8,128)(2,1)S(1)}, u32[]{:S(2)}, u32[]{:S(2)}) collective-permute-start(bf16[4,128,256]{2,1,0:T(8,128)(2,1)S(1)} %get-tuple-element.45), channel_id=1, source_target_pairs={{0,8},{8,0},{16,24},{24,16},{1,9},{9,1},{17,25},{25,17},{2,10},{10... | collective-permute-start | bytes 786440 | tf_op jit(solution)/shard_map/ppermute | solution.py:359
  30.8 1.5 %collective-permute-start.13 = (bf16[4,128,256]{2,1,0:T(8,128)(2,1)S(1)}, bf16[4,128,256]{2,1,0:T(8,128)(2,1)S(1)}, u32[]{:S(2)}, u32[]{:S(2)}) collective-permute-start(bf16[4,128,256]{2,1,0:T(8,128)(2,1)S(1)} %get-tuple-element.47), channel_id=1, source_target_pairs={{0,24},{8,16},{16,8},{24,0},{1,25},{9,17},{17,9},{25,1},{2,26},{10... | collective-permute-start | bytes 786440 | tf_op jit(solution)/shard_map/ppermute | solution.py:359
  32.4 3.2 %collective-permute-start.8 = (bf16[4,64,256]{2,1,0:T(8,128)(2,1)S(1)}, bf16[4,64,256]{2,1,0:T(8,128)(2,1)S(1)}, u32[]{:S(2)}, u32[]{:S(2)}) collective-permute-start(bf16[4,64,256]{2,1,0:T(8,128)(2,1)S(1)} %get-tuple-element.42), channel_id=1, source_target_pairs={{0,2},{1,3},{2,0},{3,1},{4,6},{5,7},{6,4},{7,5},{8,10},{9,11},{10,... | collective-permute-start | bytes 393224 | tf_op jit(solution)/shard_map/ppermute | solution.py:359
  35.7 4.3 %collective-permute-done.8.refs_1_ = bf16[4,64,256]{2,1,0:T(8,128)(2,1)S(1)} collective-permute-done((bf16[4,64,256]{2,1,0:T(8,128)(2,1)S(1)}, bf16[4,64,256]{2,1,0:T(8,128)(2,1)S(1)}, u32[]{:S(2)}, u32[]{:S(2)}) %collective-permute-start.8) | collective-permute-done | bytes 131104 | tf_op jit(solution)/shard_map/ppermute | solution.py:359
  40.1 4.7 %collective-permute-done.12.refs_2_ = bf16[4,128,256]{2,1,0:T(8,128)(2,1)S(1)} collective-permute-done((bf16[4,128,256]{2,1,0:T(8,128)(2,1)S(1)}, bf16[4,128,256]{2,1,0:T(8,128)(2,1)S(1)}, u32[]{:S(2)}, u32[]{:S(2)}) %collective-permute-start.12) | collective-permute-done | bytes 262176 | tf_op jit(solution)/shard_map/ppermute | solution.py:359
  47.3 1.6 %collective-permute-start.18 = (bf16[512,256]{1,0:T(8,128)(2,1)S(1)}, bf16[512,256]{1,0:T(8,128)(2,1)S(1)}, u32[]{:S(2)}, u32[]{:S(2)}) collective-permute-start(bf16[512,256]{1,0:T(8,128)(2,1)S(1)} %get-tuple-element.48.refs_3_.refs_6_), channel_id=1, source_target_pairs={{0,8},{8,0},{16,24},{24,16},{1,9},{9,1},{17,25},{25,17},{2,10},{10... | collective-permute-start | bytes 786440 | tf_op jit(solution)/shard_map/ppermute | solution.py:359
  49.0 2.7 %collective-permute-start.14 = (bf16[256,256]{1,0:T(8,128)(2,1)S(1)}, bf16[256,256]{1,0:T(8,128)(2,1)S(1)}, u32[]{:S(2)}, u32[]{:S(2)}) collective-permute-start(bf16[256,256]{1,0:T(8,128)(2,1)S(1)} %get-tuple-element.50.refs_0_), channel_id=1, source_target_pairs={{0,2},{1,3},{2,0},{3,1},{4,6},{5,7},{6,4},{7,5},{8,10},{9,11},{10,... | collective-permute-start | bytes 393224 | tf_op jit(solution)/shard_map/ppermute | solution.py:359
  51.7 3.2 %collective-permute-done.15.refs_0_ = bf16[256,256]{1,0:T(8,128)(2,1)S(1)} collective-permute-done((bf16[256,256]{1,0:T(8,128)(2,1)S(1)}, bf16[256,256]{1,0:T(8,128)(2,1)S(1)}, u32[]{:S(2)}, u32[]{:S(2)}) %collective-permute-start.15) | collective-permute-done | bytes 131104 | tf_op jit(solution)/shard_map/ppermute | solution.py:359
  56.5 2.6 %collective-permute-done.19.refs_5_.refs_8_ = bf16[512,256]{1,0:T(8,128)(2,1)S(1)} collective-permute-done((bf16[512,256]{1,0:T(8,128)(2,1)S(1)}, bf16[512,256]{1,0:T(8,128)(2,1)S(1)}, u32[]{:S(2)}, u32[]{:S(2)}) %collective-permute-start.19) | collective-permute-done | bytes 262176 | tf_op jit(solution)/shard_map/ppermute | solution.py:359
  60.4 1.9 %collective-permute-done.20.refs_5_ = bf16[4,256,256]{2,1,0:T(8,128)(2,1)S(1)} collective-permute-done((bf16[4,256,256]{2,1,0:T(8,128)(2,1)S(1)}, bf16[4,256,256]{2,1,0:T(8,128)(2,1)S(1)}, u32[]{:S(2)}, u32[]{:S(2)}) %collective-permute-start.20) | collective-permute-done | bytes 524320 | tf_op jit(solution)/shard_map/ppermute | solution.py:359
  62.3 3.5 %shard_map.97 = (f32[4,4,64,256]{3,2,1,0:T(8,128)S(1)}, bf16[4,4,64,256]{3,2,1,0:T(8,128)(2,1)S(1)}, bf16[4,128,256]{2,1,0:T(8,128)(2,1)S(1)}, bf16[4,128,256]{2...) custom-call(s32[2,8]{1,0:T(2,128)S(1)} %bitcast.15, s32[1]{0:T(128)} %bitcast.9.refs_1_, ...), custom_call_target="tpu_custom_call" | custom-call | flops 3221225472 | bytes 16777216 | tf_op jit(solution)/shard_map/pallas_call | solution.py:275
  65.9 2.6 %collective-permute-start.25 = (bf16[4,128,256]{2,1,0:T(8,128)(2,1)S(1)}, bf16[4,128,256]{2,1,0:T(8,128)(2,1)S(1)}, u32[]{:S(2)}, u32[]{:S(2)}) collective-permute-start(bf16[4,128,256]{2,1,0:T(8,128)(2,1)S(1)} %get-tuple-element.61), channel_id=1, source_target_pairs={{0,8},{8,0},{16,24},{24,16},{1,9},{9,1},{17,25},{25,17},{2,10},{10... | collective-permute-start | bytes 786440 | tf_op jit(solution)/shard_map/ppermute | solution.py:359
  68.4 1.5 %collective-permute-start.27 = (bf16[4,128,256]{2,1,0:T(8,128)(2,1)S(1)}, bf16[4,128,256]{2,1,0:T(8,128)(2,1)S(1)}, u32[]{:S(2)}, u32[]{:S(2)}) collective-permute-start(bf16[4,128,256]{2,1,0:T(8,128)(2,1)S(1)} %get-tuple-element.63), channel_id=1, source_target_pairs={{0,24},{8,16},{16,8},{24,0},{1,25},{9,17},{17,9},{25,1},{2,26},{10... | collective-permute-start | bytes 786440 | tf_op jit(solution)/shard_map/ppermute | solution.py:359
  70.0 3.5 %collective-permute-start.22 = (bf16[4,64,256]{2,1,0:T(8,128)(2,1)S(1)}, bf16[4,64,256]{2,1,0:T(8,128)(2,1)S(1)}, u32[]{:S(2)}, u32[]{:S(2)}) collective-permute-start(bf16[4,64,256]{2,1,0:T(8,128)(2,1)S(1)} %get-tuple-element.57), channel_id=1, source_target_pairs={{0,2},{1,3},{2,0},{3,1},{4,6},{5,7},{6,4},{7,5},{8,10},{9,11},{10,... | collective-permute-start | bytes 393224 | tf_op jit(solution)/shard_map/ppermute | solution.py:359
  73.6 4.3 %collective-permute-done.22.refs_1_ = bf16[4,64,256]{2,1,0:T(8,128)(2,1)S(1)} collective-permute-done((bf16[4,64,256]{2,1,0:T(8,128)(2,1)S(1)}, bf16[4,64,256]{2,1,0:T(8,128)(2,1)S(1)}, u32[]{:S(2)}, u32[]{:S(2)}) %collective-permute-start.22) | collective-permute-done | bytes 131104 | tf_op jit(solution)/shard_map/ppermute | solution.py:359
  78.0 4.4 %collective-permute-done.26.refs_2_ = bf16[4,128,256]{2,1,0:T(8,128)(2,1)S(1)} collective-permute-done((bf16[4,128,256]{2,1,0:T(8,128)(2,1)S(1)}, bf16[4,128,256]{2,1,0:T(8,128)(2,1)S(1)}, u32[]{:S(2)}, u32[]{:S(2)}) %collective-permute-start.26) | collective-permute-done | bytes 262176 | tf_op jit(solution)/shard_map/ppermute | solution.py:359
  (58 shorter events, 11.8 us)
Async XLA Ops:
  2.6 12.4 %collective-permute-start.1 = (bf16[272,256]{1,0:T(8,128)(2,1)}, bf16[272,256]{1,0:T(8,128)(2,1)S(1)}, u32[]{:S(2)}, u32[]{:S(2)}) collective-permute-start(bf16[272,256]{1,0:T(8,128)(2,1)} %get-tuple-element.35.refs_0_), channel_id=1, source_target_pairs={{0,4},{1,5},{2,6},{3,7},{4,0},{5,1},{6,2},{7,3},{8,12},{9,13},{10,... | collective-permute-start | bytes 417800 | tf_op jit(solution)/shard_map/ppermute | solution.py:359
  6.7 10.6 %collective-permute-start.5 = (bf16[528,256]{1,0:T(8,128)(2,1)}, bf16[528,256]{1,0:T(8,128)(2,1)S(1)}, u32[]{:S(2)}, u32[]{:S(2)}) collective-permute-start(bf16[528,256]{1,0:T(8,128)(2,1)} %get-tuple-element.37.refs_6_), channel_id=1, source_target_pairs={{0,24},{8,16},{16,8},{24,0},{1,25},{9,17},{17,9},{25,1},{2,26},{10... | collective-permute-start | bytes 811016 | tf_op jit(solution)/shard_map/ppermute | solution.py:359
  9.2 12.4 %collective-permute-start.4 = (bf16[528,256]{1,0:T(8,128)(2,1)}, bf16[528,256]{1,0:T(8,128)(2,1)S(1)}, u32[]{:S(2)}, u32[]{:S(2)}) collective-permute-start(bf16[528,256]{1,0:T(8,128)(2,1)} %get-tuple-element.37.refs_6_), channel_id=1, source_target_pairs={{0,16},{8,24},{16,0},{24,8},{1,17},{9,25},{17,1},{25,9},{2,18},{10... | collective-permute-start | bytes 811016 | tf_op jit(solution)/shard_map/ppermute | solution.py:359
  9.7 12.0 %collective-permute-start.3 = (bf16[528,256]{1,0:T(8,128)(2,1)}, bf16[528,256]{1,0:T(8,128)(2,1)S(1)}, u32[]{:S(2)}, u32[]{:S(2)}) collective-permute-start(bf16[528,256]{1,0:T(8,128)(2,1)} %get-tuple-element.37.refs_6_), channel_id=1, source_target_pairs={{0,8},{8,0},{16,24},{24,16},{1,9},{9,1},{17,25},{25,17},{2,10},{10... | collective-permute-start | bytes 811016 | tf_op jit(solution)/shard_map/ppermute | solution.py:359
  10.2 6.3 %collective-permute-start = (bf16[272,256]{1,0:T(8,128)(2,1)}, bf16[272,256]{1,0:T(8,128)(2,1)S(1)}, u32[]{:S(2)}, u32[]{:S(2)}) collective-permute-start(bf16[272,256]{1,0:T(8,128)(2,1)} %get-tuple-element.35.refs_0_), channel_id=1, source_target_pairs={{0,2},{1,3},{2,0},{3,1},{4,6},{5,7},{6,4},{7,5},{8,10},{9,11},{10,... | collective-permute-start | bytes 417800 | tf_op jit(solution)/shard_map/ppermute | solution.py:359
  15.0 6.7 %collective-permute-start.2 = (bf16[272,256]{1,0:T(8,128)(2,1)S(1)}, bf16[272,256]{1,0:T(8,128)(2,1)S(1)}, u32[]{:S(2)}, u32[]{:S(2)}) collective-permute-start(bf16[272,256]{1,0:T(8,128)(2,1)S(1)} %bitcast.10), channel_id=1, source_target_pairs={{0,2},{1,3},{2,0},{3,1},{4,6},{5,7},{6,4},{7,5},{8,10},{9,11},{10,... | collective-permute-start | bytes 417800 | tf_op jit(solution)/shard_map/ppermute | solution.py:359
  27.6 12.5 %collective-permute-start.11 = (bf16[4,128,256]{2,1,0:T(8,128)(2,1)S(1)}, bf16[4,128,256]{2,1,0:T(8,128)(2,1)S(1)}, u32[]{:S(2)}, u32[]{:S(2)}) collective-permute-start(bf16[4,128,256]{2,1,0:T(8,128)(2,1)S(1)} %get-tuple-element.45), channel_id=1, source_target_pairs={{0,8},{8,0},{16,24},{24,16},{1,9},{9,1},{17,25},{25,17},{2,10},{10... | collective-permute-start | bytes 786440 | tf_op jit(solution)/shard_map/ppermute | solution.py:359
  30.8 14.0 %collective-permute-start.12 = (bf16[4,128,256]{2,1,0:T(8,128)(2,1)S(1)}, bf16[4,128,256]{2,1,0:T(8,128)(2,1)S(1)}, u32[]{:S(2)}, u32[]{:S(2)}) collective-permute-start(bf16[4,128,256]{2,1,0:T(8,128)(2,1)S(1)} %get-tuple-element.46), channel_id=1, source_target_pairs={{0,16},{8,24},{16,0},{24,8},{1,17},{9,25},{17,1},{25,9},{2,18},{10... | collective-permute-start | bytes 786440 | tf_op jit(solution)/shard_map/ppermute | solution.py:359
  30.8 14.0 %collective-permute-start.13 = (bf16[4,128,256]{2,1,0:T(8,128)(2,1)S(1)}, bf16[4,128,256]{2,1,0:T(8,128)(2,1)S(1)}, u32[]{:S(2)}, u32[]{:S(2)}) collective-permute-start(bf16[4,128,256]{2,1,0:T(8,128)(2,1)S(1)} %get-tuple-element.47), channel_id=1, source_target_pairs={{0,24},{8,16},{16,8},{24,0},{1,25},{9,17},{17,9},{25,1},{2,26},{10... | collective-permute-start | bytes 786440 | tf_op jit(solution)/shard_map/ppermute | solution.py:359
  32.4 7.5 %collective-permute-start.8 = (bf16[4,64,256]{2,1,0:T(8,128)(2,1)S(1)}, bf16[4,64,256]{2,1,0:T(8,128)(2,1)S(1)}, u32[]{:S(2)}, u32[]{:S(2)}) collective-permute-start(bf16[4,64,256]{2,1,0:T(8,128)(2,1)S(1)} %get-tuple-element.42), channel_id=1, source_target_pairs={{0,2},{1,3},{2,0},{3,1},{4,6},{5,7},{6,4},{7,5},{8,10},{9,11},{10,... | collective-permute-start | bytes 393224 | tf_op jit(solution)/shard_map/ppermute | solution.py:359
  35.6 10.6 %collective-permute-start.10 = (bf16[4,64,256]{2,1,0:T(8,128)(2,1)S(1)}, bf16[4,64,256]{2,1,0:T(8,128)(2,1)S(1)}, u32[]{:S(2)}, u32[]{:S(2)}) collective-permute-start(bf16[4,64,256]{2,1,0:T(8,128)(2,1)S(1)} %get-tuple-element.43), channel_id=1, source_target_pairs={{0,2},{1,3},{2,0},{3,1},{4,6},{5,7},{6,4},{7,5},{8,10},{9,11},{10,... | collective-permute-start | bytes 393224 | tf_op jit(solution)/shard_map/ppermute | solution.py:359
  40.0 6.2 %collective-permute-start.9 = (bf16[4,64,256]{2,1,0:T(8,128)(2,1)S(1)}, bf16[4,64,256]{2,1,0:T(8,128)(2,1)S(1)}, u32[]{:S(2)}, u32[]{:S(2)}) collective-permute-start(bf16[4,64,256]{2,1,0:T(8,128)(2,1)S(1)} %shard_map.92.refs_4_), channel_id=1, source_target_pairs={{0,4},{1,5},{2,6},{3,7},{4,0},{5,1},{6,2},{7,3},{8,12},{9,13},{10,... | collective-permute-start | bytes 393224 | tf_op jit(solution)/shard_map/ppermute | solution.py:359
  45.0 10.3 %collective-permute-start.16 = (bf16[512,256]{1,0:T(8,128)(2,1)S(1)}, bf16[512,256]{1,0:T(8,128)(2,1)S(1)}, u32[]{:S(2)}, u32[]{:S(2)}) collective-permute-start(bf16[512,256]{1,0:T(8,128)(2,1)S(1)} %get-tuple-element.48.refs_3_.refs_6_), channel_id=1, source_target_pairs={{0,24},{8,16},{16,8},{24,0},{1,25},{9,17},{17,9},{25,1},{2,26},{10... | collective-permute-start | bytes 786440 | tf_op jit(solution)/shard_map/ppermute | solution.py:359
  46.3 8.6 %collective-permute-start.15 = (bf16[256,256]{1,0:T(8,128)(2,1)S(1)}, bf16[256,256]{1,0:T(8,128)(2,1)S(1)}, u32[]{:S(2)}, u32[]{:S(2)}) collective-permute-start(bf16[256,256]{1,0:T(8,128)(2,1)S(1)} %get-tuple-element.50.refs_0_), channel_id=1, source_target_pairs={{0,4},{1,5},{2,6},{3,7},{4,0},{5,1},{6,2},{7,3},{8,12},{9,13},{10,... | collective-permute-start | bytes 393224 | tf_op jit(solution)/shard_map/ppermute | solution.py:359
  47.0 12.1 %collective-permute-start.19 = (bf16[512,256]{1,0:T(8,128)(2,1)S(1)}, bf16[512,256]{1,0:T(8,128)(2,1)S(1)}, u32[]{:S(2)}, u32[]{:S(2)}) collective-permute-start(bf16[512,256]{1,0:T(8,128)(2,1)S(1)} %get-tuple-element.48.refs_3_.refs_6_), channel_id=1, source_target_pairs={{0,16},{8,24},{16,0},{24,8},{1,17},{9,25},{17,1},{25,9},{2,18},{10... | collective-permute-start | bytes 786440 | tf_op jit(solution)/shard_map/ppermute | solution.py:359
  47.3 11.8 %collective-permute-start.18 = (bf16[512,256]{1,0:T(8,128)(2,1)S(1)}, bf16[512,256]{1,0:T(8,128)(2,1)S(1)}, u32[]{:S(2)}, u32[]{:S(2)}) collective-permute-start(bf16[512,256]{1,0:T(8,128)(2,1)S(1)} %get-tuple-element.48.refs_3_.refs_6_), channel_id=1, source_target_pairs={{0,8},{8,0},{16,24},{24,16},{1,9},{9,1},{17,25},{25,17},{2,10},{10... | collective-permute-start | bytes 786440 | tf_op jit(solution)/shard_map/ppermute | solution.py:359
  49.0 7.5 %collective-permute-start.14 = (bf16[256,256]{1,0:T(8,128)(2,1)S(1)}, bf16[256,256]{1,0:T(8,128)(2,1)S(1)}, u32[]{:S(2)}, u32[]{:S(2)}) collective-permute-start(bf16[256,256]{1,0:T(8,128)(2,1)S(1)} %get-tuple-element.50.refs_0_), channel_id=1, source_target_pairs={{0,2},{1,3},{2,0},{3,1},{4,6},{5,7},{6,4},{7,5},{8,10},{9,11},{10,... | collective-permute-start | bytes 393224 | tf_op jit(solution)/shard_map/ppermute | solution.py:359
  55.2 5.0 %collective-permute-start.17 = (bf16[256,256]{1,0:T(8,128)(2,1)S(1)}, bf16[256,256]{1,0:T(8,128)(2,1)S(1)}, u32[]{:S(2)}, u32[]{:S(2)}) collective-permute-start(bf16[256,256]{1,0:T(8,128)(2,1)S(1)} %bitcast.12), channel_id=1, source_target_pairs={{0,2},{1,3},{2,0},{3,1},{4,6},{5,7},{6,4},{7,5},{8,10},{9,11},{10,... | collective-permute-start | bytes 393224 | tf_op jit(solution)/shard_map/ppermute | solution.py:359
  65.9 12.1 %collective-permute-start.25 = (bf16[4,128,256]{2,1,0:T(8,128)(2,1)S(1)}, bf16[4,128,256]{2,1,0:T(8,128)(2,1)S(1)}, u32[]{:S(2)}, u32[]{:S(2)}) collective-permute-start(bf16[4,128,256]{2,1,0:T(8,128)(2,1)S(1)} %get-tuple-element.61), channel_id=1, source_target_pairs={{0,8},{8,0},{16,24},{24,16},{1,9},{9,1},{17,25},{25,17},{2,10},{10... | collective-permute-start | bytes 786440 | tf_op jit(solution)/shard_map/ppermute | solution.py:359
  68.4 14.0 %collective-permute-start.26 = (bf16[4,128,256]{2,1,0:T(8,128)(2,1)S(1)}, bf16[4,128,256]{2,1,0:T(8,128)(2,1)S(1)}, u32[]{:S(2)}, u32[]{:S(2)}) collective-permute-start(bf16[4,128,256]{2,1,0:T(8,128)(2,1)S(1)} %get-tuple-element.62), channel_id=1, source_target_pairs={{0,16},{8,24},{16,0},{24,8},{1,17},{9,25},{17,1},{25,9},{2,18},{10... | collective-permute-start | bytes 786440 | tf_op jit(solution)/shard_map/ppermute | solution.py:359
  68.4 14.0 %collective-permute-start.27 = (bf16[4,128,256]{2,1,0:T(8,128)(2,1)S(1)}, bf16[4,128,256]{2,1,0:T(8,128)(2,1)S(1)}, u32[]{:S(2)}, u32[]{:S(2)}) collective-permute-start(bf16[4,128,256]{2,1,0:T(8,128)(2,1)S(1)} %get-tuple-element.63), channel_id=1, source_target_pairs={{0,24},{8,16},{16,8},{24,0},{1,25},{9,17},{17,9},{25,1},{2,26},{10... | collective-permute-start | bytes 786440 | tf_op jit(solution)/shard_map/ppermute | solution.py:359
  70.0 7.8 %collective-permute-start.22 = (bf16[4,64,256]{2,1,0:T(8,128)(2,1)S(1)}, bf16[4,64,256]{2,1,0:T(8,128)(2,1)S(1)}, u32[]{:S(2)}, u32[]{:S(2)}) collective-permute-start(bf16[4,64,256]{2,1,0:T(8,128)(2,1)S(1)} %get-tuple-element.57), channel_id=1, source_target_pairs={{0,2},{1,3},{2,0},{3,1},{4,6},{5,7},{6,4},{7,5},{8,10},{9,11},{10,... | collective-permute-start | bytes 393224 | tf_op jit(solution)/shard_map/ppermute | solution.py:359
  73.5 9.9 %collective-permute-start.24 = (bf16[4,64,256]{2,1,0:T(8,128)(2,1)S(1)}, bf16[4,64,256]{2,1,0:T(8,128)(2,1)S(1)}, u32[]{:S(2)}, u32[]{:S(2)}) collective-permute-start(bf16[4,64,256]{2,1,0:T(8,128)(2,1)S(1)} %get-tuple-element.58), channel_id=1, source_target_pairs={{0,2},{1,3},{2,0},{3,1},{4,6},{5,7},{6,4},{7,5},{8,10},{9,11},{10,... | collective-permute-start | bytes 393224 | tf_op jit(solution)/shard_map/ppermute | solution.py:359
  77.9 5.9 %collective-permute-start.23 = (bf16[4,64,256]{2,1,0:T(8,128)(2,1)S(1)}, bf16[4,64,256]{2,1,0:T(8,128)(2,1)S(1)}, u32[]{:S(2)}, u32[]{:S(2)}) collective-permute-start(bf16[4,64,256]{2,1,0:T(8,128)(2,1)S(1)} %shard_map.99.refs_3_.refs_4_), channel_id=1, source_target_pairs={{0,4},{1,5},{2,6},{3,7},{4,0},{5,1},{6,2},{7,3},{8,12},{9,13},{10,... | collective-permute-start | bytes 393224 | tf_op jit(solution)/shard_map/ppermute | solution.py:359
  (9 other events, 119.9 us)

commit v3 on v2

--- a/solution.py
+++ b/solution.py
@@ -110,21 +110,26 @@
     )(used, tiles)
 
 
-def join_kernel(n_parts, *refs):
-    out = refs[-1]
-    for n in range(n_parts):
-        out[n] = refs[n][...]
-
-
-def join(parts, afters):
-    return pl.pallas_call(
-        functools.partial(join_kernel, len(parts)),
-        out_shape=shape((len(parts), *parts[0].shape), parts[0].dtype),
-        in_specs=[VMEM] * len(parts) + [ANY] * len(afters),
-        out_specs=VMEM,
-        compiler_params=pltpu.CompilerParams(vmem_limit_bytes=SMALL),
-        cost_estimate=cost(0, 1 << 20),
-    )(*parts, *afters)
+def join_kernel(sizes, *refs):
+    parts, outs = list(refs[: sum(sizes)]), refs[-len(sizes) :]
+    for out in outs:
+        for n in range(out.shape[0]):
+            part = parts.pop(0)
+            out[n] = part[0] if len(part.shape) == 3 else part[...]
+
+
+def join(parts, sizes, afters):
+    piece = parts[0].shape[-2:]
+    return list(
+        pl.pallas_call(
+            functools.partial(join_kernel, sizes),
+            out_shape=[shape((size, *piece), bf16) for size in sizes],
+            in_specs=[VMEM] * len(parts) + [ANY] * len(afters),
+            out_specs=[VMEM] * len(sizes),
+            compiler_params=pltpu.CompilerParams(vmem_limit_bytes=SMALL),
+            cost_estimate=cost(0, 1 << 20),
+        )(*parts, *afters)
+    )
 
 
 def marg_table(pieces, owners, part, size):
@@ -145,8 +150,8 @@
         return [refs.pop(0) for _ in range(n)]
 
     listing, used, logs, weights = take(4)
-    sides = take(n_sides)
-    col_in = take(n_col)
+    sides, col_in = take(n_sides), take(n_col)
+    row_in = [side.at[n] for side in sides for n in range(side.shape[0])]
     if not first:
         left, right = take(2)
     keep, swap = take(2)
@@ -164,7 +169,6 @@
     col_owners = [me_row ^ k for k in col_owner]
     row_zero, col_zero = me_row * row_blocks, me_col * col_blocks
     count = used[0]
-    row_in = [side.at[n] for side in sides for n in range(side.shape[0])]
 
     for pieces, owners, panel, part in (
         (row_in, row_owners, row_panel, row_part),
@@ -379,10 +383,14 @@
     for substep in range(2):
         crossed = hop(row_pay, far)
         col_in = [col_pay] + [send(col_pay, "row", n_row_dev, k) for k in col_owner[1:]]
-        (crossed,) = join([crossed], [tabs_made if substep == 0 else col_in[-1]])
+        if substep == 0:
+            before_leg, before_swap, sizes = [tabs_made], col_in[1:-1], [1, far - 1, 1, far - 1]
+        else:
+            before_leg, before_swap, sizes = col_in[-1:], [], [far, 1, far - 1]
+        (crossed,) = join([crossed], [1], before_leg)
         row_in = [row_pay] + [hop(row_pay, k) for k in near] + [crossed] + [hop(crossed, k) for k in near]
-        row_in = [join(row_in, col_in[1:])]
-        row_in += [send(pieces, "col", n_col_dev, 1) for pieces in row_in]
+        row_in = join(row_in, sizes, before_swap)
+        row_in += [send(piece, "col", n_col_dev, 1) for piece in row_in]
         keep, swap, col_out, made = work(
             listing, used, tabs, row_in, col_in, tables, row_owner, col_owner, dims
         )

time: 85.7 us -> 86.6 us (1.011); the launches traced: 84.6 us -> 86.5 us
  starting transfers between devices: 34.1 us -> 43.3 us
  waiting for transfers between devices: 35 us -> 30.6 us
  Pallas kernels: 14 us -> 11.1 us
    ppermute x28 -> x33, starting transfers between devices: 34.1 us -> 43.3 us  [send(): return lax.ppermute(x, axis, [(k, k ^ mask) for k in range(count)])]
    ppermute x28 -> x33, waiting for transfers between devices: 35 us -> 30.6 us  [send(): return lax.ppermute(x, axis, [(k, k ^ mask) for k in range(count)])]
    pallas_call x2, Pallas kernels: 7.22 us -> 5.17 us  [work(): pl.pallas_call(functools.partial(work_kernel, first, len(row_in), n_row,...]
  transfers between devices with their start and end apart: 28 -> 33, of which waited for: 15 -> 12; matrix products, arithmetic and copies ran while one was open for 0% -> 0% of each run, Pallas kernels for 5% -> 4%
where the time goes in v3:
time: 86.6 us; the launch traced here: 86.5 us
  starting transfers between devices  43.3 us (50%)
  waiting for transfers between devices  30.6 us (35%)
  Pallas kernels  11.1 us (13%)
  between operations  1.47 us (2%)
    ppermute x33, starting transfers between devices, send(): return lax.ppermute(x, axis, [(k, k ^ mask) for k in range(count)])  43.3 us
    ppermute x33, waiting for transfers between devices, send(): return lax.ppermute(x, axis, [(k, k ^ mask) for k in range(count)])  30.6 us
    pallas_call x2, Pallas kernels, work(): pl.pallas_call(functools.partial(work_kernel, first, len(row_in), n_row,...  5.17 us
    pallas_call x4, Pallas kernels, update(): pl.pallas_call(functools.partial(update_kernel, len(parts)), out_shape=ou...  1.99 us
    pallas_call x1, Pallas kernels, pack(): pl.pallas_call(pack_kernel, out_shape=[shape((e.shape[0] * e.shape[1] + M...  1.93 us
  transfers between devices with their start and end apart: 33, of which 12 were waited for; matrix products, arithmetic and copies ran while one was open for 0% of the time, Pallas kernels for 4%

profile of v3, /device:TPU:0, one launch (start us, length us, event | category | flops | bytes accessed | tf_op | source)
XLA Modules:
  0.0 86.5 jit_solution(2989316812041237340)
XLA Ops:
  0.6 1.9 %shard_map.87 = (bf16[272,256]{1,0:T(8,128)(2,1)}, bf16[528,256]{1,0:T(8,128)(2,1)}) custom-call(f32[4,64,256]{2,1,0:T(8,128)} %emb.3, bf16[4,64]{1,0:T(4,128)(2,1)} %row_marg.1, f32[4,128,256]{2,1,0:T(8,128)} %emb.2, bf16[4,128]{1,0:T(4,128)(2,1)} %col_marg.1), custom_call_target="tpu_custom_call" | custom-call | bytes 1048576 | tf_op jit(solution)/shard_map/pallas_call | solution.py:50
  2.6 4.1 %collective-permute-start.1 = (bf16[272,256]{1,0:T(8,128)(2,1)}, bf16[272,256]{1,0:T(8,128)(2,1)S(1)}, u32[]{:S(2)}, u32[]{:S(2)}) collective-permute-start(bf16[272,256]{1,0:T(8,128)(2,1)} %get-tuple-element.42.refs_0_), channel_id=1, source_target_pairs={{0,4},{1,5},{2,6},{3,7},{4,0},{5,1},{6,2},{7,3},{8,12},{9,13},{10,... | collective-permute-start | bytes 417800 | tf_op jit(solution)/shard_map/ppermute | solution.py:363
  9.7 1.6 %collective-permute-start = (bf16[272,256]{1,0:T(8,128)(2,1)}, bf16[272,256]{1,0:T(8,128)(2,1)S(1)}, u32[]{:S(2)}, u32[]{:S(2)}) collective-permute-start(bf16[272,256]{1,0:T(8,128)(2,1)} %get-tuple-element.42.refs_0_), channel_id=1, source_target_pairs={{0,2},{1,3},{2,0},{3,1},{4,6},{5,7},{6,4},{7,5},{8,10},{9,11},{10,... | collective-permute-start | bytes 417800 | tf_op jit(solution)/shard_map/ppermute | solution.py:363
  11.9 1.7 %shard_map.86 = (f32[8,512,512]{2,1,0:T(8,128)S(1)}, bf16[8,512,512]{2,1,0:T(8,128)(2,1)S(1)}, f32[8,128]{1,0:T(8,128)S(1)}) custom-call(s32[1]{0:T(128)} %bitcast.5.used, s32[8,512,512]{2,1,0:T(8,128)} %bitcast.10), custom_call_target="tpu_custom_call" | custom-call | bytes 12582912 | tf_op jit(solution)/shard_map/pallas_call | solution.py:99
  14.5 2.4 %collective-permute-start.9 = (bf16[528,256]{1,0:T(8,128)(2,1)S(1)}, bf16[528,256]{1,0:T(8,128)(2,1)S(1)}, u32[]{:S(2)}, u32[]{:S(2)}) collective-permute-start(bf16[528,256]{1,0:T(8,128)(2,1)S(1)} %copy-done.2), channel_id=1, source_target_pairs={{0,24},{8,16},{16,8},{24,0},{1,25},{9,17},{17,9},{25,1},{2,26},{10... | collective-permute-start | bytes 811016 | tf_op jit(solution)/shard_map/ppermute | solution.py:363
  17.0 3.2 %collective-permute-done.2.refs_3_ = bf16[1,272,256]{2,1,0:T(8,128)(2,1)S(1)} collective-permute-done((bf16[1,272,256]{2,1,0:T(8,128)(2,1)S(1)}, bf16[1,272,256]{2,1,0:T(8,128)(2,1)S(1)}, u32[]{:S(2)}, u32[]{:S(2)}) %collective-permute-start.2) | collective-permute-done | bytes 139296 | tf_op jit(solution)/shard_map/ppermute | solution.py:363
  21.3 2.7 %collective-permute-done.9.refs_15_ = bf16[528,256]{1,0:T(8,128)(2,1)S(1)} collective-permute-done((bf16[528,256]{1,0:T(8,128)(2,1)S(1)}, bf16[528,256]{1,0:T(8,128)(2,1)S(1)}, u32[]{:S(2)}, u32[]{:S(2)}) %collective-permute-start.9) | collective-permute-done | bytes 270368 | tf_op jit(solution)/shard_map/ppermute | solution.py:363
  24.0 2.7 %shard_map.90 = (f32[4,4,64,256]{3,2,1,0:T(8,128)S(1)}, bf16[4,4,64,256]{3,2,1,0:T(8,128)(2,1)S(1)}, bf16[4,128,256]{2,1,0:T(8,128)(2,1)S(1)}, bf16[4,128,256]{2...) custom-call(s32[2,8]{1,0:T(2,128)S(1)} %bitcast.8, ...), custom_call_target="tpu_custom_call" | custom-call | flops 3221225472 | bytes 16777216 | tf_op jit(solution)/shard_map/pallas_call | solution.py:279
  26.7 2.1 %collective-permute-start.10 = (bf16[4,4,64,256]{3,2,1,0:T(8,128)(2,1)S(1)}, bf16[4,4,64,256]{3,2,1,0:T(8,128)(2,1)S(1)}, u32[]{:S(2)}, u32[]{:S(2)}) collective-permute-start(bf16[4,4,64,256]{3,2,1,0:T(8,128)(2,1)S(1)} %get-tuple-element.50), channel_id=1, source_target_pairs={{0,1},{1,0},{2,3},{3,2},{4,5},{5,4},{6,7},{7,6},{8,9},{9,8},{10,11... | collective-permute-start | bytes 1572872 | tf_op jit(solution)/shard_map/ppermute | solution.py:363
  30.1 2.2 %collective-permute-start.16 = (bf16[4,128,256]{2,1,0:T(8,128)(2,1)S(1)}, bf16[4,128,256]{2,1,0:T(8,128)(2,1)S(1)}, u32[]{:S(2)}, u32[]{:S(2)}) collective-permute-start(bf16[4,128,256]{2,1,0:T(8,128)(2,1)S(1)} %get-tuple-element.58), channel_id=1, source_target_pairs={{0,24},{8,16},{16,8},{24,0},{1,25},{9,17},{17,9},{25,1},{2,26},{10... | collective-permute-start | bytes 786440 | tf_op jit(solution)/shard_map/ppermute | solution.py:363
  32.4 1.6 %collective-permute-start.11 = (bf16[4,64,256]{2,1,0:T(8,128)(2,1)S(1)}, bf16[4,64,256]{2,1,0:T(8,128)(2,1)S(1)}, u32[]{:S(2)}, u32[]{:S(2)}) collective-permute-start(bf16[4,64,256]{2,1,0:T(8,128)(2,1)S(1)} %get-tuple-element.53), channel_id=1, source_target_pairs={{0,2},{1,3},{2,0},{3,1},{4,6},{5,7},{6,4},{7,5},{8,10},{9,11},{10,... | collective-permute-start | bytes 393224 | tf_op jit(solution)/shard_map/ppermute | solution.py:363
  34.5 4.0 %collective-permute-done.11.refs_1_ = bf16[4,64,256]{2,1,0:T(8,128)(2,1)S(1)} collective-permute-done((bf16[4,64,256]{2,1,0:T(8,128)(2,1)S(1)}, bf16[4,64,256]{2,1,0:T(8,128)(2,1)S(1)}, u32[]{:S(2)}, u32[]{:S(2)}) %collective-permute-start.11) | collective-permute-done | bytes 131104 | tf_op jit(solution)/shard_map/ppermute | solution.py:363
  38.5 3.5 %collective-permute-start.12 = (bf16[4,64,256]{2,1,0:T(8,128)(2,1)S(1)}, bf16[4,64,256]{2,1,0:T(8,128)(2,1)S(1)}, u32[]{:S(2)}, u32[]{:S(2)}) collective-permute-start(bf16[4,64,256]{2,1,0:T(8,128)(2,1)S(1)} %shard_map.92.refs_4_), channel_id=1, source_target_pairs={{0,4},{1,5},{2,6},{3,7},{4,0},{5,1},{6,2},{7,3},{8,12},{9,13},{10,... | collective-permute-start | bytes 393224 | tf_op jit(solution)/shard_map/ppermute | solution.py:363
  42.0 2.1 %collective-permute-done.15.refs_2_ = bf16[4,128,256]{2,1,0:T(8,128)(2,1)S(1)} collective-permute-done((bf16[4,128,256]{2,1,0:T(8,128)(2,1)S(1)}, bf16[4,128,256]{2,1,0:T(8,128)(2,1)S(1)}, u32[]{:S(2)}, u32[]{:S(2)}) %collective-permute-start.15) | collective-permute-done | bytes 262176 | tf_op jit(solution)/shard_map/ppermute | solution.py:363
  48.1 2.8 %collective-permute-start.17 = (bf16[256,256]{1,0:T(8,128)(2,1)S(1)}, bf16[256,256]{1,0:T(8,128)(2,1)S(1)}, u32[]{:S(2)}, u32[]{:S(2)}) collective-permute-start(bf16[256,256]{1,0:T(8,128)(2,1)S(1)} %get-tuple-element.61.refs_0_), channel_id=1, source_target_pairs={{0,2},{1,3},{2,0},{3,1},{4,6},{5,7},{6,4},{7,5},{8,10},{9,11},{10,... | collective-permute-start | bytes 393224 | tf_op jit(solution)/shard_map/ppermute | solution.py:363
  50.9 3.6 %collective-permute-done.18.refs_0_ = bf16[256,256]{1,0:T(8,128)(2,1)S(1)} collective-permute-done((bf16[256,256]{1,0:T(8,128)(2,1)S(1)}, bf16[256,256]{1,0:T(8,128)(2,1)S(1)}, u32[]{:S(2)}, u32[]{:S(2)}) %collective-permute-start.18) | collective-permute-done | bytes 131104 | tf_op jit(solution)/shard_map/ppermute | solution.py:363
  56.6 2.9 %collective-permute-done.20.refs_3_ = bf16[1,256,256]{2,1,0:T(8,128)(2,1)S(1)} collective-permute-done((bf16[1,256,256]{2,1,0:T(8,128)(2,1)S(1)}, bf16[1,256,256]{2,1,0:T(8,128)(2,1)S(1)}, u32[]{:S(2)}, u32[]{:S(2)}) %collective-permute-start.20) | collective-permute-done | bytes 131104 | tf_op jit(solution)/shard_map/ppermute | solution.py:363
  62.5 2.4 %shard_map.97 = (f32[4,4,64,256]{3,2,1,0:T(8,128)S(1)}, bf16[4,4,64,256]{3,2,1,0:T(8,128)(2,1)S(1)}, bf16[4,128,256]{2,1,0:T(8,128)(2,1)S(1)}, bf16[4,128,256]{2...) custom-call(s32[2,8]{1,0:T(2,128)S(1)} %bitcast.9, s32[1]{0:T(128)} %bitcast.7.refs_1_, ...), custom_call_target="tpu_custom_call" | custom-call | flops 3221225472 | bytes 16777216 | tf_op jit(solution)/shard_map/pallas_call | solution.py:279
  65.0 2.0 %collective-permute-start.26 = (bf16[4,4,64,256]{3,2,1,0:T(8,128)(2,1)S(1)}, bf16[4,4,64,256]{3,2,1,0:T(8,128)(2,1)S(1)}, u32[]{:S(2)}, u32[]{:S(2)}) collective-permute-start(bf16[4,4,64,256]{3,2,1,0:T(8,128)(2,1)S(1)} %get-tuple-element.68), channel_id=1, source_target_pairs={{0,1},{1,0},{2,3},{3,2},{4,5},{5,4},{6,7},{7,6},{8,9},{9,8},{10,11... | collective-permute-start | bytes 1572872 | tf_op jit(solution)/shard_map/ppermute | solution.py:363
  67.7 2.7 %collective-permute-start.32 = (bf16[4,128,256]{2,1,0:T(8,128)(2,1)S(1)}, bf16[4,128,256]{2,1,0:T(8,128)(2,1)S(1)}, u32[]{:S(2)}, u32[]{:S(2)}) collective-permute-start(bf16[4,128,256]{2,1,0:T(8,128)(2,1)S(1)} %get-tuple-element.77), channel_id=1, source_target_pairs={{0,24},{8,16},{16,8},{24,0},{1,25},{9,17},{17,9},{25,1},{2,26},{10... | collective-permute-start | bytes 786440 | tf_op jit(solution)/shard_map/ppermute | solution.py:363
  70.6 1.9 %collective-permute-start.27 = (bf16[4,64,256]{2,1,0:T(8,128)(2,1)S(1)}, bf16[4,64,256]{2,1,0:T(8,128)(2,1)S(1)}, u32[]{:S(2)}, u32[]{:S(2)}) collective-permute-start(bf16[4,64,256]{2,1,0:T(8,128)(2,1)S(1)} %get-tuple-element.71), channel_id=1, source_target_pairs={{0,2},{1,3},{2,0},{3,1},{4,6},{5,7},{6,4},{7,5},{8,10},{9,11},{10,... | collective-permute-start | bytes 393224 | tf_op jit(solution)/shard_map/ppermute | solution.py:363
  72.7 4.3 %collective-permute-done.27.refs_1_ = bf16[4,64,256]{2,1,0:T(8,128)(2,1)S(1)} collective-permute-done((bf16[4,64,256]{2,1,0:T(8,128)(2,1)S(1)}, bf16[4,64,256]{2,1,0:T(8,128)(2,1)S(1)}, u32[]{:S(2)}, u32[]{:S(2)}) %collective-permute-start.27) | collective-permute-done | bytes 131104 | tf_op jit(solution)/shard_map/ppermute | solution.py:363
  77.0 3.8 %collective-permute-start.28 = (bf16[4,64,256]{2,1,0:T(8,128)(2,1)S(1)}, bf16[4,64,256]{2,1,0:T(8,128)(2,1)S(1)}, u32[]{:S(2)}, u32[]{:S(2)}) collective-permute-start(bf16[4,64,256]{2,1,0:T(8,128)(2,1)S(1)} %shard_map.99.refs_3_.refs_4_), channel_id=1, source_target_pairs={{0,4},{1,5},{2,6},{3,7},{4,0},{5,1},{6,2},{7,3},{8,12},{9,13},{10,... | collective-permute-start | bytes 393224 | tf_op jit(solution)/shard_map/ppermute | solution.py:363
  82.7 3.1 %collective-permute-done.28.refs_1_ = bf16[4,64,256]{2,1,0:T(8,128)(2,1)S(1)} collective-permute-done((bf16[4,64,256]{2,1,0:T(8,128)(2,1)S(1)}, bf16[4,64,256]{2,1,0:T(8,128)(2,1)S(1)}, u32[]{:S(2)}, u32[]{:S(2)}) %collective-permute-start.28) | collective-permute-done | bytes 131104 | tf_op jit(solution)/shard_map/ppermute | solution.py:363
  (68 shorter events, 19.9 us)
Async XLA Ops:
  2.6 11.1 %collective-permute-start.1 = (bf16[272,256]{1,0:T(8,128)(2,1)}, bf16[272,256]{1,0:T(8,128)(2,1)S(1)}, u32[]{:S(2)}, u32[]{:S(2)}) collective-permute-start(bf16[272,256]{1,0:T(8,128)(2,1)} %get-tuple-element.42.refs_0_), channel_id=1, source_target_pairs={{0,4},{1,5},{2,6},{3,7},{4,0},{5,1},{6,2},{7,3},{8,12},{9,13},{10,... | collective-permute-start | bytes 417800 | tf_op jit(solution)/shard_map/ppermute | solution.py:363
  6.7 10.3 %collective-permute-start.4 = (bf16[528,256]{1,0:T(8,128)(2,1)}, bf16[528,256]{1,0:T(8,128)(2,1)S(1)}, u32[]{:S(2)}, u32[]{:S(2)}) collective-permute-start(bf16[528,256]{1,0:T(8,128)(2,1)} %get-tuple-element.44.refs_12_), channel_id=1, source_target_pairs={{0,16},{8,24},{16,0},{24,8},{1,17},{9,25},{17,1},{25,9},{2,18},{10... | collective-permute-start | bytes 811016 | tf_op jit(solution)/shard_map/ppermute | solution.py:363
  8.2 8.8 %collective-permute-start.3 = (bf16[528,256]{1,0:T(8,128)(2,1)}, bf16[528,256]{1,0:T(8,128)(2,1)S(1)}, u32[]{:S(2)}, u32[]{:S(2)}) collective-permute-start(bf16[528,256]{1,0:T(8,128)(2,1)} %get-tuple-element.44.refs_12_), channel_id=1, source_target_pairs={{0,8},{8,0},{16,24},{24,16},{1,9},{9,1},{17,25},{25,17},{2,10},{10... | collective-permute-start | bytes 811016 | tf_op jit(solution)/shard_map/ppermute | solution.py:363
  9.7 7.3 %collective-permute-start = (bf16[272,256]{1,0:T(8,128)(2,1)}, bf16[272,256]{1,0:T(8,128)(2,1)S(1)}, u32[]{:S(2)}, u32[]{:S(2)}) collective-permute-start(bf16[272,256]{1,0:T(8,128)(2,1)} %get-tuple-element.42.refs_0_), channel_id=1, source_target_pairs={{0,2},{1,3},{2,0},{3,1},{4,6},{5,7},{6,4},{7,5},{8,10},{9,11},{10,... | collective-permute-start | bytes 417800 | tf_op jit(solution)/shard_map/ppermute | solution.py:363
  13.7 6.4 %collective-permute-start.2 = (bf16[1,272,256]{2,1,0:T(8,128)(2,1)S(1)}, bf16[1,272,256]{2,1,0:T(8,128)(2,1)S(1)}, u32[]{:S(2)}, u32[]{:S(2)}) collective-permute-start(bf16[1,272,256]{2,1,0:T(8,128)(2,1)S(1)} %shard_map.88.refs_2_), channel_id=1, source_target_pairs={{0,2},{1,3},{2,0},{3,1},{4,6},{5,7},{6,4},{7,5},{8,10},{9,11},{10,... | collective-permute-start | bytes 417800 | tf_op jit(solution)/shard_map/ppermute | solution.py:363
  14.5 9.4 %collective-permute-start.9 = (bf16[528,256]{1,0:T(8,128)(2,1)S(1)}, bf16[528,256]{1,0:T(8,128)(2,1)S(1)}, u32[]{:S(2)}, u32[]{:S(2)}) collective-permute-start(bf16[528,256]{1,0:T(8,128)(2,1)S(1)} %copy-done.2), channel_id=1, source_target_pairs={{0,24},{8,16},{16,8},{24,0},{1,25},{9,17},{17,9},{25,1},{2,26},{10... | collective-permute-start | bytes 811016 | tf_op jit(solution)/shard_map/ppermute | solution.py:363
  26.7 5.6 %collective-permute-start.10 = (bf16[4,4,64,256]{3,2,1,0:T(8,128)(2,1)S(1)}, bf16[4,4,64,256]{3,2,1,0:T(8,128)(2,1)S(1)}, u32[]{:S(2)}, u32[]{:S(2)}) collective-permute-start(bf16[4,4,64,256]{3,2,1,0:T(8,128)(2,1)S(1)} %get-tuple-element.50), channel_id=1, source_target_pairs={{0,1},{1,0},{2,3},{3,2},{4,5},{5,4},{6,7},{7,6},{8,9},{9,8},{10,11... | collective-permute-start | bytes 1572872 | tf_op jit(solution)/shard_map/ppermute | solution.py:363
  28.8 13.2 %collective-permute-start.14 = (bf16[4,128,256]{2,1,0:T(8,128)(2,1)S(1)}, bf16[4,128,256]{2,1,0:T(8,128)(2,1)S(1)}, u32[]{:S(2)}, u32[]{:S(2)}) collective-permute-start(bf16[4,128,256]{2,1,0:T(8,128)(2,1)S(1)} %get-tuple-element.56), channel_id=1, source_target_pairs={{0,8},{8,0},{16,24},{24,16},{1,9},{9,1},{17,25},{25,17},{2,10},{10... | collective-permute-start | bytes 786440 | tf_op jit(solution)/shard_map/ppermute | solution.py:363
  30.1 14.0 %collective-permute-start.15 = (bf16[4,128,256]{2,1,0:T(8,128)(2,1)S(1)}, bf16[4,128,256]{2,1,0:T(8,128)(2,1)S(1)}, u32[]{:S(2)}, u32[]{:S(2)}) collective-permute-start(bf16[4,128,256]{2,1,0:T(8,128)(2,1)S(1)} %get-tuple-element.57), channel_id=1, source_target_pairs={{0,16},{8,24},{16,0},{24,8},{1,17},{9,25},{17,1},{25,9},{2,18},{10... | collective-permute-start | bytes 786440 | tf_op jit(solution)/shard_map/ppermute | solution.py:363
  30.1 14.0 %collective-permute-start.16 = (bf16[4,128,256]{2,1,0:T(8,128)(2,1)S(1)}, bf16[4,128,256]{2,1,0:T(8,128)(2,1)S(1)}, u32[]{:S(2)}, u32[]{:S(2)}) collective-permute-start(bf16[4,128,256]{2,1,0:T(8,128)(2,1)S(1)} %get-tuple-element.58), channel_id=1, source_target_pairs={{0,24},{8,16},{16,8},{24,0},{1,25},{9,17},{17,9},{25,1},{2,26},{10... | collective-permute-start | bytes 786440 | tf_op jit(solution)/shard_map/ppermute | solution.py:363
  32.4 6.1 %collective-permute-start.11 = (bf16[4,64,256]{2,1,0:T(8,128)(2,1)S(1)}, bf16[4,64,256]{2,1,0:T(8,128)(2,1)S(1)}, u32[]{:S(2)}, u32[]{:S(2)}) collective-permute-start(bf16[4,64,256]{2,1,0:T(8,128)(2,1)S(1)} %get-tuple-element.53), channel_id=1, source_target_pairs={{0,2},{1,3},{2,0},{3,1},{4,6},{5,7},{6,4},{7,5},{8,10},{9,11},{10,... | collective-permute-start | bytes 393224 | tf_op jit(solution)/shard_map/ppermute | solution.py:363
  34.0 11.6 %collective-permute-start.13 = (bf16[4,64,256]{2,1,0:T(8,128)(2,1)S(1)}, bf16[4,64,256]{2,1,0:T(8,128)(2,1)S(1)}, u32[]{:S(2)}, u32[]{:S(2)}) collective-permute-start(bf16[4,64,256]{2,1,0:T(8,128)(2,1)S(1)} %get-tuple-element.54), channel_id=1, source_target_pairs={{0,2},{1,3},{2,0},{3,1},{4,6},{5,7},{6,4},{7,5},{8,10},{9,11},{10,... | collective-permute-start | bytes 393224 | tf_op jit(solution)/shard_map/ppermute | solution.py:363
  38.5 8.4 %collective-permute-start.12 = (bf16[4,64,256]{2,1,0:T(8,128)(2,1)S(1)}, bf16[4,64,256]{2,1,0:T(8,128)(2,1)S(1)}, u32[]{:S(2)}, u32[]{:S(2)}) collective-permute-start(bf16[4,64,256]{2,1,0:T(8,128)(2,1)S(1)} %shard_map.92.refs_4_), channel_id=1, source_target_pairs={{0,4},{1,5},{2,6},{3,7},{4,0},{5,1},{6,2},{7,3},{8,12},{9,13},{10,... | collective-permute-start | bytes 393224 | tf_op jit(solution)/shard_map/ppermute | solution.py:363
  44.3 10.2 %collective-permute-start.19 = (bf16[512,256]{1,0:T(8,128)(2,1)S(1)}, bf16[512,256]{1,0:T(8,128)(2,1)S(1)}, u32[]{:S(2)}, u32[]{:S(2)}) collective-permute-start(bf16[512,256]{1,0:T(8,128)(2,1)S(1)} %get-tuple-element.59.refs_3_.refs_10_), channel_id=1, source_target_pairs={{0,24},{8,16},{16,8},{24,0},{1,25},{9,17},{17,9},{25,1},{2,26},{10... | collective-permute-start | bytes 786440 | tf_op jit(solution)/shard_map/ppermute | solution.py:363
  47.1 7.4 %collective-permute-start.18 = (bf16[256,256]{1,0:T(8,128)(2,1)S(1)}, bf16[256,256]{1,0:T(8,128)(2,1)S(1)}, u32[]{:S(2)}, u32[]{:S(2)}) collective-permute-start(bf16[256,256]{1,0:T(8,128)(2,1)S(1)} %get-tuple-element.61.refs_0_), channel_id=1, source_target_pairs={{0,4},{1,5},{2,6},{3,7},{4,0},{5,1},{6,2},{7,3},{8,12},{9,13},{10,... | collective-permute-start | bytes 393224 | tf_op jit(solution)/shard_map/ppermute | solution.py:363
  48.1 8.5 %collective-permute-start.17 = (bf16[256,256]{1,0:T(8,128)(2,1)S(1)}, bf16[256,256]{1,0:T(8,128)(2,1)S(1)}, u32[]{:S(2)}, u32[]{:S(2)}) collective-permute-start(bf16[256,256]{1,0:T(8,128)(2,1)S(1)} %get-tuple-element.61.refs_0_), channel_id=1, source_target_pairs={{0,2},{1,3},{2,0},{3,1},{4,6},{5,7},{6,4},{7,5},{8,10},{9,11},{10,... | collective-permute-start | bytes 393224 | tf_op jit(solution)/shard_map/ppermute | solution.py:363
  54.7 6.4 %collective-permute-start.25 = (bf16[512,256]{1,0:T(8,128)(2,1)S(1)}, bf16[512,256]{1,0:T(8,128)(2,1)S(1)}, u32[]{:S(2)}, u32[]{:S(2)}) collective-permute-start(bf16[512,256]{1,0:T(8,128)(2,1)S(1)} %get-tuple-element.59.refs_3_.refs_10_), channel_id=1, source_target_pairs={{0,16},{8,24},{16,0},{24,8},{1,17},{9,25},{17,1},{25,9},{2,18},{10... | collective-permute-start | bytes 786440 | tf_op jit(solution)/shard_map/ppermute | solution.py:363
  56.0 6.5 %collective-permute-start.24 = (bf16[512,256]{1,0:T(8,128)(2,1)S(1)}, bf16[512,256]{1,0:T(8,128)(2,1)S(1)}, u32[]{:S(2)}, u32[]{:S(2)}) collective-permute-start(bf16[512,256]{1,0:T(8,128)(2,1)S(1)} %get-tuple-element.59.refs_3_.refs_10_), channel_id=1, source_target_pairs={{0,8},{8,0},{16,24},{24,16},{1,9},{9,1},{17,25},{25,17},{2,10},{10... | collective-permute-start | bytes 786440 | tf_op jit(solution)/shard_map/ppermute | solution.py:363
  67.0 13.9 %collective-permute-start.30 = (bf16[4,128,256]{2,1,0:T(8,128)(2,1)S(1)}, bf16[4,128,256]{2,1,0:T(8,128)(2,1)S(1)}, u32[]{:S(2)}, u32[]{:S(2)}) collective-permute-start(bf16[4,128,256]{2,1,0:T(8,128)(2,1)S(1)} %get-tuple-element.75), channel_id=1, source_target_pairs={{0,8},{8,0},{16,24},{24,16},{1,9},{9,1},{17,25},{25,17},{2,10},{10... | collective-permute-start | bytes 786440 | tf_op jit(solution)/shard_map/ppermute | solution.py:363
  67.7 14.0 %collective-permute-start.31 = (bf16[4,128,256]{2,1,0:T(8,128)(2,1)S(1)}, bf16[4,128,256]{2,1,0:T(8,128)(2,1)S(1)}, u32[]{:S(2)}, u32[]{:S(2)}) collective-permute-start(bf16[4,128,256]{2,1,0:T(8,128)(2,1)S(1)} %get-tuple-element.76), channel_id=1, source_target_pairs={{0,16},{8,24},{16,0},{24,8},{1,17},{9,25},{17,1},{25,9},{2,18},{10... | collective-permute-start | bytes 786440 | tf_op jit(solution)/shard_map/ppermute | solution.py:363
  67.7 14.0 %collective-permute-start.32 = (bf16[4,128,256]{2,1,0:T(8,128)(2,1)S(1)}, bf16[4,128,256]{2,1,0:T(8,128)(2,1)S(1)}, u32[]{:S(2)}, u32[]{:S(2)}) collective-permute-start(bf16[4,128,256]{2,1,0:T(8,128)(2,1)S(1)} %get-tuple-element.77), channel_id=1, source_target_pairs={{0,24},{8,16},{16,8},{24,0},{1,25},{9,17},{17,9},{25,1},{2,26},{10... | collective-permute-start | bytes 786440 | tf_op jit(solution)/shard_map/ppermute | solution.py:363
  70.6 6.4 %collective-permute-start.27 = (bf16[4,64,256]{2,1,0:T(8,128)(2,1)S(1)}, bf16[4,64,256]{2,1,0:T(8,128)(2,1)S(1)}, u32[]{:S(2)}, u32[]{:S(2)}) collective-permute-start(bf16[4,64,256]{2,1,0:T(8,128)(2,1)S(1)} %get-tuple-element.71), channel_id=1, source_target_pairs={{0,2},{1,3},{2,0},{3,1},{4,6},{5,7},{6,4},{7,5},{8,10},{9,11},{10,... | collective-permute-start | bytes 393224 | tf_op jit(solution)/shard_map/ppermute | solution.py:363
  72.5 10.3 %collective-permute-start.29 = (bf16[4,64,256]{2,1,0:T(8,128)(2,1)S(1)}, bf16[4,64,256]{2,1,0:T(8,128)(2,1)S(1)}, u32[]{:S(2)}, u32[]{:S(2)}) collective-permute-start(bf16[4,64,256]{2,1,0:T(8,128)(2,1)S(1)} %get-tuple-element.72), channel_id=1, source_target_pairs={{0,2},{1,3},{2,0},{3,1},{4,6},{5,7},{6,4},{7,5},{8,10},{9,11},{10,... | collective-permute-start | bytes 393224 | tf_op jit(solution)/shard_map/ppermute | solution.py:363
  77.0 8.7 %collective-permute-start.28 = (bf16[4,64,256]{2,1,0:T(8,128)(2,1)S(1)}, bf16[4,64,256]{2,1,0:T(8,128)(2,1)S(1)}, u32[]{:S(2)}, u32[]{:S(2)}) collective-permute-start(bf16[4,64,256]{2,1,0:T(8,128)(2,1)S(1)} %shard_map.99.refs_3_.refs_4_), channel_id=1, source_target_pairs={{0,4},{1,5},{2,6},{3,7},{4,0},{5,1},{6,2},{7,3},{8,12},{9,13},{10,... | collective-permute-start | bytes 393224 | tf_op jit(solution)/shard_map/ppermute | solution.py:363
  (14 other events, 128.3 us)

commit v4 on v3

--- a/solution.py
+++ b/solution.py
@@ -297,43 +297,51 @@
     return res[0], res[1], res[2 : 2 + n_col], res[2 + n_col :]
 
 
-def merge_kernel(kept, keep, got, *outs):
-    for n, out in enumerate(outs):
-        out[...] = (keep[n] + got[n].astype(f32)).astype(out.dtype)
-
-
-def merge(keep, got, kept):
+def merge_kernel(n_held, keep, got, *refs):
+    held, outs = refs[:n_held], refs[n_held:]
+    for n in range(keep.shape[0]):
+        outs[n][...] = (keep[n] + got[n].astype(f32)).astype(outs[n].dtype)
+    for src, out in zip(held, outs[keep.shape[0] :]):
+        out[...] = src[...]
+
+
+def merge(keep, got, kept, held):
     n, *piece = keep.shape
+    outs = [shape(tuple(piece), f32 if k in kept else bf16) for k in range(n)]
+    outs += [shape(x.shape, x.dtype) for x in held]
     return pl.pallas_call(
-        functools.partial(merge_kernel, kept),
-        out_shape=[shape(tuple(piece), f32 if k in kept else bf16) for k in range(n)],
-        in_specs=[VMEM] * 2,
-        out_specs=[VMEM] * n,
+        functools.partial(merge_kernel, len(held)),
+        out_shape=outs,
+        in_specs=[VMEM] * (2 + len(held)),
+        out_specs=[VMEM] * len(outs),
         compiler_params=pltpu.CompilerParams(vmem_limit_bytes=SMALL),
         cost_estimate=cost(0, 2 << 20),
-    )(keep, got)
-
-
-def add_kernel(*refs):
-    total = refs[0][...]
-    for ref in refs[1:-1]:
-        total += ref[...].astype(f32)
-    refs[-1][...] = total.astype(bf16)
-
-
-def add(own, parts):
+    )(keep, got, *held)
+
+
+def add_kernel(n_parts, n_held, own, *refs):
+    parts, held, outs = refs[:n_parts], refs[n_parts : n_parts + n_held], refs[n_parts + n_held :]
+    total = own[...]
+    for part in parts:
+        total += part[...].astype(f32)
+    outs[0][...] = total.astype(bf16)
+    for src, out in zip(held, outs[1:]):
+        out[...] = src[...]
+
+
+def add(own, parts, held):
     return pl.pallas_call(
-        add_kernel,
-        out_shape=shape(own.shape, bf16),
-        in_specs=[VMEM] * (1 + len(parts)),
-        out_specs=VMEM,
+        functools.partial(add_kernel, len(parts), len(held)),
+        out_shape=[shape(own.shape, bf16)] + [shape(x.shape, x.dtype) for x in held],
+        in_specs=[VMEM] * (1 + len(parts) + len(held)),
+        out_specs=[VMEM] * (1 + len(held)),
         compiler_params=pltpu.CompilerParams(vmem_limit_bytes=SMALL),
         cost_estimate=cost(0, 1 << 20),
-    )(own, *parts)
-
-
-def update_kernel(n_parts, emb, *refs):
-    parts, outs = refs[:n_parts], refs[n_parts + 1 :]
+    )(own, *parts, *held)
+
+
+def update_kernel(n_parts, n_outs, emb, *refs):
+    parts, outs = refs[:n_parts], refs[-n_outs:]
     total = parts[0][...].astype(f32)
     for part in parts[1:]:
         total += part[...].astype(f32)
@@ -343,19 +351,19 @@
         outs[1][...] = new.astype(bf16).reshape(outs[1].shape)
 
 
-def update(emb, parts, after, last):
+def update(emb, parts, afters, last):
     blocks, part, width = emb.shape
     outs = [shape(emb.shape, f32)]
     if not last:
         outs.append(shape((blocks * part, width), bf16))
     res = pl.pallas_call(
-        functools.partial(update_kernel, len(parts)),
+        functools.partial(update_kernel, len(parts), len(outs)),
         out_shape=outs,
-        in_specs=[VMEM] * (1 + len(parts)) + [ANY],
+        in_specs=[VMEM] * (1 + len(parts)) + [ANY] * len(afters),
         out_specs=[VMEM] * len(outs),
         compiler_params=pltpu.CompilerParams(vmem_limit_bytes=SMALL),
         cost_estimate=cost(0, 1 << 20),
-    )(emb, *parts, after)
+    )(emb, *parts, *afters)
     return res if not last else (res[0], None)
 
 
@@ -395,12 +403,15 @@
             listing, used, tabs, row_in, col_in, tables, row_owner, col_owner, dims
         )
         tables = tables or made
-        merged = merge(keep, send(swap, "col", n_col_dev, 1), (0, far))
-        crossing = add(merged[far], [hop(merged[far + k], k) for k in near])
+        held = col_out[-1:] if substep == 1 else []
+        merged = merge(keep, send(swap, "col", n_col_dev, 1), (0, far), held)
+        col_out = [*col_out[: len(col_out) - len(held)], *merged[half:]]
+        relays = [hop(merged[far + k], k) for k in near]
+        crossing, *straight = add(merged[far], relays, [merged[k] for k in near])
         col_parts = [col_out[0]] + [send(col_out[k], "row", n_row_dev, k) for k in col_owner[1:]]
-        row_parts = [merged[0], hop(crossing, far)] + [hop(merged[k], k) for k in near]
-        col_emb, col_pay = update(col_emb, col_parts, crossing, substep == 1)
-        row_emb, row_pay = update(row_emb, row_parts, col_pay if substep == 0 else crossing, substep == 1)
+        row_parts = [merged[0]] + [hop(x, k) for x, k in zip(straight, near)] + [hop(crossing, far)]
+        col_emb, col_pay = update(col_emb, col_parts, [straight[0]], substep == 1)
+        row_emb, row_pay = update(row_emb, row_parts, [col_pay if substep == 0 else straight[0]], substep == 1)
     return (row_emb, col_emb)
 
 

time: 86.6 us -> 86.2 us (level)
  starting transfers between devices: 43.3 us -> 38.4 us
  waiting for transfers between devices: 30.6 us -> 33.6 us
  Pallas kernels: 11.1 us -> 12.8 us
    ppermute x33, starting transfers between devices: 43.3 us -> 38.4 us  [send(): return lax.ppermute(x, axis, [(k, k ^ mask) for k in range(count)])]
    ppermute x33, waiting for transfers between devices: 30.6 us -> 33.6 us  [send(): return lax.ppermute(x, axis, [(k, k ^ mask) for k in range(count)])]
    pallas_call x2, Pallas kernels: 5.17 us -> 6.42 us  [work(): pl.pallas_call(functools.partial(work_kernel, first, len(row_in), n_row,...]
  transfers between devices with their start and end apart: 33 -> 33, of which waited for: 12 -> 14; matrix products, arithmetic and copies ran while one was open for 0% -> 0% of each run, Pallas kernels for 4% -> 4%
where the time goes in v4:
time: 86.2 us; the launch traced here: 86.3 us
  starting transfers between devices  38.4 us (45%)
  waiting for transfers between devices  33.6 us (39%)
  Pallas kernels  12.8 us (15%)
  between operations  1.5 us (2%)
    ppermute x33, starting transfers between devices, send(): return lax.ppermute(x, axis, [(k, k ^ mask) for k in range(count)])  38.4 us
    ppermute x33, waiting for transfers between devices, send(): return lax.ppermute(x, axis, [(k, k ^ mask) for k in range(count)])  33.6 us
    pallas_call x2, Pallas kernels, work(): pl.pallas_call(functools.partial(work_kernel, first, len(row_in), n_row,...  6.42 us
    pallas_call x1, Pallas kernels, levels(): pl.pallas_call(levels_kernel, out_shape=[shape(tiles.shape, f32), shape(t...  2.12 us
    pallas_call x4, Pallas kernels, update(): pl.pallas_call(functools.partial(update_kernel, len(parts), len(outs)), o...  1.98 us
    pallas_call x1, Pallas kernels, pack(): pl.pallas_call(pack_kernel, out_shape=[shape((e.shape[0] * e.shape[1] + M...  1.93 us
  transfers between devices with their start and end apart: 33, of which 14 were waited for; matrix products, arithmetic and copies ran while one was open for 0% of the time, Pallas kernels for 4%

profile of v4, /device:TPU:0, one launch (start us, length us, event | category | flops | bytes accessed | tf_op | source)
XLA Modules:
  0.0 86.3 jit_solution(16190200764801733990)
XLA Ops:
  0.6 1.9 %shard_map.87 = (bf16[272,256]{1,0:T(8,128)(2,1)}, bf16[528,256]{1,0:T(8,128)(2,1)}) custom-call(f32[4,64,256]{2,1,0:T(8,128)} %emb.3, bf16[4,64]{1,0:T(4,128)(2,1)} %row_marg.1, f32[4,128,256]{2,1,0:T(8,128)} %emb.2, bf16[4,128]{1,0:T(4,128)(2,1)} %col_marg.1), custom_call_target="tpu_custom_call" | custom-call | bytes 1048576 | tf_op jit(solution)/shard_map/pallas_call | solution.py:50
  2.6 4.1 %collective-permute-start.1 = (bf16[272,256]{1,0:T(8,128)(2,1)}, bf16[272,256]{1,0:T(8,128)(2,1)S(1)}, u32[]{:S(2)}, u32[]{:S(2)}) collective-permute-start(bf16[272,256]{1,0:T(8,128)(2,1)} %get-tuple-element.47.refs_0_), channel_id=1, source_target_pairs={{0,4},{1,5},{2,6},{3,7},{4,0},{5,1},{6,2},{7,3},{8,12},{9,13},{10,... | collective-permute-start | bytes 417800 | tf_op jit(solution)/shard_map/ppermute | solution.py:371
  11.9 2.1 %shard_map.86 = (f32[8,512,512]{2,1,0:T(8,128)S(1)}, bf16[8,512,512]{2,1,0:T(8,128)(2,1)S(1)}, f32[8,128]{1,0:T(8,128)S(1)}) custom-call(s32[1]{0:T(128)} %bitcast.5.used, s32[8,512,512]{2,1,0:T(8,128)} %bitcast.10), custom_call_target="tpu_custom_call" | custom-call | bytes 12582912 | tf_op jit(solution)/shard_map/pallas_call | solution.py:99
  15.0 1.9 %collective-permute-start.9 = (bf16[528,256]{1,0:T(8,128)(2,1)S(1)}, bf16[528,256]{1,0:T(8,128)(2,1)S(1)}, u32[]{:S(2)}, u32[]{:S(2)}) collective-permute-start(bf16[528,256]{1,0:T(8,128)(2,1)S(1)} %copy-done.2), channel_id=1, source_target_pairs={{0,24},{8,16},{16,8},{24,0},{1,25},{9,17},{17,9},{25,1},{2,26},{10... | collective-permute-start | bytes 811016 | tf_op jit(solution)/shard_map/ppermute | solution.py:371
  17.0 3.6 %collective-permute-done.2.refs_3_ = bf16[1,272,256]{2,1,0:T(8,128)(2,1)S(1)} collective-permute-done((bf16[1,272,256]{2,1,0:T(8,128)(2,1)S(1)}, bf16[1,272,256]{2,1,0:T(8,128)(2,1)S(1)}, u32[]{:S(2)}, u32[]{:S(2)}) %collective-permute-start.2) | collective-permute-done | bytes 139296 | tf_op jit(solution)/shard_map/ppermute | solution.py:371
  21.7 2.7 %collective-permute-done.9.refs_15_ = bf16[528,256]{1,0:T(8,128)(2,1)S(1)} collective-permute-done((bf16[528,256]{1,0:T(8,128)(2,1)S(1)}, bf16[528,256]{1,0:T(8,128)(2,1)S(1)}, u32[]{:S(2)}, u32[]{:S(2)}) %collective-permute-start.9) | collective-permute-done | bytes 270368 | tf_op jit(solution)/shard_map/ppermute | solution.py:371
  24.4 3.3 %shard_map.90 = (f32[4,4,64,256]{3,2,1,0:T(8,128)S(1)}, bf16[4,4,64,256]{3,2,1,0:T(8,128)(2,1)S(1)}, bf16[4,128,256]{2,1,0:T(8,128)(2,1)S(1)}, bf16[4,128,256]{2...) custom-call(s32[2,8]{1,0:T(2,128)S(1)} %bitcast.8, ...), custom_call_target="tpu_custom_call" | custom-call | flops 3221225472 | bytes 16777216 | tf_op jit(solution)/shard_map/pallas_call | solution.py:279
  27.8 1.8 %collective-permute-start.10 = (bf16[4,4,64,256]{3,2,1,0:T(8,128)(2,1)S(1)}, bf16[4,4,64,256]{3,2,1,0:T(8,128)(2,1)S(1)}, u32[]{:S(2)}, u32[]{:S(2)}) collective-permute-start(bf16[4,4,64,256]{3,2,1,0:T(8,128)(2,1)S(1)} %get-tuple-element.55), channel_id=1, source_target_pairs={{0,1},{1,0},{2,3},{3,2},{4,5},{5,4},{6,7},{7,6},{8,9},{9,8},{10,11... | collective-permute-start | bytes 1572872 | tf_op jit(solution)/shard_map/ppermute | solution.py:371
  29.6 2.3 %collective-permute-start.15 = (bf16[4,128,256]{2,1,0:T(8,128)(2,1)S(1)}, bf16[4,128,256]{2,1,0:T(8,128)(2,1)S(1)}, u32[]{:S(2)}, u32[]{:S(2)}) collective-permute-start(bf16[4,128,256]{2,1,0:T(8,128)(2,1)S(1)} %get-tuple-element.64), channel_id=1, source_target_pairs={{0,16},{8,24},{16,0},{24,8},{1,17},{9,25},{17,1},{25,9},{2,18},{10... | collective-permute-start | bytes 786440 | tf_op jit(solution)/shard_map/ppermute | solution.py:371
  34.4 4.3 %collective-permute-done.11.refs_0_ = bf16[4,64,256]{2,1,0:T(8,128)(2,1)S(1)} collective-permute-done((bf16[4,64,256]{2,1,0:T(8,128)(2,1)S(1)}, bf16[4,64,256]{2,1,0:T(8,128)(2,1)S(1)}, u32[]{:S(2)}, u32[]{:S(2)}) %collective-permute-start.11) | collective-permute-done | bytes 131104 | tf_op jit(solution)/shard_map/ppermute | solution.py:371
  38.7 2.3 %collective-permute-start.13 = (bf16[4,64,256]{2,1,0:T(8,128)(2,1)S(1)}, bf16[4,64,256]{2,1,0:T(8,128)(2,1)S(1)}, u32[]{:S(2)}, u32[]{:S(2)}) collective-permute-start(bf16[4,64,256]{2,1,0:T(8,128)(2,1)S(1)} %get-tuple-element.61), channel_id=1, source_target_pairs={{0,4},{1,5},{2,6},{3,7},{4,0},{5,1},{6,2},{7,3},{8,12},{9,13},{10,... | collective-permute-start | bytes 393224 | tf_op jit(solution)/shard_map/ppermute | solution.py:371
  41.8 1.8 %collective-permute-done.15.refs_2_ = bf16[4,128,256]{2,1,0:T(8,128)(2,1)S(1)} collective-permute-done((bf16[4,128,256]{2,1,0:T(8,128)(2,1)S(1)}, bf16[4,128,256]{2,1,0:T(8,128)(2,1)S(1)}, u32[]{:S(2)}, u32[]{:S(2)}) %collective-permute-start.15) | collective-permute-done | bytes 262176 | tf_op jit(solution)/shard_map/ppermute | solution.py:371
  43.6 1.9 %collective-permute-done.16.refs_3_ = bf16[4,128,256]{2,1,0:T(8,128)(2,1)S(1)} collective-permute-done((bf16[4,128,256]{2,1,0:T(8,128)(2,1)S(1)}, bf16[4,128,256]{2,1,0:T(8,128)(2,1)S(1)}, u32[]{:S(2)}, u32[]{:S(2)}) %collective-permute-start.16) | collective-permute-done | bytes 262176 | tf_op jit(solution)/shard_map/ppermute | solution.py:371
  45.7 1.8 %collective-permute-start.19 = (bf16[512,256]{1,0:T(8,128)(2,1)S(1)}, bf16[512,256]{1,0:T(8,128)(2,1)S(1)}, u32[]{:S(2)}, u32[]{:S(2)}) collective-permute-start(bf16[512,256]{1,0:T(8,128)(2,1)S(1)} %get-tuple-element.66.refs_3_.refs_10_), channel_id=1, source_target_pairs={{0,24},{8,16},{16,8},{24,0},{1,25},{9,17},{17,9},{25,1},{2,26},{10... | collective-permute-start | bytes 786440 | tf_op jit(solution)/shard_map/ppermute | solution.py:371
  48.0 1.9 %collective-permute-start.18 = (bf16[256,256]{1,0:T(8,128)(2,1)S(1)}, bf16[256,256]{1,0:T(8,128)(2,1)S(1)}, u32[]{:S(2)}, u32[]{:S(2)}) collective-permute-start(bf16[256,256]{1,0:T(8,128)(2,1)S(1)} %get-tuple-element.68.refs_0_), channel_id=1, source_target_pairs={{0,4},{1,5},{2,6},{3,7},{4,0},{5,1},{6,2},{7,3},{8,12},{9,13},{10,... | collective-permute-start | bytes 393224 | tf_op jit(solution)/shard_map/ppermute | solution.py:371
  50.7 5.0 %collective-permute-done.18.refs_0_ = bf16[256,256]{1,0:T(8,128)(2,1)S(1)} collective-permute-done((bf16[256,256]{1,0:T(8,128)(2,1)S(1)}, bf16[256,256]{1,0:T(8,128)(2,1)S(1)}, u32[]{:S(2)}, u32[]{:S(2)}) %collective-permute-start.18) | collective-permute-done | bytes 131104 | tf_op jit(solution)/shard_map/ppermute | solution.py:371
  58.0 2.8 %collective-permute-done.20.refs_3_ = bf16[1,256,256]{2,1,0:T(8,128)(2,1)S(1)} collective-permute-done((bf16[1,256,256]{2,1,0:T(8,128)(2,1)S(1)}, bf16[1,256,256]{2,1,0:T(8,128)(2,1)S(1)}, u32[]{:S(2)}, u32[]{:S(2)}) %collective-permute-start.20) | collective-permute-done | bytes 131104 | tf_op jit(solution)/shard_map/ppermute | solution.py:371
  63.3 3.1 %shard_map.97 = (f32[4,4,64,256]{3,2,1,0:T(8,128)S(1)}, bf16[4,4,64,256]{3,2,1,0:T(8,128)(2,1)S(1)}, bf16[4,128,256]{2,1,0:T(8,128)(2,1)S(1)}, bf16[4,128,256]{2...) custom-call(s32[2,8]{1,0:T(2,128)S(1)} %bitcast.9, s32[1]{0:T(128)} %bitcast.7.refs_1_, ...), custom_call_target="tpu_custom_call" | custom-call | flops 3221225472 | bytes 16777216 | tf_op jit(solution)/shard_map/pallas_call | solution.py:279
  66.4 2.2 %collective-permute-start.26 = (bf16[4,4,64,256]{3,2,1,0:T(8,128)(2,1)S(1)}, bf16[4,4,64,256]{3,2,1,0:T(8,128)(2,1)S(1)}, u32[]{:S(2)}, u32[]{:S(2)}) collective-permute-start(bf16[4,4,64,256]{3,2,1,0:T(8,128)(2,1)S(1)} %get-tuple-element.75), channel_id=1, source_target_pairs={{0,1},{1,0},{2,3},{3,2},{4,5},{5,4},{6,7},{7,6},{8,9},{9,8},{10,11... | collective-permute-start | bytes 1572872 | tf_op jit(solution)/shard_map/ppermute | solution.py:371
  68.7 2.1 %collective-permute-start.31 = (bf16[4,128,256]{2,1,0:T(8,128)(2,1)S(1)}, bf16[4,128,256]{2,1,0:T(8,128)(2,1)S(1)}, u32[]{:S(2)}, u32[]{:S(2)}) collective-permute-start(bf16[4,128,256]{2,1,0:T(8,128)(2,1)S(1)} %get-tuple-element.86), channel_id=1, source_target_pairs={{0,16},{8,24},{16,0},{24,8},{1,17},{9,25},{17,1},{25,9},{2,18},{10... | collective-permute-start | bytes 786440 | tf_op jit(solution)/shard_map/ppermute | solution.py:371
  72.6 3.8 %collective-permute-done.27.refs_0_ = bf16[4,64,256]{2,1,0:T(8,128)(2,1)S(1)} collective-permute-done((bf16[4,64,256]{2,1,0:T(8,128)(2,1)S(1)}, bf16[4,64,256]{2,1,0:T(8,128)(2,1)S(1)}, u32[]{:S(2)}, u32[]{:S(2)}) %collective-permute-start.27) | collective-permute-done | bytes 131104 | tf_op jit(solution)/shard_map/ppermute | solution.py:371
  76.5 2.1 %collective-permute-start.29 = (bf16[4,64,256]{2,1,0:T(8,128)(2,1)S(1)}, bf16[4,64,256]{2,1,0:T(8,128)(2,1)S(1)}, u32[]{:S(2)}, u32[]{:S(2)}) collective-permute-start(bf16[4,64,256]{2,1,0:T(8,128)(2,1)S(1)} %get-tuple-element.82), channel_id=1, source_target_pairs={{0,4},{1,5},{2,6},{3,7},{4,0},{5,1},{6,2},{7,3},{8,12},{9,13},{10,... | collective-permute-start | bytes 393224 | tf_op jit(solution)/shard_map/ppermute | solution.py:371
  79.2 3.3 %collective-permute-done.31.refs_2_ = bf16[4,128,256]{2,1,0:T(8,128)(2,1)S(1)} collective-permute-done((bf16[4,128,256]{2,1,0:T(8,128)(2,1)S(1)}, bf16[4,128,256]{2,1,0:T(8,128)(2,1)S(1)}, u32[]{:S(2)}, u32[]{:S(2)}) %collective-permute-start.31) | collective-permute-done | bytes 262176 | tf_op jit(solution)/shard_map/ppermute | solution.py:371
  82.5 1.9 %collective-permute-done.32.refs_3_ = bf16[4,128,256]{2,1,0:T(8,128)(2,1)S(1)} collective-permute-done((bf16[4,128,256]{2,1,0:T(8,128)(2,1)S(1)}, bf16[4,128,256]{2,1,0:T(8,128)(2,1)S(1)}, u32[]{:S(2)}, u32[]{:S(2)}) %collective-permute-start.32) | collective-permute-done | bytes 262176 | tf_op jit(solution)/shard_map/ppermute | solution.py:371
  (68 shorter events, 20.8 us)
Async XLA Ops:
  2.6 11.5 %collective-permute-start.1 = (bf16[272,256]{1,0:T(8,128)(2,1)}, bf16[272,256]{1,0:T(8,128)(2,1)S(1)}, u32[]{:S(2)}, u32[]{:S(2)}) collective-permute-start(bf16[272,256]{1,0:T(8,128)(2,1)} %get-tuple-element.47.refs_0_), channel_id=1, source_target_pairs={{0,4},{1,5},{2,6},{3,7},{4,0},{5,1},{6,2},{7,3},{8,12},{9,13},{10,... | collective-permute-start | bytes 417800 | tf_op jit(solution)/shard_map/ppermute | solution.py:371
  6.7 10.3 %collective-permute-start.4 = (bf16[528,256]{1,0:T(8,128)(2,1)}, bf16[528,256]{1,0:T(8,128)(2,1)S(1)}, u32[]{:S(2)}, u32[]{:S(2)}) collective-permute-start(bf16[528,256]{1,0:T(8,128)(2,1)} %get-tuple-element.49.refs_12_), channel_id=1, source_target_pairs={{0,16},{8,24},{16,0},{24,8},{1,17},{9,25},{17,1},{25,9},{2,18},{10... | collective-permute-start | bytes 811016 | tf_op jit(solution)/shard_map/ppermute | solution.py:371
  8.2 8.8 %collective-permute-start.3 = (bf16[528,256]{1,0:T(8,128)(2,1)}, bf16[528,256]{1,0:T(8,128)(2,1)S(1)}, u32[]{:S(2)}, u32[]{:S(2)}) collective-permute-start(bf16[528,256]{1,0:T(8,128)(2,1)} %get-tuple-element.49.refs_12_), channel_id=1, source_target_pairs={{0,8},{8,0},{16,24},{24,16},{1,9},{9,1},{17,25},{25,17},{2,10},{10... | collective-permute-start | bytes 811016 | tf_op jit(solution)/shard_map/ppermute | solution.py:371
  9.7 7.3 %collective-permute-start = (bf16[272,256]{1,0:T(8,128)(2,1)}, bf16[272,256]{1,0:T(8,128)(2,1)S(1)}, u32[]{:S(2)}, u32[]{:S(2)}) collective-permute-start(bf16[272,256]{1,0:T(8,128)(2,1)} %get-tuple-element.47.refs_0_), channel_id=1, source_target_pairs={{0,2},{1,3},{2,0},{3,1},{4,6},{5,7},{6,4},{7,5},{8,10},{9,11},{10,... | collective-permute-start | bytes 417800 | tf_op jit(solution)/shard_map/ppermute | solution.py:371
  14.1 6.4 %collective-permute-start.2 = (bf16[1,272,256]{2,1,0:T(8,128)(2,1)S(1)}, bf16[1,272,256]{2,1,0:T(8,128)(2,1)S(1)}, u32[]{:S(2)}, u32[]{:S(2)}) collective-permute-start(bf16[1,272,256]{2,1,0:T(8,128)(2,1)S(1)} %shard_map.88.refs_2_), channel_id=1, source_target_pairs={{0,2},{1,3},{2,0},{3,1},{4,6},{5,7},{6,4},{7,5},{8,10},{9,11},{10,... | collective-permute-start | bytes 417800 | tf_op jit(solution)/shard_map/ppermute | solution.py:371
  15.0 9.3 %collective-permute-start.9 = (bf16[528,256]{1,0:T(8,128)(2,1)S(1)}, bf16[528,256]{1,0:T(8,128)(2,1)S(1)}, u32[]{:S(2)}, u32[]{:S(2)}) collective-permute-start(bf16[528,256]{1,0:T(8,128)(2,1)S(1)} %copy-done.2), channel_id=1, source_target_pairs={{0,24},{8,16},{16,8},{24,0},{1,25},{9,17},{17,9},{25,1},{2,26},{10... | collective-permute-start | bytes 811016 | tf_op jit(solution)/shard_map/ppermute | solution.py:371
  27.8 5.5 %collective-permute-start.10 = (bf16[4,4,64,256]{3,2,1,0:T(8,128)(2,1)S(1)}, bf16[4,4,64,256]{3,2,1,0:T(8,128)(2,1)S(1)}, u32[]{:S(2)}, u32[]{:S(2)}) collective-permute-start(bf16[4,4,64,256]{3,2,1,0:T(8,128)(2,1)S(1)} %get-tuple-element.55), channel_id=1, source_target_pairs={{0,1},{1,0},{2,3},{3,2},{4,5},{5,4},{6,7},{7,6},{8,9},{9,8},{10,11... | collective-permute-start | bytes 1572872 | tf_op jit(solution)/shard_map/ppermute | solution.py:371
  29.6 12.3 %collective-permute-start.14 = (bf16[4,128,256]{2,1,0:T(8,128)(2,1)S(1)}, bf16[4,128,256]{2,1,0:T(8,128)(2,1)S(1)}, u32[]{:S(2)}, u32[]{:S(2)}) collective-permute-start(bf16[4,128,256]{2,1,0:T(8,128)(2,1)S(1)} %get-tuple-element.63), channel_id=1, source_target_pairs={{0,8},{8,0},{16,24},{24,16},{1,9},{9,1},{17,25},{25,17},{2,10},{10... | collective-permute-start | bytes 786440 | tf_op jit(solution)/shard_map/ppermute | solution.py:371
  29.6 14.0 %collective-permute-start.15 = (bf16[4,128,256]{2,1,0:T(8,128)(2,1)S(1)}, bf16[4,128,256]{2,1,0:T(8,128)(2,1)S(1)}, u32[]{:S(2)}, u32[]{:S(2)}) collective-permute-start(bf16[4,128,256]{2,1,0:T(8,128)(2,1)S(1)} %get-tuple-element.64), channel_id=1, source_target_pairs={{0,16},{8,24},{16,0},{24,8},{1,17},{9,25},{17,1},{25,9},{2,18},{10... | collective-permute-start | bytes 786440 | tf_op jit(solution)/shard_map/ppermute | solution.py:371
  31.9 13.6 %collective-permute-start.16 = (bf16[4,128,256]{2,1,0:T(8,128)(2,1)S(1)}, bf16[4,128,256]{2,1,0:T(8,128)(2,1)S(1)}, u32[]{:S(2)}, u32[]{:S(2)}) collective-permute-start(bf16[4,128,256]{2,1,0:T(8,128)(2,1)S(1)} %get-tuple-element.65), channel_id=1, source_target_pairs={{0,24},{8,16},{16,8},{24,0},{1,25},{9,17},{17,9},{25,1},{2,26},{10... | collective-permute-start | bytes 786440 | tf_op jit(solution)/shard_map/ppermute | solution.py:371
  33.4 5.4 %collective-permute-start.11 = (bf16[4,64,256]{2,1,0:T(8,128)(2,1)S(1)}, bf16[4,64,256]{2,1,0:T(8,128)(2,1)S(1)}, u32[]{:S(2)}, u32[]{:S(2)}) collective-permute-start(bf16[4,64,256]{2,1,0:T(8,128)(2,1)S(1)} %get-tuple-element.58), channel_id=1, source_target_pairs={{0,2},{1,3},{2,0},{3,1},{4,6},{5,7},{6,4},{7,5},{8,10},{9,11},{10,... | collective-permute-start | bytes 393224 | tf_op jit(solution)/shard_map/ppermute | solution.py:371
  38.7 8.8 %collective-permute-start.13 = (bf16[4,64,256]{2,1,0:T(8,128)(2,1)S(1)}, bf16[4,64,256]{2,1,0:T(8,128)(2,1)S(1)}, u32[]{:S(2)}, u32[]{:S(2)}) collective-permute-start(bf16[4,64,256]{2,1,0:T(8,128)(2,1)S(1)} %get-tuple-element.61), channel_id=1, source_target_pairs={{0,4},{1,5},{2,6},{3,7},{4,0},{5,1},{6,2},{7,3},{8,12},{9,13},{10,... | collective-permute-start | bytes 393224 | tf_op jit(solution)/shard_map/ppermute | solution.py:371
  41.0 6.9 %collective-permute-start.12 = (bf16[4,64,256]{2,1,0:T(8,128)(2,1)S(1)}, bf16[4,64,256]{2,1,0:T(8,128)(2,1)S(1)}, u32[]{:S(2)}, u32[]{:S(2)}) collective-permute-start(bf16[4,64,256]{2,1,0:T(8,128)(2,1)S(1)} %get-tuple-element.60.refs_4_), channel_id=1, source_target_pairs={{0,2},{1,3},{2,0},{3,1},{4,6},{5,7},{6,4},{7,5},{8,10},{9,11},{10,... | collective-permute-start | bytes 393224 | tf_op jit(solution)/shard_map/ppermute | solution.py:371
  45.7 10.0 %collective-permute-start.19 = (bf16[512,256]{1,0:T(8,128)(2,1)S(1)}, bf16[512,256]{1,0:T(8,128)(2,1)S(1)}, u32[]{:S(2)}, u32[]{:S(2)}) collective-permute-start(bf16[512,256]{1,0:T(8,128)(2,1)S(1)} %get-tuple-element.66.refs_3_.refs_10_), channel_id=1, source_target_pairs={{0,24},{8,16},{16,8},{24,0},{1,25},{9,17},{17,9},{25,1},{2,26},{10... | collective-permute-start | bytes 786440 | tf_op jit(solution)/shard_map/ppermute | solution.py:371
  48.0 7.7 %collective-permute-start.18 = (bf16[256,256]{1,0:T(8,128)(2,1)S(1)}, bf16[256,256]{1,0:T(8,128)(2,1)S(1)}, u32[]{:S(2)}, u32[]{:S(2)}) collective-permute-start(bf16[256,256]{1,0:T(8,128)(2,1)S(1)} %get-tuple-element.68.refs_0_), channel_id=1, source_target_pairs={{0,4},{1,5},{2,6},{3,7},{4,0},{5,1},{6,2},{7,3},{8,12},{9,13},{10,... | collective-permute-start | bytes 393224 | tf_op jit(solution)/shard_map/ppermute | solution.py:371
  49.9 8.1 %collective-permute-start.17 = (bf16[256,256]{1,0:T(8,128)(2,1)S(1)}, bf16[256,256]{1,0:T(8,128)(2,1)S(1)}, u32[]{:S(2)}, u32[]{:S(2)}) collective-permute-start(bf16[256,256]{1,0:T(8,128)(2,1)S(1)} %get-tuple-element.68.refs_0_), channel_id=1, source_target_pairs={{0,2},{1,3},{2,0},{3,1},{4,6},{5,7},{6,4},{7,5},{8,10},{9,11},{10,... | collective-permute-start | bytes 393224 | tf_op jit(solution)/shard_map/ppermute | solution.py:371
  55.8 6.7 %collective-permute-start.25 = (bf16[512,256]{1,0:T(8,128)(2,1)S(1)}, bf16[512,256]{1,0:T(8,128)(2,1)S(1)}, u32[]{:S(2)}, u32[]{:S(2)}) collective-permute-start(bf16[512,256]{1,0:T(8,128)(2,1)S(1)} %get-tuple-element.66.refs_3_.refs_10_), channel_id=1, source_target_pairs={{0,16},{8,24},{16,0},{24,8},{1,17},{9,25},{17,1},{25,9},{2,18},{10... | collective-permute-start | bytes 786440 | tf_op jit(solution)/shard_map/ppermute | solution.py:371
  56.9 6.4 %collective-permute-start.24 = (bf16[512,256]{1,0:T(8,128)(2,1)S(1)}, bf16[512,256]{1,0:T(8,128)(2,1)S(1)}, u32[]{:S(2)}, u32[]{:S(2)}) collective-permute-start(bf16[512,256]{1,0:T(8,128)(2,1)S(1)} %get-tuple-element.66.refs_3_.refs_10_), channel_id=1, source_target_pairs={{0,8},{8,0},{16,24},{24,16},{1,9},{9,1},{17,25},{25,17},{2,10},{10... | collective-permute-start | bytes 786440 | tf_op jit(solution)/shard_map/ppermute | solution.py:371
  68.6 10.6 %collective-permute-start.30 = (bf16[4,128,256]{2,1,0:T(8,128)(2,1)S(1)}, bf16[4,128,256]{2,1,0:T(8,128)(2,1)S(1)}, u32[]{:S(2)}, u32[]{:S(2)}) collective-permute-start(bf16[4,128,256]{2,1,0:T(8,128)(2,1)S(1)} %get-tuple-element.85), channel_id=1, source_target_pairs={{0,8},{8,0},{16,24},{24,16},{1,9},{9,1},{17,25},{25,17},{2,10},{10... | collective-permute-start | bytes 786440 | tf_op jit(solution)/shard_map/ppermute | solution.py:371
  68.7 13.8 %collective-permute-start.31 = (bf16[4,128,256]{2,1,0:T(8,128)(2,1)S(1)}, bf16[4,128,256]{2,1,0:T(8,128)(2,1)S(1)}, u32[]{:S(2)}, u32[]{:S(2)}) collective-permute-start(bf16[4,128,256]{2,1,0:T(8,128)(2,1)S(1)} %get-tuple-element.86), channel_id=1, source_target_pairs={{0,16},{8,24},{16,0},{24,8},{1,17},{9,25},{17,1},{25,9},{2,18},{10... | collective-permute-start | bytes 786440 | tf_op jit(solution)/shard_map/ppermute | solution.py:371
  70.9 5.5 %collective-permute-start.27 = (bf16[4,64,256]{2,1,0:T(8,128)(2,1)S(1)}, bf16[4,64,256]{2,1,0:T(8,128)(2,1)S(1)}, u32[]{:S(2)}, u32[]{:S(2)}) collective-permute-start(bf16[4,64,256]{2,1,0:T(8,128)(2,1)S(1)} %get-tuple-element.79), channel_id=1, source_target_pairs={{0,2},{1,3},{2,0},{3,1},{4,6},{5,7},{6,4},{7,5},{8,10},{9,11},{10,... | collective-permute-start | bytes 393224 | tf_op jit(solution)/shard_map/ppermute | solution.py:371
  71.0 13.4 %collective-permute-start.32 = (bf16[4,128,256]{2,1,0:T(8,128)(2,1)S(1)}, bf16[4,128,256]{2,1,0:T(8,128)(2,1)S(1)}, u32[]{:S(2)}, u32[]{:S(2)}) collective-permute-start(bf16[4,128,256]{2,1,0:T(8,128)(2,1)S(1)} %get-tuple-element.87), channel_id=1, source_target_pairs={{0,24},{8,16},{16,8},{24,0},{1,25},{9,17},{17,9},{25,1},{2,26},{10... | collective-permute-start | bytes 786440 | tf_op jit(solution)/shard_map/ppermute | solution.py:371
  76.5 8.9 %collective-permute-start.29 = (bf16[4,64,256]{2,1,0:T(8,128)(2,1)S(1)}, bf16[4,64,256]{2,1,0:T(8,128)(2,1)S(1)}, u32[]{:S(2)}, u32[]{:S(2)}) collective-permute-start(bf16[4,64,256]{2,1,0:T(8,128)(2,1)S(1)} %get-tuple-element.82), channel_id=1, source_target_pairs={{0,4},{1,5},{2,6},{3,7},{4,0},{5,1},{6,2},{7,3},{8,12},{9,13},{10,... | collective-permute-start | bytes 393224 | tf_op jit(solution)/shard_map/ppermute | solution.py:371
  78.6 7.0 %collective-permute-start.28 = (bf16[4,64,256]{2,1,0:T(8,128)(2,1)S(1)}, bf16[4,64,256]{2,1,0:T(8,128)(2,1)S(1)}, u32[]{:S(2)}, u32[]{:S(2)}) collective-permute-start(bf16[4,64,256]{2,1,0:T(8,128)(2,1)S(1)} %get-tuple-element.81.refs_3_.refs_4_), channel_id=1, source_target_pairs={{0,2},{1,3},{2,0},{3,1},{4,6},{5,7},{6,4},{7,5},{8,10},{9,11},{10,... | collective-permute-start | bytes 393224 | tf_op jit(solution)/shard_map/ppermute | solution.py:371
  (14 other events, 128.8 us)

commit v5 on v4

--- a/solution.py
+++ b/solution.py
@@ -178,10 +178,6 @@
             start = pl.multiple_of(owner * part, part)
             for b in range(panel.shape[0]):
                 panel[b, pl.ds(start, part), :] = piece[b * part : (b + 1) * part, :]
-    for b in range(row_blocks):
-        row_turned[b] = row_panel[b].T
-    grad_row[...] = jnp.zeros_like(grad_row)
-    grad_turned[...] = jnp.zeros_like(grad_turned)
 
     if first:
         row_table = marg_table(row_in, row_owners, row_part, size).astype(bf16)
@@ -234,6 +230,10 @@
 
     for rows in chunks:
         make_signal(0, rows, even)
+    for b in range(row_blocks):
+        row_turned[b] = row_panel[b].T
+    grad_row[...] = jnp.zeros_like(grad_row)
+    grad_turned[...] = jnp.zeros_like(grad_turned)
     lax.fori_loop(0, pairs, pair, 0)
 
     @pl.when(2 * pairs + 1 < count)

time: 86.2 us -> 86.3 us (level)
  starting transfers between devices: 38.4 us -> 46.8 us
  waiting for transfers between devices: 33.6 us -> 26.7 us
  Pallas kernels: 12.8 us -> 11.1 us
    ppermute x33, starting transfers between devices: 38.4 us -> 46.8 us  [send(): return lax.ppermute(x, axis, [(k, k ^ mask) for k in range(count)])]
    ppermute x33, waiting for transfers between devices: 33.6 us -> 26.7 us  [send(): return lax.ppermute(x, axis, [(k, k ^ mask) for k in range(count)])]
    pallas_call x2, Pallas kernels: 6.42 us -> 5.14 us  [work(): pl.pallas_call(functools.partial(work_kernel, first, len(row_in), n_row,...]
where the time goes in v5:
time: 86.3 us; the launch traced here: 86.2 us
  starting transfers between devices  46.8 us (54%)
  waiting for transfers between devices  26.7 us (31%)
  Pallas kernels  11.1 us (13%)
  between operations  1.49 us (2%)
    ppermute x33, starting transfers between devices, send(): return lax.ppermute(x, axis, [(k, k ^ mask) for k in range(count)])  46.8 us
    ppermute x33, waiting for transfers between devices, send(): return lax.ppermute(x, axis, [(k, k ^ mask) for k in range(count)])  26.7 us
    pallas_call x2, Pallas kernels, work(): pl.pallas_call(functools.partial(work_kernel, first, len(row_in), n_row,...  5.14 us
    pallas_call x4, Pallas kernels, update(): pl.pallas_call(functools.partial(update_kernel, len(parts), len(outs)), o...  1.98 us
    pallas_call x1, Pallas kernels, pack(): pl.pallas_call(pack_kernel, out_shape=[shape((e.shape[0] * e.shape[1] + M...  1.93 us
  transfers between devices with their start and end apart: 33, of which 14 were waited for; matrix products, arithmetic and copies ran while one was open for 0% of the time, Pallas kernels for 4%

profile of v5, /device:TPU:0, one launch (start us, length us, event | category | flops | bytes accessed | tf_op | source)
XLA Modules:
  0.0 86.2 jit_solution(17718328708531578096)
XLA Ops:
  0.6 1.9 %shard_map.87 = (bf16[272,256]{1,0:T(8,128)(2,1)}, bf16[528,256]{1,0:T(8,128)(2,1)}) custom-call(f32[4,64,256]{2,1,0:T(8,128)} %emb.3, bf16[4,64]{1,0:T(4,128)(2,1)} %row_marg.1, f32[4,128,256]{2,1,0:T(8,128)} %emb.2, bf16[4,128]{1,0:T(4,128)(2,1)} %col_marg.1), custom_call_target="tpu_custom_call" | custom-call | bytes 1048576 | tf_op jit(solution)/shard_map/pallas_call | solution.py:50
  2.6 4.1 %collective-permute-start.1 = (bf16[272,256]{1,0:T(8,128)(2,1)}, bf16[272,256]{1,0:T(8,128)(2,1)S(1)}, u32[]{:S(2)}, u32[]{:S(2)}) collective-permute-start(bf16[272,256]{1,0:T(8,128)(2,1)} %get-tuple-element.47.refs_0_), channel_id=1, source_target_pairs={{0,4},{1,5},{2,6},{3,7},{4,0},{5,1},{6,2},{7,3},{8,12},{9,13},{10,... | collective-permute-start | bytes 417800 | tf_op jit(solution)/shard_map/ppermute | solution.py:371
  11.9 1.7 %shard_map.86 = (f32[8,512,512]{2,1,0:T(8,128)S(1)}, bf16[8,512,512]{2,1,0:T(8,128)(2,1)S(1)}, f32[8,128]{1,0:T(8,128)S(1)}) custom-call(s32[1]{0:T(128)} %bitcast.5.used, s32[8,512,512]{2,1,0:T(8,128)} %bitcast.10), custom_call_target="tpu_custom_call" | custom-call | bytes 12582912 | tf_op jit(solution)/shard_map/pallas_call | solution.py:99
  13.7 2.6 %collective-permute-start.2 = (bf16[1,272,256]{2,1,0:T(8,128)(2,1)S(1)}, bf16[1,272,256]{2,1,0:T(8,128)(2,1)S(1)}, u32[]{:S(2)}, u32[]{:S(2)}) collective-permute-start(bf16[1,272,256]{2,1,0:T(8,128)(2,1)S(1)} %shard_map.88.refs_2_), channel_id=1, source_target_pairs={{0,2},{1,3},{2,0},{3,1},{4,6},{5,7},{6,4},{7,5},{8,10},{9,11},{10,... | collective-permute-start | bytes 417800 | tf_op jit(solution)/shard_map/ppermute | solution.py:371
  17.0 2.3 %collective-permute-done.2.refs_3_ = bf16[1,272,256]{2,1,0:T(8,128)(2,1)S(1)} collective-permute-done((bf16[1,272,256]{2,1,0:T(8,128)(2,1)S(1)}, bf16[1,272,256]{2,1,0:T(8,128)(2,1)S(1)}, u32[]{:S(2)}, u32[]{:S(2)}) %collective-permute-start.2) | collective-permute-done | bytes 139296 | tf_op jit(solution)/shard_map/ppermute | solution.py:371
  20.5 3.6 %collective-permute-done.9.refs_15_ = bf16[528,256]{1,0:T(8,128)(2,1)S(1)} collective-permute-done((bf16[528,256]{1,0:T(8,128)(2,1)S(1)}, bf16[528,256]{1,0:T(8,128)(2,1)S(1)}, u32[]{:S(2)}, u32[]{:S(2)}) %collective-permute-start.9) | collective-permute-done | bytes 270368 | tf_op jit(solution)/shard_map/ppermute | solution.py:371
  24.1 2.7 %shard_map.90 = (f32[4,4,64,256]{3,2,1,0:T(8,128)S(1)}, bf16[4,4,64,256]{3,2,1,0:T(8,128)(2,1)S(1)}, bf16[4,128,256]{2,1,0:T(8,128)(2,1)S(1)}, bf16[4,128,256]{2...) custom-call(s32[2,8]{1,0:T(2,128)S(1)} %bitcast.8, ...), custom_call_target="tpu_custom_call" | custom-call | flops 3221225472 | bytes 16777216 | tf_op jit(solution)/shard_map/pallas_call | solution.py:279
  26.9 2.8 %collective-permute-start.14 = (bf16[4,128,256]{2,1,0:T(8,128)(2,1)S(1)}, bf16[4,128,256]{2,1,0:T(8,128)(2,1)S(1)}, u32[]{:S(2)}, u32[]{:S(2)}) collective-permute-start(bf16[4,128,256]{2,1,0:T(8,128)(2,1)S(1)} %get-tuple-element.63), channel_id=1, source_target_pairs={{0,8},{8,0},{16,24},{24,16},{1,9},{9,1},{17,25},{25,17},{2,10},{10... | collective-permute-start | bytes 786440 | tf_op jit(solution)/shard_map/ppermute | solution.py:371
  31.3 2.4 %collective-permute-start.11 = (bf16[4,64,256]{2,1,0:T(8,128)(2,1)S(1)}, bf16[4,64,256]{2,1,0:T(8,128)(2,1)S(1)}, u32[]{:S(2)}, u32[]{:S(2)}) collective-permute-start(bf16[4,64,256]{2,1,0:T(8,128)(2,1)S(1)} %get-tuple-element.58), channel_id=1, source_target_pairs={{0,2},{1,3},{2,0},{3,1},{4,6},{5,7},{6,4},{7,5},{8,10},{9,11},{10,... | collective-permute-start | bytes 393224 | tf_op jit(solution)/shard_map/ppermute | solution.py:371
  33.7 3.3 %collective-permute-done.11.refs_0_ = bf16[4,64,256]{2,1,0:T(8,128)(2,1)S(1)} collective-permute-done((bf16[4,64,256]{2,1,0:T(8,128)(2,1)S(1)}, bf16[4,64,256]{2,1,0:T(8,128)(2,1)S(1)}, u32[]{:S(2)}, u32[]{:S(2)}) %collective-permute-start.11) | collective-permute-done | bytes 131104 | tf_op jit(solution)/shard_map/ppermute | solution.py:371
  37.0 3.9 %collective-permute-start.13 = (bf16[4,64,256]{2,1,0:T(8,128)(2,1)S(1)}, bf16[4,64,256]{2,1,0:T(8,128)(2,1)S(1)}, u32[]{:S(2)}, u32[]{:S(2)}) collective-permute-start(bf16[4,64,256]{2,1,0:T(8,128)(2,1)S(1)} %get-tuple-element.61), channel_id=1, source_target_pairs={{0,4},{1,5},{2,6},{3,7},{4,0},{5,1},{6,2},{7,3},{8,12},{9,13},{10,... | collective-permute-start | bytes 393224 | tf_op jit(solution)/shard_map/ppermute | solution.py:371
  40.9 1.7 %collective-permute-start.12 = (bf16[4,64,256]{2,1,0:T(8,128)(2,1)S(1)}, bf16[4,64,256]{2,1,0:T(8,128)(2,1)S(1)}, u32[]{:S(2)}, u32[]{:S(2)}) collective-permute-start(bf16[4,64,256]{2,1,0:T(8,128)(2,1)S(1)} %get-tuple-element.60.refs_4_), channel_id=1, source_target_pairs={{0,2},{1,3},{2,0},{3,1},{4,6},{5,7},{6,4},{7,5},{8,10},{9,11},{10,... | collective-permute-start | bytes 393224 | tf_op jit(solution)/shard_map/ppermute | solution.py:371
  48.2 2.4 %collective-permute-start.17 = (bf16[256,256]{1,0:T(8,128)(2,1)S(1)}, bf16[256,256]{1,0:T(8,128)(2,1)S(1)}, u32[]{:S(2)}, u32[]{:S(2)}) collective-permute-start(bf16[256,256]{1,0:T(8,128)(2,1)S(1)} %get-tuple-element.68.refs_0_), channel_id=1, source_target_pairs={{0,2},{1,3},{2,0},{3,1},{4,6},{5,7},{6,4},{7,5},{8,10},{9,11},{10,... | collective-permute-start | bytes 393224 | tf_op jit(solution)/shard_map/ppermute | solution.py:371
  50.6 3.1 %collective-permute-done.18.refs_0_ = bf16[256,256]{1,0:T(8,128)(2,1)S(1)} collective-permute-done((bf16[256,256]{1,0:T(8,128)(2,1)S(1)}, bf16[256,256]{1,0:T(8,128)(2,1)S(1)}, u32[]{:S(2)}, u32[]{:S(2)}) %collective-permute-start.18) | collective-permute-done | bytes 131104 | tf_op jit(solution)/shard_map/ppermute | solution.py:371
  56.5 2.3 %collective-permute-done.20.refs_3_ = bf16[1,256,256]{2,1,0:T(8,128)(2,1)S(1)} collective-permute-done((bf16[1,256,256]{2,1,0:T(8,128)(2,1)S(1)}, bf16[1,256,256]{2,1,0:T(8,128)(2,1)S(1)}, u32[]{:S(2)}, u32[]{:S(2)}) %collective-permute-start.20) | collective-permute-done | bytes 131104 | tf_op jit(solution)/shard_map/ppermute | solution.py:371
  59.5 2.2 %collective-permute-done.25.refs_12_ = bf16[512,256]{1,0:T(8,128)(2,1)S(1)} collective-permute-done((bf16[512,256]{1,0:T(8,128)(2,1)S(1)}, bf16[512,256]{1,0:T(8,128)(2,1)S(1)}, u32[]{:S(2)}, u32[]{:S(2)}) %collective-permute-start.25) | collective-permute-done | bytes 262176 | tf_op jit(solution)/shard_map/ppermute | solution.py:371
  62.7 2.4 %shard_map.97 = (f32[4,4,64,256]{3,2,1,0:T(8,128)S(1)}, bf16[4,4,64,256]{3,2,1,0:T(8,128)(2,1)S(1)}, bf16[4,128,256]{2,1,0:T(8,128)(2,1)S(1)}, bf16[4,128,256]{2...) custom-call(s32[2,8]{1,0:T(2,128)S(1)} %bitcast.9, s32[1]{0:T(128)} %bitcast.7.refs_1_, ...), custom_call_target="tpu_custom_call" | custom-call | flops 3221225472 | bytes 16777216 | tf_op jit(solution)/shard_map/pallas_call | solution.py:279
  65.3 2.0 %collective-permute-start.30 = (bf16[4,128,256]{2,1,0:T(8,128)(2,1)S(1)}, bf16[4,128,256]{2,1,0:T(8,128)(2,1)S(1)}, u32[]{:S(2)}, u32[]{:S(2)}) collective-permute-start(bf16[4,128,256]{2,1,0:T(8,128)(2,1)S(1)} %get-tuple-element.85), channel_id=1, source_target_pairs={{0,8},{8,0},{16,24},{24,16},{1,9},{9,1},{17,25},{25,17},{2,10},{10... | collective-permute-start | bytes 786440 | tf_op jit(solution)/shard_map/ppermute | solution.py:371
  67.4 3.5 %collective-permute-start.27 = (bf16[4,64,256]{2,1,0:T(8,128)(2,1)S(1)}, bf16[4,64,256]{2,1,0:T(8,128)(2,1)S(1)}, u32[]{:S(2)}, u32[]{:S(2)}) collective-permute-start(bf16[4,64,256]{2,1,0:T(8,128)(2,1)S(1)} %get-tuple-element.79), channel_id=1, source_target_pairs={{0,2},{1,3},{2,0},{3,1},{4,6},{5,7},{6,4},{7,5},{8,10},{9,11},{10,... | collective-permute-start | bytes 393224 | tf_op jit(solution)/shard_map/ppermute | solution.py:371
  70.9 1.6 %collective-permute-start.32 = (bf16[4,128,256]{2,1,0:T(8,128)(2,1)S(1)}, bf16[4,128,256]{2,1,0:T(8,128)(2,1)S(1)}, u32[]{:S(2)}, u32[]{:S(2)}) collective-permute-start(bf16[4,128,256]{2,1,0:T(8,128)(2,1)S(1)} %get-tuple-element.87), channel_id=1, source_target_pairs={{0,24},{8,16},{16,8},{24,0},{1,25},{9,17},{17,9},{25,1},{2,26},{10... | collective-permute-start | bytes 786440 | tf_op jit(solution)/shard_map/ppermute | solution.py:371
  72.6 2.1 %collective-permute-done.27.refs_0_ = bf16[4,64,256]{2,1,0:T(8,128)(2,1)S(1)} collective-permute-done((bf16[4,64,256]{2,1,0:T(8,128)(2,1)S(1)}, bf16[4,64,256]{2,1,0:T(8,128)(2,1)S(1)}, u32[]{:S(2)}, u32[]{:S(2)}) %collective-permute-start.27) | collective-permute-done | bytes 131104 | tf_op jit(solution)/shard_map/ppermute | solution.py:371
  74.7 4.1 %collective-permute-start.29 = (bf16[4,64,256]{2,1,0:T(8,128)(2,1)S(1)}, bf16[4,64,256]{2,1,0:T(8,128)(2,1)S(1)}, u32[]{:S(2)}, u32[]{:S(2)}) collective-permute-start(bf16[4,64,256]{2,1,0:T(8,128)(2,1)S(1)} %get-tuple-element.82), channel_id=1, source_target_pairs={{0,4},{1,5},{2,6},{3,7},{4,0},{5,1},{6,2},{7,3},{8,12},{9,13},{10,... | collective-permute-start | bytes 393224 | tf_op jit(solution)/shard_map/ppermute | solution.py:371
  78.8 1.7 %collective-permute-start.28 = (bf16[4,64,256]{2,1,0:T(8,128)(2,1)S(1)}, bf16[4,64,256]{2,1,0:T(8,128)(2,1)S(1)}, u32[]{:S(2)}, u32[]{:S(2)}) collective-permute-start(bf16[4,64,256]{2,1,0:T(8,128)(2,1)S(1)} %get-tuple-element.81.refs_3_.refs_4_), channel_id=1, source_target_pairs={{0,2},{1,3},{2,0},{3,1},{4,6},{5,7},{6,4},{7,5},{8,10},{9,11},{10,... | collective-permute-start | bytes 393224 | tf_op jit(solution)/shard_map/ppermute | solution.py:371
  82.3 2.8 %collective-permute-done.29.refs_2_ = bf16[4,64,256]{2,1,0:T(8,128)(2,1)S(1)} collective-permute-done((bf16[4,64,256]{2,1,0:T(8,128)(2,1)S(1)}, bf16[4,64,256]{2,1,0:T(8,128)(2,1)S(1)}, u32[]{:S(2)}, u32[]{:S(2)}) %collective-permute-start.29) | collective-permute-done | bytes 131104 | tf_op jit(solution)/shard_map/ppermute | solution.py:371
  (68 shorter events, 21.3 us)
Async XLA Ops:
  2.6 11.1 %collective-permute-start.1 = (bf16[272,256]{1,0:T(8,128)(2,1)}, bf16[272,256]{1,0:T(8,128)(2,1)S(1)}, u32[]{:S(2)}, u32[]{:S(2)}) collective-permute-start(bf16[272,256]{1,0:T(8,128)(2,1)} %get-tuple-element.47.refs_0_), channel_id=1, source_target_pairs={{0,4},{1,5},{2,6},{3,7},{4,0},{5,1},{6,2},{7,3},{8,12},{9,13},{10,... | collective-permute-start | bytes 417800 | tf_op jit(solution)/shard_map/ppermute | solution.py:371
  6.7 10.3 %collective-permute-start.4 = (bf16[528,256]{1,0:T(8,128)(2,1)}, bf16[528,256]{1,0:T(8,128)(2,1)S(1)}, u32[]{:S(2)}, u32[]{:S(2)}) collective-permute-start(bf16[528,256]{1,0:T(8,128)(2,1)} %get-tuple-element.49.refs_12_), channel_id=1, source_target_pairs={{0,16},{8,24},{16,0},{24,8},{1,17},{9,25},{17,1},{25,9},{2,18},{10... | collective-permute-start | bytes 811016 | tf_op jit(solution)/shard_map/ppermute | solution.py:371
  8.2 8.8 %collective-permute-start.3 = (bf16[528,256]{1,0:T(8,128)(2,1)}, bf16[528,256]{1,0:T(8,128)(2,1)S(1)}, u32[]{:S(2)}, u32[]{:S(2)}) collective-permute-start(bf16[528,256]{1,0:T(8,128)(2,1)} %get-tuple-element.49.refs_12_), channel_id=1, source_target_pairs={{0,8},{8,0},{16,24},{24,16},{1,9},{9,1},{17,25},{25,17},{2,10},{10... | collective-permute-start | bytes 811016 | tf_op jit(solution)/shard_map/ppermute | solution.py:371
  9.7 7.3 %collective-permute-start = (bf16[272,256]{1,0:T(8,128)(2,1)}, bf16[272,256]{1,0:T(8,128)(2,1)S(1)}, u32[]{:S(2)}, u32[]{:S(2)}) collective-permute-start(bf16[272,256]{1,0:T(8,128)(2,1)} %get-tuple-element.47.refs_0_), channel_id=1, source_target_pairs={{0,2},{1,3},{2,0},{3,1},{4,6},{5,7},{6,4},{7,5},{8,10},{9,11},{10,... | collective-permute-start | bytes 417800 | tf_op jit(solution)/shard_map/ppermute | solution.py:371
  13.7 5.6 %collective-permute-start.2 = (bf16[1,272,256]{2,1,0:T(8,128)(2,1)S(1)}, bf16[1,272,256]{2,1,0:T(8,128)(2,1)S(1)}, u32[]{:S(2)}, u32[]{:S(2)}) collective-permute-start(bf16[1,272,256]{2,1,0:T(8,128)(2,1)S(1)} %shard_map.88.refs_2_), channel_id=1, source_target_pairs={{0,2},{1,3},{2,0},{3,1},{4,6},{5,7},{6,4},{7,5},{8,10},{9,11},{10,... | collective-permute-start | bytes 417800 | tf_op jit(solution)/shard_map/ppermute | solution.py:371
  16.3 7.7 %collective-permute-start.9 = (bf16[528,256]{1,0:T(8,128)(2,1)S(1)}, bf16[528,256]{1,0:T(8,128)(2,1)S(1)}, u32[]{:S(2)}, u32[]{:S(2)}) collective-permute-start(bf16[528,256]{1,0:T(8,128)(2,1)S(1)} %copy-done.2), channel_id=1, source_target_pairs={{0,24},{8,16},{16,8},{24,0},{1,25},{9,17},{17,9},{25,1},{2,26},{10... | collective-permute-start | bytes 811016 | tf_op jit(solution)/shard_map/ppermute | solution.py:371
  26.9 15.8 %collective-permute-start.14 = (bf16[4,128,256]{2,1,0:T(8,128)(2,1)S(1)}, bf16[4,128,256]{2,1,0:T(8,128)(2,1)S(1)}, u32[]{:S(2)}, u32[]{:S(2)}) collective-permute-start(bf16[4,128,256]{2,1,0:T(8,128)(2,1)S(1)} %get-tuple-element.63), channel_id=1, source_target_pairs={{0,8},{8,0},{16,24},{24,16},{1,9},{9,1},{17,25},{25,17},{2,10},{10... | collective-permute-start | bytes 786440 | tf_op jit(solution)/shard_map/ppermute | solution.py:371
  29.6 14.0 %collective-permute-start.15 = (bf16[4,128,256]{2,1,0:T(8,128)(2,1)S(1)}, bf16[4,128,256]{2,1,0:T(8,128)(2,1)S(1)}, u32[]{:S(2)}, u32[]{:S(2)}) collective-permute-start(bf16[4,128,256]{2,1,0:T(8,128)(2,1)S(1)} %get-tuple-element.64), channel_id=1, source_target_pairs={{0,16},{8,24},{16,0},{24,8},{1,17},{9,25},{17,1},{25,9},{2,18},{10... | collective-permute-start | bytes 786440 | tf_op jit(solution)/shard_map/ppermute | solution.py:371
  29.6 14.0 %collective-permute-start.16 = (bf16[4,128,256]{2,1,0:T(8,128)(2,1)S(1)}, bf16[4,128,256]{2,1,0:T(8,128)(2,1)S(1)}, u32[]{:S(2)}, u32[]{:S(2)}) collective-permute-start(bf16[4,128,256]{2,1,0:T(8,128)(2,1)S(1)} %get-tuple-element.65), channel_id=1, source_target_pairs={{0,24},{8,16},{16,8},{24,0},{1,25},{9,17},{17,9},{25,1},{2,26},{10... | collective-permute-start | bytes 786440 | tf_op jit(solution)/shard_map/ppermute | solution.py:371
  31.3 5.7 %collective-permute-start.11 = (bf16[4,64,256]{2,1,0:T(8,128)(2,1)S(1)}, bf16[4,64,256]{2,1,0:T(8,128)(2,1)S(1)}, u32[]{:S(2)}, u32[]{:S(2)}) collective-permute-start(bf16[4,64,256]{2,1,0:T(8,128)(2,1)S(1)} %get-tuple-element.58), channel_id=1, source_target_pairs={{0,2},{1,3},{2,0},{3,1},{4,6},{5,7},{6,4},{7,5},{8,10},{9,11},{10,... | collective-permute-start | bytes 393224 | tf_op jit(solution)/shard_map/ppermute | solution.py:371
  37.0 9.5 %collective-permute-start.13 = (bf16[4,64,256]{2,1,0:T(8,128)(2,1)S(1)}, bf16[4,64,256]{2,1,0:T(8,128)(2,1)S(1)}, u32[]{:S(2)}, u32[]{:S(2)}) collective-permute-start(bf16[4,64,256]{2,1,0:T(8,128)(2,1)S(1)} %get-tuple-element.61), channel_id=1, source_target_pairs={{0,4},{1,5},{2,6},{3,7},{4,0},{5,1},{6,2},{7,3},{8,12},{9,13},{10,... | collective-permute-start | bytes 393224 | tf_op jit(solution)/shard_map/ppermute | solution.py:371
  40.9 6.0 %collective-permute-start.12 = (bf16[4,64,256]{2,1,0:T(8,128)(2,1)S(1)}, bf16[4,64,256]{2,1,0:T(8,128)(2,1)S(1)}, u32[]{:S(2)}, u32[]{:S(2)}) collective-permute-start(bf16[4,64,256]{2,1,0:T(8,128)(2,1)S(1)} %get-tuple-element.60.refs_4_), channel_id=1, source_target_pairs={{0,2},{1,3},{2,0},{3,1},{4,6},{5,7},{6,4},{7,5},{8,10},{9,11},{10,... | collective-permute-start | bytes 393224 | tf_op jit(solution)/shard_map/ppermute | solution.py:371
  43.8 9.9 %collective-permute-start.19 = (bf16[512,256]{1,0:T(8,128)(2,1)S(1)}, bf16[512,256]{1,0:T(8,128)(2,1)S(1)}, u32[]{:S(2)}, u32[]{:S(2)}) collective-permute-start(bf16[512,256]{1,0:T(8,128)(2,1)S(1)} %get-tuple-element.66.refs_3_.refs_10_), channel_id=1, source_target_pairs={{0,24},{8,16},{16,8},{24,0},{1,25},{9,17},{17,9},{25,1},{2,26},{10... | collective-permute-start | bytes 786440 | tf_op jit(solution)/shard_map/ppermute | solution.py:371
  47.0 6.8 %collective-permute-start.18 = (bf16[256,256]{1,0:T(8,128)(2,1)S(1)}, bf16[256,256]{1,0:T(8,128)(2,1)S(1)}, u32[]{:S(2)}, u32[]{:S(2)}) collective-permute-start(bf16[256,256]{1,0:T(8,128)(2,1)S(1)} %get-tuple-element.68.refs_0_), channel_id=1, source_target_pairs={{0,4},{1,5},{2,6},{3,7},{4,0},{5,1},{6,2},{7,3},{8,12},{9,13},{10,... | collective-permute-start | bytes 393224 | tf_op jit(solution)/shard_map/ppermute | solution.py:371
  48.2 8.3 %collective-permute-start.17 = (bf16[256,256]{1,0:T(8,128)(2,1)S(1)}, bf16[256,256]{1,0:T(8,128)(2,1)S(1)}, u32[]{:S(2)}, u32[]{:S(2)}) collective-permute-start(bf16[256,256]{1,0:T(8,128)(2,1)S(1)} %get-tuple-element.68.refs_0_), channel_id=1, source_target_pairs={{0,2},{1,3},{2,0},{3,1},{4,6},{5,7},{6,4},{7,5},{8,10},{9,11},{10,... | collective-permute-start | bytes 393224 | tf_op jit(solution)/shard_map/ppermute | solution.py:371
  53.7 5.0 %collective-permute-start.20 = (bf16[1,256,256]{2,1,0:T(8,128)(2,1)S(1)}, bf16[1,256,256]{2,1,0:T(8,128)(2,1)S(1)}, u32[]{:S(2)}, u32[]{:S(2)}) collective-permute-start(bf16[1,256,256]{2,1,0:T(8,128)(2,1)S(1)} %shard_map.95.refs_2_), channel_id=1, source_target_pairs={{0,2},{1,3},{2,0},{3,1},{4,6},{5,7},{6,4},{7,5},{8,10},{9,11},{10,... | collective-permute-start | bytes 393224 | tf_op jit(solution)/shard_map/ppermute | solution.py:371
  55.1 6.6 %collective-permute-start.25 = (bf16[512,256]{1,0:T(8,128)(2,1)S(1)}, bf16[512,256]{1,0:T(8,128)(2,1)S(1)}, u32[]{:S(2)}, u32[]{:S(2)}) collective-permute-start(bf16[512,256]{1,0:T(8,128)(2,1)S(1)} %get-tuple-element.66.refs_3_.refs_10_), channel_id=1, source_target_pairs={{0,16},{8,24},{16,0},{24,8},{1,17},{9,25},{17,1},{25,9},{2,18},{10... | collective-permute-start | bytes 786440 | tf_op jit(solution)/shard_map/ppermute | solution.py:371
  56.0 6.7 %collective-permute-start.24 = (bf16[512,256]{1,0:T(8,128)(2,1)S(1)}, bf16[512,256]{1,0:T(8,128)(2,1)S(1)}, u32[]{:S(2)}, u32[]{:S(2)}) collective-permute-start(bf16[512,256]{1,0:T(8,128)(2,1)S(1)} %get-tuple-element.66.refs_3_.refs_10_), channel_id=1, source_target_pairs={{0,8},{8,0},{16,24},{24,16},{1,9},{9,1},{17,25},{25,17},{2,10},{10... | collective-permute-start | bytes 786440 | tf_op jit(solution)/shard_map/ppermute | solution.py:371
  65.3 15.3 %collective-permute-start.30 = (bf16[4,128,256]{2,1,0:T(8,128)(2,1)S(1)}, bf16[4,128,256]{2,1,0:T(8,128)(2,1)S(1)}, u32[]{:S(2)}, u32[]{:S(2)}) collective-permute-start(bf16[4,128,256]{2,1,0:T(8,128)(2,1)S(1)} %get-tuple-element.85), channel_id=1, source_target_pairs={{0,8},{8,0},{16,24},{24,16},{1,9},{9,1},{17,25},{25,17},{2,10},{10... | collective-permute-start | bytes 786440 | tf_op jit(solution)/shard_map/ppermute | solution.py:371
  67.3 14.0 %collective-permute-start.31 = (bf16[4,128,256]{2,1,0:T(8,128)(2,1)S(1)}, bf16[4,128,256]{2,1,0:T(8,128)(2,1)S(1)}, u32[]{:S(2)}, u32[]{:S(2)}) collective-permute-start(bf16[4,128,256]{2,1,0:T(8,128)(2,1)S(1)} %get-tuple-element.86), channel_id=1, source_target_pairs={{0,16},{8,24},{16,0},{24,8},{1,17},{9,25},{17,1},{25,9},{2,18},{10... | collective-permute-start | bytes 786440 | tf_op jit(solution)/shard_map/ppermute | solution.py:371
  67.4 7.3 %collective-permute-start.27 = (bf16[4,64,256]{2,1,0:T(8,128)(2,1)S(1)}, bf16[4,64,256]{2,1,0:T(8,128)(2,1)S(1)}, u32[]{:S(2)}, u32[]{:S(2)}) collective-permute-start(bf16[4,64,256]{2,1,0:T(8,128)(2,1)S(1)} %get-tuple-element.79), channel_id=1, source_target_pairs={{0,2},{1,3},{2,0},{3,1},{4,6},{5,7},{6,4},{7,5},{8,10},{9,11},{10,... | collective-permute-start | bytes 393224 | tf_op jit(solution)/shard_map/ppermute | solution.py:371
  70.9 10.4 %collective-permute-start.32 = (bf16[4,128,256]{2,1,0:T(8,128)(2,1)S(1)}, bf16[4,128,256]{2,1,0:T(8,128)(2,1)S(1)}, u32[]{:S(2)}, u32[]{:S(2)}) collective-permute-start(bf16[4,128,256]{2,1,0:T(8,128)(2,1)S(1)} %get-tuple-element.87), channel_id=1, source_target_pairs={{0,24},{8,16},{16,8},{24,0},{1,25},{9,17},{17,9},{25,1},{2,26},{10... | collective-permute-start | bytes 786440 | tf_op jit(solution)/shard_map/ppermute | solution.py:371
  74.7 10.3 %collective-permute-start.29 = (bf16[4,64,256]{2,1,0:T(8,128)(2,1)S(1)}, bf16[4,64,256]{2,1,0:T(8,128)(2,1)S(1)}, u32[]{:S(2)}, u32[]{:S(2)}) collective-permute-start(bf16[4,64,256]{2,1,0:T(8,128)(2,1)S(1)} %get-tuple-element.82), channel_id=1, source_target_pairs={{0,4},{1,5},{2,6},{3,7},{4,0},{5,1},{6,2},{7,3},{8,12},{9,13},{10,... | collective-permute-start | bytes 393224 | tf_op jit(solution)/shard_map/ppermute | solution.py:371
  78.8 6.6 %collective-permute-start.28 = (bf16[4,64,256]{2,1,0:T(8,128)(2,1)S(1)}, bf16[4,64,256]{2,1,0:T(8,128)(2,1)S(1)}, u32[]{:S(2)}, u32[]{:S(2)}) collective-permute-start(bf16[4,64,256]{2,1,0:T(8,128)(2,1)S(1)} %get-tuple-element.81.refs_3_.refs_4_), channel_id=1, source_target_pairs={{0,2},{1,3},{2,0},{3,1},{4,6},{5,7},{6,4},{7,5},{8,10},{9,11},{10,... | collective-permute-start | bytes 393224 | tf_op jit(solution)/shard_map/ppermute | solution.py:371
  (14 other events, 131.2 us)

commit v6 on v5

--- a/solution.py
+++ b/solution.py
@@ -379,7 +379,8 @@
     half = n_col_dev // 2
     far = half // 2
     near = range(1, far)
-    row_owner = [2 * k for k in range(half)] + [2 * k + 1 for k in range(half)]
+    distances = [0, *reversed(range(1, half))]
+    row_owner = [2 * k for k in distances] + [2 * k + 1 for k in distances]
     col_owner = list(range(n_row_dev))
 
     def hop(x, distance):
@@ -389,15 +390,9 @@
     *tabs, tabs_made = levels(used, tiles)
     tables = None
     for substep in range(2):
-        crossed = hop(row_pay, far)
+        row_in = [row_pay] + [hop(row_pay, k) for k in distances[1:]]
         col_in = [col_pay] + [send(col_pay, "row", n_row_dev, k) for k in col_owner[1:]]
-        if substep == 0:
-            before_leg, before_swap, sizes = [tabs_made], col_in[1:-1], [1, far - 1, 1, far - 1]
-        else:
-            before_leg, before_swap, sizes = col_in[-1:], [], [far, 1, far - 1]
-        (crossed,) = join([crossed], [1], before_leg)
-        row_in = [row_pay] + [hop(row_pay, k) for k in near] + [crossed] + [hop(crossed, k) for k in near]
-        row_in = join(row_in, sizes, before_swap)
+        row_in = join(row_in, [1] * half, col_in[1:-1] + ([tabs_made] if substep == 0 else []))
         row_in += [send(piece, "col", n_col_dev, 1) for piece in row_in]
         keep, swap, col_out, made = work(
             listing, used, tabs, row_in, col_in, tables, row_owner, col_owner, dims

time: 86.3 us -> 85.4 us (0.990); the launches traced: 86.2 us -> 84.3 us
  starting transfers between devices: 46.8 us -> 39.1 us
  waiting for transfers between devices: 26.7 us -> 29.6 us
  Pallas kernels: 11.1 us -> 14 us
    ppermute x33 -> x34, starting transfers between devices: 46.8 us -> 39.1 us  [send(): return lax.ppermute(x, axis, [(k, k ^ mask) for k in range(count)])]
    ppermute x33 -> x34, waiting for transfers between devices: 26.7 us -> 29.6 us  [send(): return lax.ppermute(x, axis, [(k, k ^ mask) for k in range(count)])]
    pallas_call x2, Pallas kernels: 5.14 us -> 7.24 us  [work(): pl.pallas_call(functools.partial(work_kernel, first, len(row_in), n_row,...]
  transfers between devices with their start and end apart: 33 -> 34, of which waited for: 14 -> 19; matrix products, arithmetic and copies ran while one was open for 0% -> 0% of each run, Pallas kernels for 4% -> 5%
where the time goes in v6:
time: 85.4 us; the launch traced here: 84.3 us
  starting transfers between devices  39.1 us (46%)
  waiting for transfers between devices  29.6 us (35%)
  Pallas kernels  14 us (16%)
  between operations  1.45 us (2%)
    ppermute x34, starting transfers between devices, send(): return lax.ppermute(x, axis, [(k, k ^ mask) for k in range(count)])  39.1 us
    ppermute x34, waiting for transfers between devices, send(): return lax.ppermute(x, axis, [(k, k ^ mask) for k in range(count)])  29.6 us
    pallas_call x2, Pallas kernels, work(): pl.pallas_call(functools.partial(work_kernel, first, len(row_in), n_row,...  7.24 us
    pallas_call x1, Pallas kernels, levels(): pl.pallas_call(levels_kernel, out_shape=[shape(tiles.shape, f32), shape(t...  2.54 us
    pallas_call x4, Pallas kernels, update(): pl.pallas_call(functools.partial(update_kernel, len(parts), len(outs)), o...  1.98 us
    pallas_call x1, Pallas kernels, pack(): pl.pallas_call(pack_kernel, out_shape=[shape((e.shape[0] * e.shape[1] + M...  1.93 us
  transfers between devices with their start and end apart: 34, of which 19 were waited for; matrix products, arithmetic and copies ran while one was open for 0% of the time, Pallas kernels for 5%

profile of v6, /device:TPU:0, one launch (start us, length us, event | category | flops | bytes accessed | tf_op | source)
XLA Modules:
  0.0 84.3 jit_solution(7426658816108067838)
XLA Ops:
  0.6 1.9 %shard_map.87 = (bf16[272,256]{1,0:T(8,128)(2,1)}, bf16[528,256]{1,0:T(8,128)(2,1)}) custom-call(f32[4,64,256]{2,1,0:T(8,128)} %emb.3, bf16[4,64]{1,0:T(4,128)(2,1)} %row_marg.1, f32[4,128,256]{2,1,0:T(8,128)} %emb.2, bf16[4,128]{1,0:T(4,128)(2,1)} %col_marg.1), custom_call_target="tpu_custom_call" | custom-call | bytes 1048576 | tf_op jit(solution)/shard_map/pallas_call | solution.py:50
  2.6 3.0 %collective-permute-start.4 = (bf16[528,256]{1,0:T(8,128)(2,1)}, bf16[528,256]{1,0:T(8,128)(2,1)S(1)}, u32[]{:S(2)}, u32[]{:S(2)}) collective-permute-start(bf16[528,256]{1,0:T(8,128)(2,1)} %get-tuple-element.49.refs_12_), channel_id=1, source_target_pairs={{0,16},{8,24},{16,0},{24,8},{1,17},{9,25},{17,1},{25,9},{2,18},{10... | collective-permute-start | bytes 811016 | tf_op jit(solution)/shard_map/ppermute | solution.py:371
  8.7 2.6 %collective-permute-start.1 = (bf16[272,256]{1,0:T(8,128)(2,1)}, bf16[272,256]{1,0:T(8,128)(2,1)S(1)}, u32[]{:S(2)}, u32[]{:S(2)}) collective-permute-start(bf16[272,256]{1,0:T(8,128)(2,1)} %get-tuple-element.48.refs_0_), channel_id=1, source_target_pairs={{0,4},{1,5},{2,6},{3,7},{4,0},{5,1},{6,2},{7,3},{8,12},{9,13},{10,... | collective-permute-start | bytes 417800 | tf_op jit(solution)/shard_map/ppermute | solution.py:371
  11.5 2.5 %collective-permute-done.2.refs_3_ = bf16[272,256]{1,0:T(8,128)(2,1)S(1)} collective-permute-done((bf16[272,256]{1,0:T(8,128)(2,1)}, bf16[272,256]{1,0:T(8,128)(2,1)S(1)}, u32[]{:S(2)}, u32[]{:S(2)}) %collective-permute-start.2) | collective-permute-done | bytes 139296 | tf_op jit(solution)/shard_map/ppermute | solution.py:371
  14.7 2.5 %shard_map.86 = (f32[8,512,512]{2,1,0:T(8,128)S(1)}, bf16[8,512,512]{2,1,0:T(8,128)(2,1)S(1)}, f32[8,128]{1,0:T(8,128)S(1)}) custom-call(s32[1]{0:T(128)} %bitcast.5.used, s32[8,512,512]{2,1,0:T(8,128)} %bitcast.10), custom_call_target="tpu_custom_call" | custom-call | bytes 12582912 | tf_op jit(solution)/shard_map/pallas_call | solution.py:99
  17.2 4.7 %collective-permute-done.1.refs_2_ = bf16[272,256]{1,0:T(8,128)(2,1)S(1)} collective-permute-done((bf16[272,256]{1,0:T(8,128)(2,1)}, bf16[272,256]{1,0:T(8,128)(2,1)S(1)}, u32[]{:S(2)}, u32[]{:S(2)}) %collective-permute-start.1) | collective-permute-done | bytes 139296 | tf_op jit(solution)/shard_map/ppermute | solution.py:371
  24.1 3.8 %shard_map.89 = (f32[4,4,64,256]{3,2,1,0:T(8,128)S(1)}, bf16[4,4,64,256]{3,2,1,0:T(8,128)(2,1)S(1)}, bf16[4,128,256]{2,1,0:T(8,128)(2,1)S(1)}, bf16[4,128,256]{2...) custom-call(s32[2,8]{1,0:T(2,128)S(1)} %bitcast.8, ...), custom_call_target="tpu_custom_call" | custom-call | flops 3221225472 | bytes 16777216 | tf_op jit(solution)/shard_map/pallas_call | solution.py:279
  28.3 2.2 %collective-permute-start.15 = (bf16[4,128,256]{2,1,0:T(8,128)(2,1)S(1)}, bf16[4,128,256]{2,1,0:T(8,128)(2,1)S(1)}, u32[]{:S(2)}, u32[]{:S(2)}) collective-permute-start(bf16[4,128,256]{2,1,0:T(8,128)(2,1)S(1)} %get-tuple-element.65), channel_id=1, source_target_pairs={{0,16},{8,24},{16,0},{24,8},{1,17},{9,25},{17,1},{25,9},{2,18},{10... | collective-permute-start | bytes 786440 | tf_op jit(solution)/shard_map/ppermute | solution.py:371
  30.6 2.5 %collective-permute-start.11 = (bf16[4,64,256]{2,1,0:T(8,128)(2,1)S(1)}, bf16[4,64,256]{2,1,0:T(8,128)(2,1)S(1)}, u32[]{:S(2)}, u32[]{:S(2)}) collective-permute-start(bf16[4,64,256]{2,1,0:T(8,128)(2,1)S(1)} %get-tuple-element.59), channel_id=1, source_target_pairs={{0,2},{1,3},{2,0},{3,1},{4,6},{5,7},{6,4},{7,5},{8,10},{9,11},{10,... | collective-permute-start | bytes 393224 | tf_op jit(solution)/shard_map/ppermute | solution.py:371
  34.6 2.1 %collective-permute-done.11.refs_0_ = bf16[4,64,256]{2,1,0:T(8,128)(2,1)S(1)} collective-permute-done((bf16[4,64,256]{2,1,0:T(8,128)(2,1)S(1)}, bf16[4,64,256]{2,1,0:T(8,128)(2,1)S(1)}, u32[]{:S(2)}, u32[]{:S(2)}) %collective-permute-start.11) | collective-permute-done | bytes 131104 | tf_op jit(solution)/shard_map/ppermute | solution.py:371
  38.4 1.7 %collective-permute-start.12 = (bf16[4,64,256]{2,1,0:T(8,128)(2,1)S(1)}, bf16[4,64,256]{2,1,0:T(8,128)(2,1)S(1)}, u32[]{:S(2)}, u32[]{:S(2)}) collective-permute-start(bf16[4,64,256]{2,1,0:T(8,128)(2,1)S(1)} %get-tuple-element.61.refs_4_), channel_id=1, source_target_pairs={{0,2},{1,3},{2,0},{3,1},{4,6},{5,7},{6,4},{7,5},{8,10},{9,11},{10,... | collective-permute-start | bytes 393224 | tf_op jit(solution)/shard_map/ppermute | solution.py:371
  40.1 1.9 %collective-permute-done.15.refs_2_ = bf16[4,128,256]{2,1,0:T(8,128)(2,1)S(1)} collective-permute-done((bf16[4,128,256]{2,1,0:T(8,128)(2,1)S(1)}, bf16[4,128,256]{2,1,0:T(8,128)(2,1)S(1)}, u32[]{:S(2)}, u32[]{:S(2)}) %collective-permute-start.15) | collective-permute-done | bytes 262176 | tf_op jit(solution)/shard_map/ppermute | solution.py:371
  42.0 1.8 %collective-permute-done.16.refs_3_ = bf16[4,128,256]{2,1,0:T(8,128)(2,1)S(1)} collective-permute-done((bf16[4,128,256]{2,1,0:T(8,128)(2,1)S(1)}, bf16[4,128,256]{2,1,0:T(8,128)(2,1)S(1)}, u32[]{:S(2)}, u32[]{:S(2)}) %collective-permute-start.16) | collective-permute-done | bytes 262176 | tf_op jit(solution)/shard_map/ppermute | solution.py:371
  46.5 2.5 %collective-permute-start.19 = (bf16[256,256]{1,0:T(8,128)(2,1)S(1)}, bf16[256,256]{1,0:T(8,128)(2,1)S(1)}, u32[]{:S(2)}, u32[]{:S(2)}) collective-permute-start(bf16[256,256]{1,0:T(8,128)(2,1)S(1)} %get-tuple-element.69.refs_0_), channel_id=1, source_target_pairs={{0,2},{1,3},{2,0},{3,1},{4,6},{5,7},{6,4},{7,5},{8,10},{9,11},{10,... | collective-permute-start | bytes 393224 | tf_op jit(solution)/shard_map/ppermute | solution.py:371
  49.0 1.7 %collective-permute-start.18 = (bf16[256,256]{1,0:T(8,128)(2,1)S(1)}, bf16[256,256]{1,0:T(8,128)(2,1)S(1)}, u32[]{:S(2)}, u32[]{:S(2)}) collective-permute-start(bf16[256,256]{1,0:T(8,128)(2,1)S(1)} %get-tuple-element.69.refs_0_), channel_id=1, source_target_pairs={{0,4},{1,5},{2,6},{3,7},{4,0},{5,1},{6,2},{7,3},{8,12},{9,13},{10,... | collective-permute-start | bytes 393224 | tf_op jit(solution)/shard_map/ppermute | solution.py:371
  51.5 1.9 %collective-permute-done.19.refs_3_ = bf16[256,256]{1,0:T(8,128)(2,1)S(1)} collective-permute-done((bf16[256,256]{1,0:T(8,128)(2,1)S(1)}, bf16[256,256]{1,0:T(8,128)(2,1)S(1)}, u32[]{:S(2)}, u32[]{:S(2)}) %collective-permute-start.19) | collective-permute-done | bytes 131104 | tf_op jit(solution)/shard_map/ppermute | solution.py:371
  54.3 6.1 %collective-permute-done.18.refs_2_ = bf16[256,256]{1,0:T(8,128)(2,1)S(1)} collective-permute-done((bf16[256,256]{1,0:T(8,128)(2,1)S(1)}, bf16[256,256]{1,0:T(8,128)(2,1)S(1)}, u32[]{:S(2)}, u32[]{:S(2)}) %collective-permute-start.18) | collective-permute-done | bytes 131104 | tf_op jit(solution)/shard_map/ppermute | solution.py:371
  62.6 3.5 %shard_map.95 = (f32[4,4,64,256]{3,2,1,0:T(8,128)S(1)}, bf16[4,4,64,256]{3,2,1,0:T(8,128)(2,1)S(1)}, bf16[4,128,256]{2,1,0:T(8,128)(2,1)S(1)}, bf16[4,128,256]{2...) custom-call(s32[2,8]{1,0:T(2,128)S(1)} %bitcast.9, s32[1]{0:T(128)} %bitcast.7.refs_1_, ...), custom_call_target="tpu_custom_call" | custom-call | flops 3221225472 | bytes 16777216 | tf_op jit(solution)/shard_map/pallas_call | solution.py:279
  66.5 2.7 %collective-permute-start.32 = (bf16[4,128,256]{2,1,0:T(8,128)(2,1)S(1)}, bf16[4,128,256]{2,1,0:T(8,128)(2,1)S(1)}, u32[]{:S(2)}, u32[]{:S(2)}) collective-permute-start(bf16[4,128,256]{2,1,0:T(8,128)(2,1)S(1)} %get-tuple-element.88), channel_id=1, source_target_pairs={{0,16},{8,24},{16,0},{24,8},{1,17},{9,25},{17,1},{25,9},{2,18},{10... | collective-permute-start | bytes 786440 | tf_op jit(solution)/shard_map/ppermute | solution.py:371
  69.3 2.1 %collective-permute-start.28 = (bf16[4,64,256]{2,1,0:T(8,128)(2,1)S(1)}, bf16[4,64,256]{2,1,0:T(8,128)(2,1)S(1)}, u32[]{:S(2)}, u32[]{:S(2)}) collective-permute-start(bf16[4,64,256]{2,1,0:T(8,128)(2,1)S(1)} %get-tuple-element.81), channel_id=1, source_target_pairs={{0,2},{1,3},{2,0},{3,1},{4,6},{5,7},{6,4},{7,5},{8,10},{9,11},{10,... | collective-permute-start | bytes 393224 | tf_op jit(solution)/shard_map/ppermute | solution.py:371
  72.9 2.1 %collective-permute-done.28.refs_0_ = bf16[4,64,256]{2,1,0:T(8,128)(2,1)S(1)} collective-permute-done((bf16[4,64,256]{2,1,0:T(8,128)(2,1)S(1)}, bf16[4,64,256]{2,1,0:T(8,128)(2,1)S(1)}, u32[]{:S(2)}, u32[]{:S(2)}) %collective-permute-start.28) | collective-permute-done | bytes 131104 | tf_op jit(solution)/shard_map/ppermute | solution.py:371
  76.3 1.7 %collective-permute-start.29 = (bf16[4,64,256]{2,1,0:T(8,128)(2,1)S(1)}, bf16[4,64,256]{2,1,0:T(8,128)(2,1)S(1)}, u32[]{:S(2)}, u32[]{:S(2)}) collective-permute-start(bf16[4,64,256]{2,1,0:T(8,128)(2,1)S(1)} %get-tuple-element.83.refs_3_.refs_4_), channel_id=1, source_target_pairs={{0,2},{1,3},{2,0},{3,1},{4,6},{5,7},{6,4},{7,5},{8,10},{9,11},{10,... | collective-permute-start | bytes 393224 | tf_op jit(solution)/shard_map/ppermute | solution.py:371
  78.1 2.3 %collective-permute-done.32.refs_2_ = bf16[4,128,256]{2,1,0:T(8,128)(2,1)S(1)} collective-permute-done((bf16[4,128,256]{2,1,0:T(8,128)(2,1)S(1)}, bf16[4,128,256]{2,1,0:T(8,128)(2,1)S(1)}, u32[]{:S(2)}, u32[]{:S(2)}) %collective-permute-start.32) | collective-permute-done | bytes 262176 | tf_op jit(solution)/shard_map/ppermute | solution.py:371
  80.3 1.8 %collective-permute-done.33.refs_3_ = bf16[4,128,256]{2,1,0:T(8,128)(2,1)S(1)} collective-permute-done((bf16[4,128,256]{2,1,0:T(8,128)(2,1)S(1)}, bf16[4,128,256]{2,1,0:T(8,128)(2,1)S(1)}, u32[]{:S(2)}, u32[]{:S(2)}) %collective-permute-start.33) | collective-permute-done | bytes 262176 | tf_op jit(solution)/shard_map/ppermute | solution.py:371
  (68 shorter events, 21.1 us)
Async XLA Ops:
  2.6 19.3 %collective-permute-start.4 = (bf16[528,256]{1,0:T(8,128)(2,1)}, bf16[528,256]{1,0:T(8,128)(2,1)S(1)}, u32[]{:S(2)}, u32[]{:S(2)}) collective-permute-start(bf16[528,256]{1,0:T(8,128)(2,1)} %get-tuple-element.49.refs_12_), channel_id=1, source_target_pairs={{0,16},{8,24},{16,0},{24,8},{1,17},{9,25},{17,1},{25,9},{2,18},{10... | collective-permute-start | bytes 811016 | tf_op jit(solution)/shard_map/ppermute | solution.py:371
  5.6 16.3 %collective-permute-start.3 = (bf16[528,256]{1,0:T(8,128)(2,1)}, bf16[528,256]{1,0:T(8,128)(2,1)S(1)}, u32[]{:S(2)}, u32[]{:S(2)}) collective-permute-start(bf16[528,256]{1,0:T(8,128)(2,1)} %get-tuple-element.49.refs_12_), channel_id=1, source_target_pairs={{0,8},{8,0},{16,24},{24,16},{1,9},{9,1},{17,25},{25,17},{2,10},{10... | collective-permute-start | bytes 811016 | tf_op jit(solution)/shard_map/ppermute | solution.py:371
  7.1 6.9 %collective-permute-start.2 = (bf16[272,256]{1,0:T(8,128)(2,1)}, bf16[272,256]{1,0:T(8,128)(2,1)S(1)}, u32[]{:S(2)}, u32[]{:S(2)}) collective-permute-start(bf16[272,256]{1,0:T(8,128)(2,1)} %get-tuple-element.48.refs_0_), channel_id=1, source_target_pairs={{0,2},{1,3},{2,0},{3,1},{4,6},{5,7},{6,4},{7,5},{8,10},{9,11},{10,... | collective-permute-start | bytes 417800 | tf_op jit(solution)/shard_map/ppermute | solution.py:371
  8.7 13.2 %collective-permute-start.1 = (bf16[272,256]{1,0:T(8,128)(2,1)}, bf16[272,256]{1,0:T(8,128)(2,1)S(1)}, u32[]{:S(2)}, u32[]{:S(2)}) collective-permute-start(bf16[272,256]{1,0:T(8,128)(2,1)} %get-tuple-element.48.refs_0_), channel_id=1, source_target_pairs={{0,4},{1,5},{2,6},{3,7},{4,0},{5,1},{6,2},{7,3},{8,12},{9,13},{10,... | collective-permute-start | bytes 417800 | tf_op jit(solution)/shard_map/ppermute | solution.py:371
  11.3 10.6 %collective-permute-start = (bf16[272,256]{1,0:T(8,128)(2,1)}, bf16[272,256]{1,0:T(8,128)(2,1)S(1)}, u32[]{:S(2)}, u32[]{:S(2)}) collective-permute-start(bf16[272,256]{1,0:T(8,128)(2,1)} %get-tuple-element.48.refs_0_), channel_id=1, source_target_pairs={{0,6},{1,7},{2,4},{3,5},{4,2},{5,3},{6,0},{7,1},{8,14},{9,15},{10,... | collective-permute-start | bytes 417800 | tf_op jit(solution)/shard_map/ppermute | solution.py:371
  14.0 9.1 %collective-permute-start.9 = (bf16[528,256]{1,0:T(8,128)(2,1)}, bf16[528,256]{1,0:T(8,128)(2,1)S(1)}, u32[]{:S(2)}, u32[]{:S(2)}) collective-permute-start(bf16[528,256]{1,0:T(8,128)(2,1)} %get-tuple-element.49.refs_12_), channel_id=1, source_target_pairs={{0,24},{8,16},{16,8},{24,0},{1,25},{9,17},{17,9},{25,1},{2,26},{10... | collective-permute-start | bytes 811016 | tf_op jit(solution)/shard_map/ppermute | solution.py:371
  28.3 11.8 %collective-permute-start.14 = (bf16[4,128,256]{2,1,0:T(8,128)(2,1)S(1)}, bf16[4,128,256]{2,1,0:T(8,128)(2,1)S(1)}, u32[]{:S(2)}, u32[]{:S(2)}) collective-permute-start(bf16[4,128,256]{2,1,0:T(8,128)(2,1)S(1)} %get-tuple-element.64), channel_id=1, source_target_pairs={{0,8},{8,0},{16,24},{24,16},{1,9},{9,1},{17,25},{25,17},{2,10},{10... | collective-permute-start | bytes 786440 | tf_op jit(solution)/shard_map/ppermute | solution.py:371
  28.3 13.7 %collective-permute-start.15 = (bf16[4,128,256]{2,1,0:T(8,128)(2,1)S(1)}, bf16[4,128,256]{2,1,0:T(8,128)(2,1)S(1)}, u32[]{:S(2)}, u32[]{:S(2)}) collective-permute-start(bf16[4,128,256]{2,1,0:T(8,128)(2,1)S(1)} %get-tuple-element.65), channel_id=1, source_target_pairs={{0,16},{8,24},{16,0},{24,8},{1,17},{9,25},{17,1},{25,9},{2,18},{10... | collective-permute-start | bytes 786440 | tf_op jit(solution)/shard_map/ppermute | solution.py:371
  30.6 6.1 %collective-permute-start.11 = (bf16[4,64,256]{2,1,0:T(8,128)(2,1)S(1)}, bf16[4,64,256]{2,1,0:T(8,128)(2,1)S(1)}, u32[]{:S(2)}, u32[]{:S(2)}) collective-permute-start(bf16[4,64,256]{2,1,0:T(8,128)(2,1)S(1)} %get-tuple-element.59), channel_id=1, source_target_pairs={{0,2},{1,3},{2,0},{3,1},{4,6},{5,7},{6,4},{7,5},{8,10},{9,11},{10,... | collective-permute-start | bytes 393224 | tf_op jit(solution)/shard_map/ppermute | solution.py:371
  33.1 10.7 %collective-permute-start.16 = (bf16[4,128,256]{2,1,0:T(8,128)(2,1)S(1)}, bf16[4,128,256]{2,1,0:T(8,128)(2,1)S(1)}, u32[]{:S(2)}, u32[]{:S(2)}) collective-permute-start(bf16[4,128,256]{2,1,0:T(8,128)(2,1)S(1)} %get-tuple-element.66), channel_id=1, source_target_pairs={{0,24},{8,16},{16,8},{24,0},{1,25},{9,17},{17,9},{25,1},{2,26},{10... | collective-permute-start | bytes 786440 | tf_op jit(solution)/shard_map/ppermute | solution.py:371
  36.7 9.7 %collective-permute-start.13 = (bf16[4,64,256]{2,1,0:T(8,128)(2,1)S(1)}, bf16[4,64,256]{2,1,0:T(8,128)(2,1)S(1)}, u32[]{:S(2)}, u32[]{:S(2)}) collective-permute-start(bf16[4,64,256]{2,1,0:T(8,128)(2,1)S(1)} %get-tuple-element.62), channel_id=1, source_target_pairs={{0,4},{1,5},{2,6},{3,7},{4,0},{5,1},{6,2},{7,3},{8,12},{9,13},{10,... | collective-permute-start | bytes 393224 | tf_op jit(solution)/shard_map/ppermute | solution.py:371
  38.4 8.0 %collective-permute-start.12 = (bf16[4,64,256]{2,1,0:T(8,128)(2,1)S(1)}, bf16[4,64,256]{2,1,0:T(8,128)(2,1)S(1)}, u32[]{:S(2)}, u32[]{:S(2)}) collective-permute-start(bf16[4,64,256]{2,1,0:T(8,128)(2,1)S(1)} %get-tuple-element.61.refs_4_), channel_id=1, source_target_pairs={{0,2},{1,3},{2,0},{3,1},{4,6},{5,7},{6,4},{7,5},{8,10},{9,11},{10,... | collective-permute-start | bytes 393224 | tf_op jit(solution)/shard_map/ppermute | solution.py:371
  44.0 16.4 %collective-permute-start.21 = (bf16[512,256]{1,0:T(8,128)(2,1)S(1)}, bf16[512,256]{1,0:T(8,128)(2,1)S(1)}, u32[]{:S(2)}, u32[]{:S(2)}) collective-permute-start(bf16[512,256]{1,0:T(8,128)(2,1)S(1)} %get-tuple-element.67.refs_3_.refs_12_), channel_id=1, source_target_pairs={{0,16},{8,24},{16,0},{24,8},{1,17},{9,25},{17,1},{25,9},{2,18},{10... | collective-permute-start | bytes 786440 | tf_op jit(solution)/shard_map/ppermute | solution.py:371
  44.7 15.7 %collective-permute-start.20 = (bf16[512,256]{1,0:T(8,128)(2,1)S(1)}, bf16[512,256]{1,0:T(8,128)(2,1)S(1)}, u32[]{:S(2)}, u32[]{:S(2)}) collective-permute-start(bf16[512,256]{1,0:T(8,128)(2,1)S(1)} %get-tuple-element.67.refs_3_.refs_12_), channel_id=1, source_target_pairs={{0,8},{8,0},{16,24},{24,16},{1,9},{9,1},{17,25},{25,17},{2,10},{10... | collective-permute-start | bytes 786440 | tf_op jit(solution)/shard_map/ppermute | solution.py:371
  46.5 6.9 %collective-permute-start.19 = (bf16[256,256]{1,0:T(8,128)(2,1)S(1)}, bf16[256,256]{1,0:T(8,128)(2,1)S(1)}, u32[]{:S(2)}, u32[]{:S(2)}) collective-permute-start(bf16[256,256]{1,0:T(8,128)(2,1)S(1)} %get-tuple-element.69.refs_0_), channel_id=1, source_target_pairs={{0,2},{1,3},{2,0},{3,1},{4,6},{5,7},{6,4},{7,5},{8,10},{9,11},{10,... | collective-permute-start | bytes 393224 | tf_op jit(solution)/shard_map/ppermute | solution.py:371
  49.0 11.4 %collective-permute-start.18 = (bf16[256,256]{1,0:T(8,128)(2,1)S(1)}, bf16[256,256]{1,0:T(8,128)(2,1)S(1)}, u32[]{:S(2)}, u32[]{:S(2)}) collective-permute-start(bf16[256,256]{1,0:T(8,128)(2,1)S(1)} %get-tuple-element.69.refs_0_), channel_id=1, source_target_pairs={{0,4},{1,5},{2,6},{3,7},{4,0},{5,1},{6,2},{7,3},{8,12},{9,13},{10,... | collective-permute-start | bytes 393224 | tf_op jit(solution)/shard_map/ppermute | solution.py:371
  50.7 9.7 %collective-permute-start.17 = (bf16[256,256]{1,0:T(8,128)(2,1)S(1)}, bf16[256,256]{1,0:T(8,128)(2,1)S(1)}, u32[]{:S(2)}, u32[]{:S(2)}) collective-permute-start(bf16[256,256]{1,0:T(8,128)(2,1)S(1)} %get-tuple-element.69.refs_0_), channel_id=1, source_target_pairs={{0,6},{1,7},{2,4},{3,5},{4,2},{5,3},{6,0},{7,1},{8,14},{9,15},{10,... | collective-permute-start | bytes 393224 | tf_op jit(solution)/shard_map/ppermute | solution.py:371
  53.4 8.2 %collective-permute-start.26 = (bf16[512,256]{1,0:T(8,128)(2,1)S(1)}, bf16[512,256]{1,0:T(8,128)(2,1)S(1)}, u32[]{:S(2)}, u32[]{:S(2)}) collective-permute-start(bf16[512,256]{1,0:T(8,128)(2,1)S(1)} %get-tuple-element.67.refs_3_.refs_12_), channel_id=1, source_target_pairs={{0,24},{8,16},{16,8},{24,0},{1,25},{9,17},{17,9},{25,1},{2,26},{10... | collective-permute-start | bytes 786440 | tf_op jit(solution)/shard_map/ppermute | solution.py:371
  66.5 11.6 %collective-permute-start.31 = (bf16[4,128,256]{2,1,0:T(8,128)(2,1)S(1)}, bf16[4,128,256]{2,1,0:T(8,128)(2,1)S(1)}, u32[]{:S(2)}, u32[]{:S(2)}) collective-permute-start(bf16[4,128,256]{2,1,0:T(8,128)(2,1)S(1)} %get-tuple-element.87), channel_id=1, source_target_pairs={{0,8},{8,0},{16,24},{24,16},{1,9},{9,1},{17,25},{25,17},{2,10},{10... | collective-permute-start | bytes 786440 | tf_op jit(solution)/shard_map/ppermute | solution.py:371
  66.5 13.9 %collective-permute-start.32 = (bf16[4,128,256]{2,1,0:T(8,128)(2,1)S(1)}, bf16[4,128,256]{2,1,0:T(8,128)(2,1)S(1)}, u32[]{:S(2)}, u32[]{:S(2)}) collective-permute-start(bf16[4,128,256]{2,1,0:T(8,128)(2,1)S(1)} %get-tuple-element.88), channel_id=1, source_target_pairs={{0,16},{8,24},{16,0},{24,8},{1,17},{9,25},{17,1},{25,9},{2,18},{10... | collective-permute-start | bytes 786440 | tf_op jit(solution)/shard_map/ppermute | solution.py:371
  69.3 5.7 %collective-permute-start.28 = (bf16[4,64,256]{2,1,0:T(8,128)(2,1)S(1)}, bf16[4,64,256]{2,1,0:T(8,128)(2,1)S(1)}, u32[]{:S(2)}, u32[]{:S(2)}) collective-permute-start(bf16[4,64,256]{2,1,0:T(8,128)(2,1)S(1)} %get-tuple-element.81), channel_id=1, source_target_pairs={{0,2},{1,3},{2,0},{3,1},{4,6},{5,7},{6,4},{7,5},{8,10},{9,11},{10,... | collective-permute-start | bytes 393224 | tf_op jit(solution)/shard_map/ppermute | solution.py:371
  71.4 10.7 %collective-permute-start.33 = (bf16[4,128,256]{2,1,0:T(8,128)(2,1)S(1)}, bf16[4,128,256]{2,1,0:T(8,128)(2,1)S(1)}, u32[]{:S(2)}, u32[]{:S(2)}) collective-permute-start(bf16[4,128,256]{2,1,0:T(8,128)(2,1)S(1)} %get-tuple-element.89), channel_id=1, source_target_pairs={{0,24},{8,16},{16,8},{24,0},{1,25},{9,17},{17,9},{25,1},{2,26},{10... | collective-permute-start | bytes 786440 | tf_op jit(solution)/shard_map/ppermute | solution.py:371
  75.0 8.5 %collective-permute-start.30 = (bf16[4,64,256]{2,1,0:T(8,128)(2,1)S(1)}, bf16[4,64,256]{2,1,0:T(8,128)(2,1)S(1)}, u32[]{:S(2)}, u32[]{:S(2)}) collective-permute-start(bf16[4,64,256]{2,1,0:T(8,128)(2,1)S(1)} %get-tuple-element.84), channel_id=1, source_target_pairs={{0,4},{1,5},{2,6},{3,7},{4,0},{5,1},{6,2},{7,3},{8,12},{9,13},{10,... | collective-permute-start | bytes 393224 | tf_op jit(solution)/shard_map/ppermute | solution.py:371
  76.3 7.2 %collective-permute-start.29 = (bf16[4,64,256]{2,1,0:T(8,128)(2,1)S(1)}, bf16[4,64,256]{2,1,0:T(8,128)(2,1)S(1)}, u32[]{:S(2)}, u32[]{:S(2)}) collective-permute-start(bf16[4,64,256]{2,1,0:T(8,128)(2,1)S(1)} %get-tuple-element.83.refs_3_.refs_4_), channel_id=1, source_target_pairs={{0,2},{1,3},{2,0},{3,1},{4,6},{5,7},{6,4},{7,5},{8,10},{9,11},{10,... | collective-permute-start | bytes 393224 | tf_op jit(solution)/shard_map/ppermute | solution.py:371
  (15 other events, 123.5 us)

commit v7 on v5

--- a/solution.py
+++ b/solution.py
@@ -190,7 +190,7 @@
         for b in range(col_blocks):
             right[b] = jnp.broadcast_to(col_table[b : b + 1, :], right.shape[1:])
 
-    chunks = [slice(at, at + 256) for at in range(0, size, 256)]
+    chunks = [slice(at, at + 128) for at in range(0, size, 128)]
 
     def place(slot):
         return listing[0, slot] - row_zero, listing[1, slot] - col_zero

time: 86.3 us -> 86.2 us (level); the launches traced: 86.2 us -> 87.8 us
  starting transfers between devices: 46.8 us -> 50.3 us
  waiting for transfers between devices: 26.7 us -> 24.8 us
    ppermute x33, starting transfers between devices: 46.8 us -> 50.3 us  [send(): return lax.ppermute(x, axis, [(k, k ^ mask) for k in range(count)])]
    ppermute x33, waiting for transfers between devices: 26.7 us -> 24.8 us  [send(): return lax.ppermute(x, axis, [(k, k ^ mask) for k in range(count)])]
  transfers between devices with their start and end apart: 33 -> 33, of which waited for: 14 -> 13; matrix products, arithmetic and copies ran while one was open for 0% -> 0% of each run, Pallas kernels for 4% -> 4%
where the time goes in v7:
time: 86.2 us; the launch traced here: 87.8 us
  starting transfers between devices  50.3 us (58%)
  waiting for transfers between devices  24.8 us (29%)
  Pallas kernels  11.2 us (13%)
  between operations  1.49 us (2%)
    ppermute x33, starting transfers between devices, send(): return lax.ppermute(x, axis, [(k, k ^ mask) for k in range(count)])  50.3 us
    ppermute x33, waiting for transfers between devices, send(): return lax.ppermute(x, axis, [(k, k ^ mask) for k in range(count)])  24.8 us
    pallas_call x2, Pallas kernels, work(): pl.pallas_call(functools.partial(work_kernel, first, len(row_in), n_row,...  5.21 us
    pallas_call x4, Pallas kernels, update(): pl.pallas_call(functools.partial(update_kernel, len(parts), len(outs)), o...  1.98 us
    pallas_call x1, Pallas kernels, pack(): pl.pallas_call(pack_kernel, out_shape=[shape((e.shape[0] * e.shape[1] + M...  1.93 us
  transfers between devices with their start and end apart: 33, of which 13 were waited for; matrix products, arithmetic and copies ran while one was open for 0% of the time, Pallas kernels for 4%

profile of v7, /device:TPU:0, one launch (start us, length us, event | category | flops | bytes accessed | tf_op | source)
XLA Modules:
  0.0 87.8 jit_solution(1429918669001353616)
XLA Ops:
  0.6 1.9 %shard_map.87 = (bf16[272,256]{1,0:T(8,128)(2,1)}, bf16[528,256]{1,0:T(8,128)(2,1)}) custom-call(f32[4,64,256]{2,1,0:T(8,128)} %emb.3, bf16[4,64]{1,0:T(4,128)(2,1)} %row_marg.1, f32[4,128,256]{2,1,0:T(8,128)} %emb.2, bf16[4,128]{1,0:T(4,128)(2,1)} %col_marg.1), custom_call_target="tpu_custom_call" | custom-call | bytes 1048576 | tf_op jit(solution)/shard_map/pallas_call | solution.py:50
  2.6 4.1 %collective-permute-start.1 = (bf16[272,256]{1,0:T(8,128)(2,1)}, bf16[272,256]{1,0:T(8,128)(2,1)S(1)}, u32[]{:S(2)}, u32[]{:S(2)}) collective-permute-start(bf16[272,256]{1,0:T(8,128)(2,1)} %get-tuple-element.47.refs_0_), channel_id=1, source_target_pairs={{0,4},{1,5},{2,6},{3,7},{4,0},{5,1},{6,2},{7,3},{8,12},{9,13},{10,... | collective-permute-start | bytes 417800 | tf_op jit(solution)/shard_map/ppermute | solution.py:371
  14.5 2.4 %collective-permute-start.9 = (bf16[528,256]{1,0:T(8,128)(2,1)S(1)}, bf16[528,256]{1,0:T(8,128)(2,1)S(1)}, u32[]{:S(2)}, u32[]{:S(2)}) collective-permute-start(bf16[528,256]{1,0:T(8,128)(2,1)S(1)} %copy-done.2), channel_id=1, source_target_pairs={{0,24},{8,16},{16,8},{24,0},{1,25},{9,17},{17,9},{25,1},{2,26},{10... | collective-permute-start | bytes 811016 | tf_op jit(solution)/shard_map/ppermute | solution.py:371
  17.0 2.3 %collective-permute-done.2.refs_3_ = bf16[1,272,256]{2,1,0:T(8,128)(2,1)S(1)} collective-permute-done((bf16[1,272,256]{2,1,0:T(8,128)(2,1)S(1)}, bf16[1,272,256]{2,1,0:T(8,128)(2,1)S(1)}, u32[]{:S(2)}, u32[]{:S(2)}) %collective-permute-start.2) | collective-permute-done | bytes 139296 | tf_op jit(solution)/shard_map/ppermute | solution.py:371
  20.4 3.1 %collective-permute-done.9.refs_15_ = bf16[528,256]{1,0:T(8,128)(2,1)S(1)} collective-permute-done((bf16[528,256]{1,0:T(8,128)(2,1)S(1)}, bf16[528,256]{1,0:T(8,128)(2,1)S(1)}, u32[]{:S(2)}, u32[]{:S(2)}) %collective-permute-start.9) | collective-permute-done | bytes 270368 | tf_op jit(solution)/shard_map/ppermute | solution.py:371
  23.6 2.7 %shard_map.90 = (f32[4,4,64,256]{3,2,1,0:T(8,128)S(1)}, bf16[4,4,64,256]{3,2,1,0:T(8,128)(2,1)S(1)}, bf16[4,128,256]{2,1,0:T(8,128)(2,1)S(1)}, bf16[4,128,256]{2...) custom-call(s32[2,8]{1,0:T(2,128)S(1)} %bitcast.8, ...), custom_call_target="tpu_custom_call" | custom-call | flops 3221225472 | bytes 16777216 | tf_op jit(solution)/shard_map/pallas_call | solution.py:279
  28.0 2.3 %collective-permute-start.15 = (bf16[4,128,256]{2,1,0:T(8,128)(2,1)S(1)}, bf16[4,128,256]{2,1,0:T(8,128)(2,1)S(1)}, u32[]{:S(2)}, u32[]{:S(2)}) collective-permute-start(bf16[4,128,256]{2,1,0:T(8,128)(2,1)S(1)} %get-tuple-element.64), channel_id=1, source_target_pairs={{0,16},{8,24},{16,0},{24,8},{1,17},{9,25},{17,1},{25,9},{2,18},{10... | collective-permute-start | bytes 786440 | tf_op jit(solution)/shard_map/ppermute | solution.py:371
  31.0 2.4 %collective-permute-start.11 = (bf16[4,64,256]{2,1,0:T(8,128)(2,1)S(1)}, bf16[4,64,256]{2,1,0:T(8,128)(2,1)S(1)}, u32[]{:S(2)}, u32[]{:S(2)}) collective-permute-start(bf16[4,64,256]{2,1,0:T(8,128)(2,1)S(1)} %get-tuple-element.58), channel_id=1, source_target_pairs={{0,2},{1,3},{2,0},{3,1},{4,6},{5,7},{6,4},{7,5},{8,10},{9,11},{10,... | collective-permute-start | bytes 393224 | tf_op jit(solution)/shard_map/ppermute | solution.py:371
  33.4 3.5 %collective-permute-done.11.refs_0_ = bf16[4,64,256]{2,1,0:T(8,128)(2,1)S(1)} collective-permute-done((bf16[4,64,256]{2,1,0:T(8,128)(2,1)S(1)}, bf16[4,64,256]{2,1,0:T(8,128)(2,1)S(1)}, u32[]{:S(2)}, u32[]{:S(2)}) %collective-permute-start.11) | collective-permute-done | bytes 131104 | tf_op jit(solution)/shard_map/ppermute | solution.py:371
  37.0 4.7 %collective-permute-start.13 = (bf16[4,64,256]{2,1,0:T(8,128)(2,1)S(1)}, bf16[4,64,256]{2,1,0:T(8,128)(2,1)S(1)}, u32[]{:S(2)}, u32[]{:S(2)}) collective-permute-start(bf16[4,64,256]{2,1,0:T(8,128)(2,1)S(1)} %get-tuple-element.61), channel_id=1, source_target_pairs={{0,4},{1,5},{2,6},{3,7},{4,0},{5,1},{6,2},{7,3},{8,12},{9,13},{10,... | collective-permute-start | bytes 393224 | tf_op jit(solution)/shard_map/ppermute | solution.py:371
  41.6 1.7 %collective-permute-start.12 = (bf16[4,64,256]{2,1,0:T(8,128)(2,1)S(1)}, bf16[4,64,256]{2,1,0:T(8,128)(2,1)S(1)}, u32[]{:S(2)}, u32[]{:S(2)}) collective-permute-start(bf16[4,64,256]{2,1,0:T(8,128)(2,1)S(1)} %get-tuple-element.60.refs_4_), channel_id=1, source_target_pairs={{0,2},{1,3},{2,0},{3,1},{4,6},{5,7},{6,4},{7,5},{8,10},{9,11},{10,... | collective-permute-start | bytes 393224 | tf_op jit(solution)/shard_map/ppermute | solution.py:371
  43.6 2.7 %collective-permute-start.19 = (bf16[512,256]{1,0:T(8,128)(2,1)S(1)}, bf16[512,256]{1,0:T(8,128)(2,1)S(1)}, u32[]{:S(2)}, u32[]{:S(2)}) collective-permute-start(bf16[512,256]{1,0:T(8,128)(2,1)S(1)} %get-tuple-element.66.refs_3_.refs_10_), channel_id=1, source_target_pairs={{0,24},{8,16},{16,8},{24,0},{1,25},{9,17},{17,9},{25,1},{2,26},{10... | collective-permute-start | bytes 786440 | tf_op jit(solution)/shard_map/ppermute | solution.py:371
  47.5 2.5 %collective-permute-start.18 = (bf16[256,256]{1,0:T(8,128)(2,1)S(1)}, bf16[256,256]{1,0:T(8,128)(2,1)S(1)}, u32[]{:S(2)}, u32[]{:S(2)}) collective-permute-start(bf16[256,256]{1,0:T(8,128)(2,1)S(1)} %get-tuple-element.68.refs_0_), channel_id=1, source_target_pairs={{0,4},{1,5},{2,6},{3,7},{4,0},{5,1},{6,2},{7,3},{8,12},{9,13},{10,... | collective-permute-start | bytes 393224 | tf_op jit(solution)/shard_map/ppermute | solution.py:371
  50.0 1.9 %collective-permute-start.17 = (bf16[256,256]{1,0:T(8,128)(2,1)S(1)}, bf16[256,256]{1,0:T(8,128)(2,1)S(1)}, u32[]{:S(2)}, u32[]{:S(2)}) collective-permute-start(bf16[256,256]{1,0:T(8,128)(2,1)S(1)} %get-tuple-element.68.refs_0_), channel_id=1, source_target_pairs={{0,2},{1,3},{2,0},{3,1},{4,6},{5,7},{6,4},{7,5},{8,10},{9,11},{10,... | collective-permute-start | bytes 393224 | tf_op jit(solution)/shard_map/ppermute | solution.py:371
  52.0 3.7 %collective-permute-done.18.refs_0_ = bf16[256,256]{1,0:T(8,128)(2,1)S(1)} collective-permute-done((bf16[256,256]{1,0:T(8,128)(2,1)S(1)}, bf16[256,256]{1,0:T(8,128)(2,1)S(1)}, u32[]{:S(2)}, u32[]{:S(2)}) %collective-permute-start.18) | collective-permute-done | bytes 131104 | tf_op jit(solution)/shard_map/ppermute | solution.py:371
  58.5 2.2 %collective-permute-done.20.refs_3_ = bf16[1,256,256]{2,1,0:T(8,128)(2,1)S(1)} collective-permute-done((bf16[1,256,256]{2,1,0:T(8,128)(2,1)S(1)}, bf16[1,256,256]{2,1,0:T(8,128)(2,1)S(1)}, u32[]{:S(2)}, u32[]{:S(2)}) %collective-permute-start.20) | collective-permute-done | bytes 131104 | tf_op jit(solution)/shard_map/ppermute | solution.py:371
  61.4 1.7 %collective-permute-done.25.refs_12_ = bf16[512,256]{1,0:T(8,128)(2,1)S(1)} collective-permute-done((bf16[512,256]{1,0:T(8,128)(2,1)S(1)}, bf16[512,256]{1,0:T(8,128)(2,1)S(1)}, u32[]{:S(2)}, u32[]{:S(2)}) %collective-permute-start.25) | collective-permute-done | bytes 262176 | tf_op jit(solution)/shard_map/ppermute | solution.py:371
  64.3 2.5 %shard_map.97 = (f32[4,4,64,256]{3,2,1,0:T(8,128)S(1)}, bf16[4,4,64,256]{3,2,1,0:T(8,128)(2,1)S(1)}, bf16[4,128,256]{2,1,0:T(8,128)(2,1)S(1)}, bf16[4,128,256]{2...) custom-call(s32[2,8]{1,0:T(2,128)S(1)} %bitcast.9, s32[1]{0:T(128)} %bitcast.7.refs_1_, ...), custom_call_target="tpu_custom_call" | custom-call | flops 3221225472 | bytes 16777216 | tf_op jit(solution)/shard_map/pallas_call | solution.py:279
  67.5 2.3 %collective-permute-start.31 = (bf16[4,128,256]{2,1,0:T(8,128)(2,1)S(1)}, bf16[4,128,256]{2,1,0:T(8,128)(2,1)S(1)}, u32[]{:S(2)}, u32[]{:S(2)}) collective-permute-start(bf16[4,128,256]{2,1,0:T(8,128)(2,1)S(1)} %get-tuple-element.86), channel_id=1, source_target_pairs={{0,16},{8,24},{16,0},{24,8},{1,17},{9,25},{17,1},{25,9},{2,18},{10... | collective-permute-start | bytes 786440 | tf_op jit(solution)/shard_map/ppermute | solution.py:371
  69.9 3.8 %collective-permute-start.27 = (bf16[4,64,256]{2,1,0:T(8,128)(2,1)S(1)}, bf16[4,64,256]{2,1,0:T(8,128)(2,1)S(1)}, u32[]{:S(2)}, u32[]{:S(2)}) collective-permute-start(bf16[4,64,256]{2,1,0:T(8,128)(2,1)S(1)} %get-tuple-element.79), channel_id=1, source_target_pairs={{0,2},{1,3},{2,0},{3,1},{4,6},{5,7},{6,4},{7,5},{8,10},{9,11},{10,... | collective-permute-start | bytes 393224 | tf_op jit(solution)/shard_map/ppermute | solution.py:371
  75.0 2.3 %collective-permute-done.27.refs_0_ = bf16[4,64,256]{2,1,0:T(8,128)(2,1)S(1)} collective-permute-done((bf16[4,64,256]{2,1,0:T(8,128)(2,1)S(1)}, bf16[4,64,256]{2,1,0:T(8,128)(2,1)S(1)}, u32[]{:S(2)}, u32[]{:S(2)}) %collective-permute-start.27) | collective-permute-done | bytes 131104 | tf_op jit(solution)/shard_map/ppermute | solution.py:371
  77.3 3.4 %collective-permute-start.29 = (bf16[4,64,256]{2,1,0:T(8,128)(2,1)S(1)}, bf16[4,64,256]{2,1,0:T(8,128)(2,1)S(1)}, u32[]{:S(2)}, u32[]{:S(2)}) collective-permute-start(bf16[4,64,256]{2,1,0:T(8,128)(2,1)S(1)} %get-tuple-element.82), channel_id=1, source_target_pairs={{0,4},{1,5},{2,6},{3,7},{4,0},{5,1},{6,2},{7,3},{8,12},{9,13},{10,... | collective-permute-start | bytes 393224 | tf_op jit(solution)/shard_map/ppermute | solution.py:371
  80.7 1.7 %collective-permute-start.28 = (bf16[4,64,256]{2,1,0:T(8,128)(2,1)S(1)}, bf16[4,64,256]{2,1,0:T(8,128)(2,1)S(1)}, u32[]{:S(2)}, u32[]{:S(2)}) collective-permute-start(bf16[4,64,256]{2,1,0:T(8,128)(2,1)S(1)} %get-tuple-element.81.refs_3_.refs_4_), channel_id=1, source_target_pairs={{0,2},{1,3},{2,0},{3,1},{4,6},{5,7},{6,4},{7,5},{8,10},{9,11},{10,... | collective-permute-start | bytes 393224 | tf_op jit(solution)/shard_map/ppermute | solution.py:371
  84.1 2.5 %collective-permute-done.29.refs_2_ = bf16[4,64,256]{2,1,0:T(8,128)(2,1)S(1)} collective-permute-done((bf16[4,64,256]{2,1,0:T(8,128)(2,1)S(1)}, bf16[4,64,256]{2,1,0:T(8,128)(2,1)S(1)}, u32[]{:S(2)}, u32[]{:S(2)}) %collective-permute-start.29) | collective-permute-done | bytes 131104 | tf_op jit(solution)/shard_map/ppermute | solution.py:371
  (68 shorter events, 21.8 us)
Async XLA Ops:
  2.6 11.1 %collective-permute-start.1 = (bf16[272,256]{1,0:T(8,128)(2,1)}, bf16[272,256]{1,0:T(8,128)(2,1)S(1)}, u32[]{:S(2)}, u32[]{:S(2)}) collective-permute-start(bf16[272,256]{1,0:T(8,128)(2,1)} %get-tuple-element.47.refs_0_), channel_id=1, source_target_pairs={{0,4},{1,5},{2,6},{3,7},{4,0},{5,1},{6,2},{7,3},{8,12},{9,13},{10,... | collective-permute-start | bytes 417800 | tf_op jit(solution)/shard_map/ppermute | solution.py:371
  6.7 10.3 %collective-permute-start.4 = (bf16[528,256]{1,0:T(8,128)(2,1)}, bf16[528,256]{1,0:T(8,128)(2,1)S(1)}, u32[]{:S(2)}, u32[]{:S(2)}) collective-permute-start(bf16[528,256]{1,0:T(8,128)(2,1)} %get-tuple-element.49.refs_12_), channel_id=1, source_target_pairs={{0,16},{8,24},{16,0},{24,8},{1,17},{9,25},{17,1},{25,9},{2,18},{10... | collective-permute-start | bytes 811016 | tf_op jit(solution)/shard_map/ppermute | solution.py:371
  8.2 8.8 %collective-permute-start.3 = (bf16[528,256]{1,0:T(8,128)(2,1)}, bf16[528,256]{1,0:T(8,128)(2,1)S(1)}, u32[]{:S(2)}, u32[]{:S(2)}) collective-permute-start(bf16[528,256]{1,0:T(8,128)(2,1)} %get-tuple-element.49.refs_12_), channel_id=1, source_target_pairs={{0,8},{8,0},{16,24},{24,16},{1,9},{9,1},{17,25},{25,17},{2,10},{10... | collective-permute-start | bytes 811016 | tf_op jit(solution)/shard_map/ppermute | solution.py:371
  9.7 7.3 %collective-permute-start = (bf16[272,256]{1,0:T(8,128)(2,1)}, bf16[272,256]{1,0:T(8,128)(2,1)S(1)}, u32[]{:S(2)}, u32[]{:S(2)}) collective-permute-start(bf16[272,256]{1,0:T(8,128)(2,1)} %get-tuple-element.47.refs_0_), channel_id=1, source_target_pairs={{0,2},{1,3},{2,0},{3,1},{4,6},{5,7},{6,4},{7,5},{8,10},{9,11},{10,... | collective-permute-start | bytes 417800 | tf_op jit(solution)/shard_map/ppermute | solution.py:371
  13.7 5.6 %collective-permute-start.2 = (bf16[1,272,256]{2,1,0:T(8,128)(2,1)S(1)}, bf16[1,272,256]{2,1,0:T(8,128)(2,1)S(1)}, u32[]{:S(2)}, u32[]{:S(2)}) collective-permute-start(bf16[1,272,256]{2,1,0:T(8,128)(2,1)S(1)} %shard_map.88.refs_2_), channel_id=1, source_target_pairs={{0,2},{1,3},{2,0},{3,1},{4,6},{5,7},{6,4},{7,5},{8,10},{9,11},{10,... | collective-permute-start | bytes 417800 | tf_op jit(solution)/shard_map/ppermute | solution.py:371
  14.5 9.0 %collective-permute-start.9 = (bf16[528,256]{1,0:T(8,128)(2,1)S(1)}, bf16[528,256]{1,0:T(8,128)(2,1)S(1)}, u32[]{:S(2)}, u32[]{:S(2)}) collective-permute-start(bf16[528,256]{1,0:T(8,128)(2,1)S(1)} %copy-done.2), channel_id=1, source_target_pairs={{0,24},{8,16},{16,8},{24,0},{1,25},{9,17},{17,9},{25,1},{2,26},{10... | collective-permute-start | bytes 811016 | tf_op jit(solution)/shard_map/ppermute | solution.py:371
  26.4 17.0 %collective-permute-start.14 = (bf16[4,128,256]{2,1,0:T(8,128)(2,1)S(1)}, bf16[4,128,256]{2,1,0:T(8,128)(2,1)S(1)}, u32[]{:S(2)}, u32[]{:S(2)}) collective-permute-start(bf16[4,128,256]{2,1,0:T(8,128)(2,1)S(1)} %get-tuple-element.63), channel_id=1, source_target_pairs={{0,8},{8,0},{16,24},{24,16},{1,9},{9,1},{17,25},{25,17},{2,10},{10... | collective-permute-start | bytes 786440 | tf_op jit(solution)/shard_map/ppermute | solution.py:371
  28.0 15.4 %collective-permute-start.15 = (bf16[4,128,256]{2,1,0:T(8,128)(2,1)S(1)}, bf16[4,128,256]{2,1,0:T(8,128)(2,1)S(1)}, u32[]{:S(2)}, u32[]{:S(2)}) collective-permute-start(bf16[4,128,256]{2,1,0:T(8,128)(2,1)S(1)} %get-tuple-element.64), channel_id=1, source_target_pairs={{0,16},{8,24},{16,0},{24,8},{1,17},{9,25},{17,1},{25,9},{2,18},{10... | collective-permute-start | bytes 786440 | tf_op jit(solution)/shard_map/ppermute | solution.py:371
  30.3 13.1 %collective-permute-start.16 = (bf16[4,128,256]{2,1,0:T(8,128)(2,1)S(1)}, bf16[4,128,256]{2,1,0:T(8,128)(2,1)S(1)}, u32[]{:S(2)}, u32[]{:S(2)}) collective-permute-start(bf16[4,128,256]{2,1,0:T(8,128)(2,1)S(1)} %get-tuple-element.65), channel_id=1, source_target_pairs={{0,24},{8,16},{16,8},{24,0},{1,25},{9,17},{17,9},{25,1},{2,26},{10... | collective-permute-start | bytes 786440 | tf_op jit(solution)/shard_map/ppermute | solution.py:371
  31.0 6.0 %collective-permute-start.11 = (bf16[4,64,256]{2,1,0:T(8,128)(2,1)S(1)}, bf16[4,64,256]{2,1,0:T(8,128)(2,1)S(1)}, u32[]{:S(2)}, u32[]{:S(2)}) collective-permute-start(bf16[4,64,256]{2,1,0:T(8,128)(2,1)S(1)} %get-tuple-element.58), channel_id=1, source_target_pairs={{0,2},{1,3},{2,0},{3,1},{4,6},{5,7},{6,4},{7,5},{8,10},{9,11},{10,... | collective-permute-start | bytes 393224 | tf_op jit(solution)/shard_map/ppermute | solution.py:371
  37.0 10.1 %collective-permute-start.13 = (bf16[4,64,256]{2,1,0:T(8,128)(2,1)S(1)}, bf16[4,64,256]{2,1,0:T(8,128)(2,1)S(1)}, u32[]{:S(2)}, u32[]{:S(2)}) collective-permute-start(bf16[4,64,256]{2,1,0:T(8,128)(2,1)S(1)} %get-tuple-element.61), channel_id=1, source_target_pairs={{0,4},{1,5},{2,6},{3,7},{4,0},{5,1},{6,2},{7,3},{8,12},{9,13},{10,... | collective-permute-start | bytes 393224 | tf_op jit(solution)/shard_map/ppermute | solution.py:371
  41.6 5.8 %collective-permute-start.12 = (bf16[4,64,256]{2,1,0:T(8,128)(2,1)S(1)}, bf16[4,64,256]{2,1,0:T(8,128)(2,1)S(1)}, u32[]{:S(2)}, u32[]{:S(2)}) collective-permute-start(bf16[4,64,256]{2,1,0:T(8,128)(2,1)S(1)} %get-tuple-element.60.refs_4_), channel_id=1, source_target_pairs={{0,2},{1,3},{2,0},{3,1},{4,6},{5,7},{6,4},{7,5},{8,10},{9,11},{10,... | collective-permute-start | bytes 393224 | tf_op jit(solution)/shard_map/ppermute | solution.py:371
  43.6 12.0 %collective-permute-start.19 = (bf16[512,256]{1,0:T(8,128)(2,1)S(1)}, bf16[512,256]{1,0:T(8,128)(2,1)S(1)}, u32[]{:S(2)}, u32[]{:S(2)}) collective-permute-start(bf16[512,256]{1,0:T(8,128)(2,1)S(1)} %get-tuple-element.66.refs_3_.refs_10_), channel_id=1, source_target_pairs={{0,24},{8,16},{16,8},{24,0},{1,25},{9,17},{17,9},{25,1},{2,26},{10... | collective-permute-start | bytes 786440 | tf_op jit(solution)/shard_map/ppermute | solution.py:371
  47.5 8.1 %collective-permute-start.18 = (bf16[256,256]{1,0:T(8,128)(2,1)S(1)}, bf16[256,256]{1,0:T(8,128)(2,1)S(1)}, u32[]{:S(2)}, u32[]{:S(2)}) collective-permute-start(bf16[256,256]{1,0:T(8,128)(2,1)S(1)} %get-tuple-element.68.refs_0_), channel_id=1, source_target_pairs={{0,4},{1,5},{2,6},{3,7},{4,0},{5,1},{6,2},{7,3},{8,12},{9,13},{10,... | collective-permute-start | bytes 393224 | tf_op jit(solution)/shard_map/ppermute | solution.py:371
  50.0 8.5 %collective-permute-start.17 = (bf16[256,256]{1,0:T(8,128)(2,1)S(1)}, bf16[256,256]{1,0:T(8,128)(2,1)S(1)}, u32[]{:S(2)}, u32[]{:S(2)}) collective-permute-start(bf16[256,256]{1,0:T(8,128)(2,1)S(1)} %get-tuple-element.68.refs_0_), channel_id=1, source_target_pairs={{0,2},{1,3},{2,0},{3,1},{4,6},{5,7},{6,4},{7,5},{8,10},{9,11},{10,... | collective-permute-start | bytes 393224 | tf_op jit(solution)/shard_map/ppermute | solution.py:371
  55.6 5.0 %collective-permute-start.20 = (bf16[1,256,256]{2,1,0:T(8,128)(2,1)S(1)}, bf16[1,256,256]{2,1,0:T(8,128)(2,1)S(1)}, u32[]{:S(2)}, u32[]{:S(2)}) collective-permute-start(bf16[1,256,256]{2,1,0:T(8,128)(2,1)S(1)} %shard_map.95.refs_2_), channel_id=1, source_target_pairs={{0,2},{1,3},{2,0},{3,1},{4,6},{5,7},{6,4},{7,5},{8,10},{9,11},{10,... | collective-permute-start | bytes 393224 | tf_op jit(solution)/shard_map/ppermute | solution.py:371
  56.4 6.7 %collective-permute-start.25 = (bf16[512,256]{1,0:T(8,128)(2,1)S(1)}, bf16[512,256]{1,0:T(8,128)(2,1)S(1)}, u32[]{:S(2)}, u32[]{:S(2)}) collective-permute-start(bf16[512,256]{1,0:T(8,128)(2,1)S(1)} %get-tuple-element.66.refs_3_.refs_10_), channel_id=1, source_target_pairs={{0,16},{8,24},{16,0},{24,8},{1,17},{9,25},{17,1},{25,9},{2,18},{10... | collective-permute-start | bytes 786440 | tf_op jit(solution)/shard_map/ppermute | solution.py:371
  57.9 6.4 %collective-permute-start.24 = (bf16[512,256]{1,0:T(8,128)(2,1)S(1)}, bf16[512,256]{1,0:T(8,128)(2,1)S(1)}, u32[]{:S(2)}, u32[]{:S(2)}) collective-permute-start(bf16[512,256]{1,0:T(8,128)(2,1)S(1)} %get-tuple-element.66.refs_3_.refs_10_), channel_id=1, source_target_pairs={{0,8},{8,0},{16,24},{24,16},{1,9},{9,1},{17,25},{25,17},{2,10},{10... | collective-permute-start | bytes 786440 | tf_op jit(solution)/shard_map/ppermute | solution.py:371
  66.8 15.6 %collective-permute-start.30 = (bf16[4,128,256]{2,1,0:T(8,128)(2,1)S(1)}, bf16[4,128,256]{2,1,0:T(8,128)(2,1)S(1)}, u32[]{:S(2)}, u32[]{:S(2)}) collective-permute-start(bf16[4,128,256]{2,1,0:T(8,128)(2,1)S(1)} %get-tuple-element.85), channel_id=1, source_target_pairs={{0,8},{8,0},{16,24},{24,16},{1,9},{9,1},{17,25},{25,17},{2,10},{10... | collective-permute-start | bytes 786440 | tf_op jit(solution)/shard_map/ppermute | solution.py:371
  67.5 14.9 %collective-permute-start.31 = (bf16[4,128,256]{2,1,0:T(8,128)(2,1)S(1)}, bf16[4,128,256]{2,1,0:T(8,128)(2,1)S(1)}, u32[]{:S(2)}, u32[]{:S(2)}) collective-permute-start(bf16[4,128,256]{2,1,0:T(8,128)(2,1)S(1)} %get-tuple-element.86), channel_id=1, source_target_pairs={{0,16},{8,24},{16,0},{24,8},{1,17},{9,25},{17,1},{25,9},{2,18},{10... | collective-permute-start | bytes 786440 | tf_op jit(solution)/shard_map/ppermute | solution.py:371
  69.9 7.3 %collective-permute-start.27 = (bf16[4,64,256]{2,1,0:T(8,128)(2,1)S(1)}, bf16[4,64,256]{2,1,0:T(8,128)(2,1)S(1)}, u32[]{:S(2)}, u32[]{:S(2)}) collective-permute-start(bf16[4,64,256]{2,1,0:T(8,128)(2,1)S(1)} %get-tuple-element.79), channel_id=1, source_target_pairs={{0,2},{1,3},{2,0},{3,1},{4,6},{5,7},{6,4},{7,5},{8,10},{9,11},{10,... | collective-permute-start | bytes 393224 | tf_op jit(solution)/shard_map/ppermute | solution.py:371
  73.7 9.4 %collective-permute-start.32 = (bf16[4,128,256]{2,1,0:T(8,128)(2,1)S(1)}, bf16[4,128,256]{2,1,0:T(8,128)(2,1)S(1)}, u32[]{:S(2)}, u32[]{:S(2)}) collective-permute-start(bf16[4,128,256]{2,1,0:T(8,128)(2,1)S(1)} %get-tuple-element.87), channel_id=1, source_target_pairs={{0,24},{8,16},{16,8},{24,0},{1,25},{9,17},{17,9},{25,1},{2,26},{10... | collective-permute-start | bytes 786440 | tf_op jit(solution)/shard_map/ppermute | solution.py:371
  77.3 9.3 %collective-permute-start.29 = (bf16[4,64,256]{2,1,0:T(8,128)(2,1)S(1)}, bf16[4,64,256]{2,1,0:T(8,128)(2,1)S(1)}, u32[]{:S(2)}, u32[]{:S(2)}) collective-permute-start(bf16[4,64,256]{2,1,0:T(8,128)(2,1)S(1)} %get-tuple-element.82), channel_id=1, source_target_pairs={{0,4},{1,5},{2,6},{3,7},{4,0},{5,1},{6,2},{7,3},{8,12},{9,13},{10,... | collective-permute-start | bytes 393224 | tf_op jit(solution)/shard_map/ppermute | solution.py:371
  80.7 6.3 %collective-permute-start.28 = (bf16[4,64,256]{2,1,0:T(8,128)(2,1)S(1)}, bf16[4,64,256]{2,1,0:T(8,128)(2,1)S(1)}, u32[]{:S(2)}, u32[]{:S(2)}) collective-permute-start(bf16[4,64,256]{2,1,0:T(8,128)(2,1)S(1)} %get-tuple-element.81.refs_3_.refs_4_), channel_id=1, source_target_pairs={{0,2},{1,3},{2,0},{3,1},{4,6},{5,7},{6,4},{7,5},{8,10},{9,11},{10,... | collective-permute-start | bytes 393224 | tf_op jit(solution)/shard_map/ppermute | solution.py:371
  (14 other events, 128.4 us)

commit v8 on v5

--- a/solution.py
+++ b/solution.py
@@ -216,9 +216,10 @@
         grad_turned[j] += jnp.dot(row_turned[i], signal[...], preferred_element_type=f32)
 
     def step(slot, before, now):
-        for rows in chunks:
+        for n, rows in enumerate(chunks):
             make_signal(slot, rows, now)
-            add_row(slot - 1, rows, before)
+            if n == 0:
+                add_row(slot - 1, slice(0, size), before)
         add_col(slot - 1, before)
 
     pairs = (count - 1) // 2

time: 86.3 us -> 86.4 us (level); the launches traced: 86.2 us -> 85 us
  starting transfers between devices: 46.8 us -> 43.4 us
  waiting for transfers between devices: 26.7 us -> 29 us
    ppermute x33, starting transfers between devices: 46.8 us -> 43.4 us  [send(): return lax.ppermute(x, axis, [(k, k ^ mask) for k in range(count)])]
    ppermute x33, waiting for transfers between devices: 26.7 us -> 29 us  [send(): return lax.ppermute(x, axis, [(k, k ^ mask) for k in range(count)])]
where the time goes in v8:
time: 86.4 us; the launch traced here: 85 us
  starting transfers between devices  43.4 us (50%)
  waiting for transfers between devices  29 us (34%)
  Pallas kernels  11.1 us (13%)
  between operations  1.5 us (2%)
    ppermute x33, starting transfers between devices, send(): return lax.ppermute(x, axis, [(k, k ^ mask) for k in range(count)])  43.4 us
    ppermute x33, waiting for transfers between devices, send(): return lax.ppermute(x, axis, [(k, k ^ mask) for k in range(count)])  29 us
    pallas_call x2, Pallas kernels, work(): pl.pallas_call(functools.partial(work_kernel, first, len(row_in), n_row,...  5.14 us
    pallas_call x4, Pallas kernels, update(): pl.pallas_call(functools.partial(update_kernel, len(parts), len(outs)), o...  1.98 us
    pallas_call x1, Pallas kernels, pack(): pl.pallas_call(pack_kernel, out_shape=[shape((e.shape[0] * e.shape[1] + M...  1.93 us
  transfers between devices with their start and end apart: 33, of which 14 were waited for; matrix products, arithmetic and copies ran while one was open for 0% of the time, Pallas kernels for 4%

profile of v8, /device:TPU:0, one launch (start us, length us, event | category | flops | bytes accessed | tf_op | source)
XLA Modules:
  0.0 85.0 jit_solution(2697927249349758541)
XLA Ops:
  0.6 1.9 %shard_map.87 = (bf16[272,256]{1,0:T(8,128)(2,1)}, bf16[528,256]{1,0:T(8,128)(2,1)}) custom-call(f32[4,64,256]{2,1,0:T(8,128)} %emb.3, bf16[4,64]{1,0:T(4,128)(2,1)} %row_marg.1, f32[4,128,256]{2,1,0:T(8,128)} %emb.2, bf16[4,128]{1,0:T(4,128)(2,1)} %col_marg.1), custom_call_target="tpu_custom_call" | custom-call | bytes 1048576 | tf_op jit(solution)/shard_map/pallas_call | solution.py:50
  2.6 4.1 %collective-permute-start.1 = (bf16[272,256]{1,0:T(8,128)(2,1)}, bf16[272,256]{1,0:T(8,128)(2,1)S(1)}, u32[]{:S(2)}, u32[]{:S(2)}) collective-permute-start(bf16[272,256]{1,0:T(8,128)(2,1)} %get-tuple-element.47.refs_0_), channel_id=1, source_target_pairs={{0,4},{1,5},{2,6},{3,7},{4,0},{5,1},{6,2},{7,3},{8,12},{9,13},{10,... | collective-permute-start | bytes 417800 | tf_op jit(solution)/shard_map/ppermute | solution.py:372
  11.9 1.7 %shard_map.86 = (f32[8,512,512]{2,1,0:T(8,128)S(1)}, bf16[8,512,512]{2,1,0:T(8,128)(2,1)S(1)}, f32[8,128]{1,0:T(8,128)S(1)}) custom-call(s32[1]{0:T(128)} %bitcast.5.used, s32[8,512,512]{2,1,0:T(8,128)} %bitcast.10), custom_call_target="tpu_custom_call" | custom-call | bytes 12582912 | tf_op jit(solution)/shard_map/pallas_call | solution.py:99
  14.5 2.4 %collective-permute-start.9 = (bf16[528,256]{1,0:T(8,128)(2,1)S(1)}, bf16[528,256]{1,0:T(8,128)(2,1)S(1)}, u32[]{:S(2)}, u32[]{:S(2)}) collective-permute-start(bf16[528,256]{1,0:T(8,128)(2,1)S(1)} %copy-done.2), channel_id=1, source_target_pairs={{0,24},{8,16},{16,8},{24,0},{1,25},{9,17},{17,9},{25,1},{2,26},{10... | collective-permute-start | bytes 811016 | tf_op jit(solution)/shard_map/ppermute | solution.py:372
  17.0 2.3 %collective-permute-done.2.refs_3_ = bf16[1,272,256]{2,1,0:T(8,128)(2,1)S(1)} collective-permute-done((bf16[1,272,256]{2,1,0:T(8,128)(2,1)S(1)}, bf16[1,272,256]{2,1,0:T(8,128)(2,1)S(1)}, u32[]{:S(2)}, u32[]{:S(2)}) %collective-permute-start.2) | collective-permute-done | bytes 139296 | tf_op jit(solution)/shard_map/ppermute | solution.py:372
  20.4 3.1 %collective-permute-done.9.refs_15_ = bf16[528,256]{1,0:T(8,128)(2,1)S(1)} collective-permute-done((bf16[528,256]{1,0:T(8,128)(2,1)S(1)}, bf16[528,256]{1,0:T(8,128)(2,1)S(1)}, u32[]{:S(2)}, u32[]{:S(2)}) %collective-permute-start.9) | collective-permute-done | bytes 270368 | tf_op jit(solution)/shard_map/ppermute | solution.py:372
  23.6 2.7 %shard_map.90 = (f32[4,4,64,256]{3,2,1,0:T(8,128)S(1)}, bf16[4,4,64,256]{3,2,1,0:T(8,128)(2,1)S(1)}, bf16[4,128,256]{2,1,0:T(8,128)(2,1)S(1)}, bf16[4,128,256]{2...) custom-call(s32[2,8]{1,0:T(2,128)S(1)} %bitcast.8, ...), custom_call_target="tpu_custom_call" | custom-call | flops 3221225472 | bytes 16777216 | tf_op jit(solution)/shard_map/pallas_call | solution.py:280
  26.4 2.0 %collective-permute-start.14 = (bf16[4,128,256]{2,1,0:T(8,128)(2,1)S(1)}, bf16[4,128,256]{2,1,0:T(8,128)(2,1)S(1)}, u32[]{:S(2)}, u32[]{:S(2)}) collective-permute-start(bf16[4,128,256]{2,1,0:T(8,128)(2,1)S(1)} %get-tuple-element.63), channel_id=1, source_target_pairs={{0,8},{8,0},{16,24},{24,16},{1,9},{9,1},{17,25},{25,17},{2,10},{10... | collective-permute-start | bytes 786440 | tf_op jit(solution)/shard_map/ppermute | solution.py:372
  28.4 3.6 %collective-permute-start.15 = (bf16[4,128,256]{2,1,0:T(8,128)(2,1)S(1)}, bf16[4,128,256]{2,1,0:T(8,128)(2,1)S(1)}, u32[]{:S(2)}, u32[]{:S(2)}) collective-permute-start(bf16[4,128,256]{2,1,0:T(8,128)(2,1)S(1)} %get-tuple-element.64), channel_id=1, source_target_pairs={{0,16},{8,24},{16,0},{24,8},{1,17},{9,25},{17,1},{25,9},{2,18},{10... | collective-permute-start | bytes 786440 | tf_op jit(solution)/shard_map/ppermute | solution.py:372
  32.6 5.0 %collective-permute-done.11.refs_0_ = bf16[4,64,256]{2,1,0:T(8,128)(2,1)S(1)} collective-permute-done((bf16[4,64,256]{2,1,0:T(8,128)(2,1)S(1)}, bf16[4,64,256]{2,1,0:T(8,128)(2,1)S(1)}, u32[]{:S(2)}, u32[]{:S(2)}) %collective-permute-start.11) | collective-permute-done | bytes 131104 | tf_op jit(solution)/shard_map/ppermute | solution.py:372
  37.6 2.5 %collective-permute-start.13 = (bf16[4,64,256]{2,1,0:T(8,128)(2,1)S(1)}, bf16[4,64,256]{2,1,0:T(8,128)(2,1)S(1)}, u32[]{:S(2)}, u32[]{:S(2)}) collective-permute-start(bf16[4,64,256]{2,1,0:T(8,128)(2,1)S(1)} %get-tuple-element.61), channel_id=1, source_target_pairs={{0,4},{1,5},{2,6},{3,7},{4,0},{5,1},{6,2},{7,3},{8,12},{9,13},{10,... | collective-permute-start | bytes 393224 | tf_op jit(solution)/shard_map/ppermute | solution.py:372
  40.1 1.7 %collective-permute-start.12 = (bf16[4,64,256]{2,1,0:T(8,128)(2,1)S(1)}, bf16[4,64,256]{2,1,0:T(8,128)(2,1)S(1)}, u32[]{:S(2)}, u32[]{:S(2)}) collective-permute-start(bf16[4,64,256]{2,1,0:T(8,128)(2,1)S(1)} %get-tuple-element.60.refs_4_), channel_id=1, source_target_pairs={{0,2},{1,3},{2,0},{3,1},{4,6},{5,7},{6,4},{7,5},{8,10},{9,11},{10,... | collective-permute-start | bytes 393224 | tf_op jit(solution)/shard_map/ppermute | solution.py:372
  44.5 1.8 %collective-permute-start.19 = (bf16[512,256]{1,0:T(8,128)(2,1)S(1)}, bf16[512,256]{1,0:T(8,128)(2,1)S(1)}, u32[]{:S(2)}, u32[]{:S(2)}) collective-permute-start(bf16[512,256]{1,0:T(8,128)(2,1)S(1)} %get-tuple-element.66.refs_3_.refs_10_), channel_id=1, source_target_pairs={{0,24},{8,16},{16,8},{24,0},{1,25},{9,17},{17,9},{25,1},{2,26},{10... | collective-permute-start | bytes 786440 | tf_op jit(solution)/shard_map/ppermute | solution.py:372
  46.4 2.4 %collective-permute-start.18 = (bf16[256,256]{1,0:T(8,128)(2,1)S(1)}, bf16[256,256]{1,0:T(8,128)(2,1)S(1)}, u32[]{:S(2)}, u32[]{:S(2)}) collective-permute-start(bf16[256,256]{1,0:T(8,128)(2,1)S(1)} %get-tuple-element.68.refs_0_), channel_id=1, source_target_pairs={{0,4},{1,5},{2,6},{3,7},{4,0},{5,1},{6,2},{7,3},{8,12},{9,13},{10,... | collective-permute-start | bytes 393224 | tf_op jit(solution)/shard_map/ppermute | solution.py:372
  48.8 1.9 %collective-permute-start.17 = (bf16[256,256]{1,0:T(8,128)(2,1)S(1)}, bf16[256,256]{1,0:T(8,128)(2,1)S(1)}, u32[]{:S(2)}, u32[]{:S(2)}) collective-permute-start(bf16[256,256]{1,0:T(8,128)(2,1)S(1)} %get-tuple-element.68.refs_0_), channel_id=1, source_target_pairs={{0,2},{1,3},{2,0},{3,1},{4,6},{5,7},{6,4},{7,5},{8,10},{9,11},{10,... | collective-permute-start | bytes 393224 | tf_op jit(solution)/shard_map/ppermute | solution.py:372
  50.7 3.7 %collective-permute-done.18.refs_0_ = bf16[256,256]{1,0:T(8,128)(2,1)S(1)} collective-permute-done((bf16[256,256]{1,0:T(8,128)(2,1)S(1)}, bf16[256,256]{1,0:T(8,128)(2,1)S(1)}, u32[]{:S(2)}, u32[]{:S(2)}) %collective-permute-start.18) | collective-permute-done | bytes 131104 | tf_op jit(solution)/shard_map/ppermute | solution.py:372
  57.3 2.2 %collective-permute-done.20.refs_3_ = bf16[1,256,256]{2,1,0:T(8,128)(2,1)S(1)} collective-permute-done((bf16[1,256,256]{2,1,0:T(8,128)(2,1)S(1)}, bf16[1,256,256]{2,1,0:T(8,128)(2,1)S(1)}, u32[]{:S(2)}, u32[]{:S(2)}) %collective-permute-start.20) | collective-permute-done | bytes 131104 | tf_op jit(solution)/shard_map/ppermute | solution.py:372
  60.1 2.2 %collective-permute-done.25.refs_12_ = bf16[512,256]{1,0:T(8,128)(2,1)S(1)} collective-permute-done((bf16[512,256]{1,0:T(8,128)(2,1)S(1)}, bf16[512,256]{1,0:T(8,128)(2,1)S(1)}, u32[]{:S(2)}, u32[]{:S(2)}) %collective-permute-start.25) | collective-permute-done | bytes 262176 | tf_op jit(solution)/shard_map/ppermute | solution.py:372
  62.6 2.4 %shard_map.97 = (f32[4,4,64,256]{3,2,1,0:T(8,128)S(1)}, bf16[4,4,64,256]{3,2,1,0:T(8,128)(2,1)S(1)}, bf16[4,128,256]{2,1,0:T(8,128)(2,1)S(1)}, bf16[4,128,256]{2...) custom-call(s32[2,8]{1,0:T(2,128)S(1)} %bitcast.9, s32[1]{0:T(128)} %bitcast.7.refs_1_, ...), custom_call_target="tpu_custom_call" | custom-call | flops 3221225472 | bytes 16777216 | tf_op jit(solution)/shard_map/pallas_call | solution.py:280
  65.2 1.9 %collective-permute-start.30 = (bf16[4,128,256]{2,1,0:T(8,128)(2,1)S(1)}, bf16[4,128,256]{2,1,0:T(8,128)(2,1)S(1)}, u32[]{:S(2)}, u32[]{:S(2)}) collective-permute-start(bf16[4,128,256]{2,1,0:T(8,128)(2,1)S(1)} %get-tuple-element.85), channel_id=1, source_target_pairs={{0,8},{8,0},{16,24},{24,16},{1,9},{9,1},{17,25},{25,17},{2,10},{10... | collective-permute-start | bytes 786440 | tf_op jit(solution)/shard_map/ppermute | solution.py:372
  67.0 3.0 %collective-permute-start.31 = (bf16[4,128,256]{2,1,0:T(8,128)(2,1)S(1)}, bf16[4,128,256]{2,1,0:T(8,128)(2,1)S(1)}, u32[]{:S(2)}, u32[]{:S(2)}) collective-permute-start(bf16[4,128,256]{2,1,0:T(8,128)(2,1)S(1)} %get-tuple-element.86), channel_id=1, source_target_pairs={{0,16},{8,24},{16,0},{24,8},{1,17},{9,25},{17,1},{25,9},{2,18},{10... | collective-permute-start | bytes 786440 | tf_op jit(solution)/shard_map/ppermute | solution.py:372
  71.3 3.9 %collective-permute-done.27.refs_0_ = bf16[4,64,256]{2,1,0:T(8,128)(2,1)S(1)} collective-permute-done((bf16[4,64,256]{2,1,0:T(8,128)(2,1)S(1)}, bf16[4,64,256]{2,1,0:T(8,128)(2,1)S(1)}, u32[]{:S(2)}, u32[]{:S(2)}) %collective-permute-start.27) | collective-permute-done | bytes 131104 | tf_op jit(solution)/shard_map/ppermute | solution.py:372
  75.2 2.8 %collective-permute-start.29 = (bf16[4,64,256]{2,1,0:T(8,128)(2,1)S(1)}, bf16[4,64,256]{2,1,0:T(8,128)(2,1)S(1)}, u32[]{:S(2)}, u32[]{:S(2)}) collective-permute-start(bf16[4,64,256]{2,1,0:T(8,128)(2,1)S(1)} %get-tuple-element.82), channel_id=1, source_target_pairs={{0,4},{1,5},{2,6},{3,7},{4,0},{5,1},{6,2},{7,3},{8,12},{9,13},{10,... | collective-permute-start | bytes 393224 | tf_op jit(solution)/shard_map/ppermute | solution.py:372
  78.0 1.6 %collective-permute-start.28 = (bf16[4,64,256]{2,1,0:T(8,128)(2,1)S(1)}, bf16[4,64,256]{2,1,0:T(8,128)(2,1)S(1)}, u32[]{:S(2)}, u32[]{:S(2)}) collective-permute-start(bf16[4,64,256]{2,1,0:T(8,128)(2,1)S(1)} %get-tuple-element.81.refs_3_.refs_4_), channel_id=1, source_target_pairs={{0,2},{1,3},{2,0},{3,1},{4,6},{5,7},{6,4},{7,5},{8,10},{9,11},{10,... | collective-permute-start | bytes 393224 | tf_op jit(solution)/shard_map/ppermute | solution.py:372
  (68 shorter events, 20.6 us)
Async XLA Ops:
  2.6 11.1 %collective-permute-start.1 = (bf16[272,256]{1,0:T(8,128)(2,1)}, bf16[272,256]{1,0:T(8,128)(2,1)S(1)}, u32[]{:S(2)}, u32[]{:S(2)}) collective-permute-start(bf16[272,256]{1,0:T(8,128)(2,1)} %get-tuple-element.47.refs_0_), channel_id=1, source_target_pairs={{0,4},{1,5},{2,6},{3,7},{4,0},{5,1},{6,2},{7,3},{8,12},{9,13},{10,... | collective-permute-start | bytes 417800 | tf_op jit(solution)/shard_map/ppermute | solution.py:372
  6.7 10.3 %collective-permute-start.4 = (bf16[528,256]{1,0:T(8,128)(2,1)}, bf16[528,256]{1,0:T(8,128)(2,1)S(1)}, u32[]{:S(2)}, u32[]{:S(2)}) collective-permute-start(bf16[528,256]{1,0:T(8,128)(2,1)} %get-tuple-element.49.refs_12_), channel_id=1, source_target_pairs={{0,16},{8,24},{16,0},{24,8},{1,17},{9,25},{17,1},{25,9},{2,18},{10... | collective-permute-start | bytes 811016 | tf_op jit(solution)/shard_map/ppermute | solution.py:372
  8.2 8.8 %collective-permute-start.3 = (bf16[528,256]{1,0:T(8,128)(2,1)}, bf16[528,256]{1,0:T(8,128)(2,1)S(1)}, u32[]{:S(2)}, u32[]{:S(2)}) collective-permute-start(bf16[528,256]{1,0:T(8,128)(2,1)} %get-tuple-element.49.refs_12_), channel_id=1, source_target_pairs={{0,8},{8,0},{16,24},{24,16},{1,9},{9,1},{17,25},{25,17},{2,10},{10... | collective-permute-start | bytes 811016 | tf_op jit(solution)/shard_map/ppermute | solution.py:372
  9.7 7.3 %collective-permute-start = (bf16[272,256]{1,0:T(8,128)(2,1)}, bf16[272,256]{1,0:T(8,128)(2,1)S(1)}, u32[]{:S(2)}, u32[]{:S(2)}) collective-permute-start(bf16[272,256]{1,0:T(8,128)(2,1)} %get-tuple-element.47.refs_0_), channel_id=1, source_target_pairs={{0,2},{1,3},{2,0},{3,1},{4,6},{5,7},{6,4},{7,5},{8,10},{9,11},{10,... | collective-permute-start | bytes 417800 | tf_op jit(solution)/shard_map/ppermute | solution.py:372
  13.7 5.6 %collective-permute-start.2 = (bf16[1,272,256]{2,1,0:T(8,128)(2,1)S(1)}, bf16[1,272,256]{2,1,0:T(8,128)(2,1)S(1)}, u32[]{:S(2)}, u32[]{:S(2)}) collective-permute-start(bf16[1,272,256]{2,1,0:T(8,128)(2,1)S(1)} %shard_map.88.refs_2_), channel_id=1, source_target_pairs={{0,2},{1,3},{2,0},{3,1},{4,6},{5,7},{6,4},{7,5},{8,10},{9,11},{10,... | collective-permute-start | bytes 417800 | tf_op jit(solution)/shard_map/ppermute | solution.py:372
  14.5 9.0 %collective-permute-start.9 = (bf16[528,256]{1,0:T(8,128)(2,1)S(1)}, bf16[528,256]{1,0:T(8,128)(2,1)S(1)}, u32[]{:S(2)}, u32[]{:S(2)}) collective-permute-start(bf16[528,256]{1,0:T(8,128)(2,1)S(1)} %copy-done.2), channel_id=1, source_target_pairs={{0,24},{8,16},{16,8},{24,0},{1,25},{9,17},{17,9},{25,1},{2,26},{10... | collective-permute-start | bytes 811016 | tf_op jit(solution)/shard_map/ppermute | solution.py:372
  26.3 6.1 %collective-permute-start.10 = (bf16[4,4,64,256]{3,2,1,0:T(8,128)(2,1)S(1)}, bf16[4,4,64,256]{3,2,1,0:T(8,128)(2,1)S(1)}, u32[]{:S(2)}, u32[]{:S(2)}) collective-permute-start(bf16[4,4,64,256]{3,2,1,0:T(8,128)(2,1)S(1)} %get-tuple-element.55), channel_id=1, source_target_pairs={{0,1},{1,0},{2,3},{3,2},{4,5},{5,4},{6,7},{7,6},{8,9},{9,8},{10,11... | collective-permute-start | bytes 1572872 | tf_op jit(solution)/shard_map/ppermute | solution.py:372
  26.4 15.4 %collective-permute-start.14 = (bf16[4,128,256]{2,1,0:T(8,128)(2,1)S(1)}, bf16[4,128,256]{2,1,0:T(8,128)(2,1)S(1)}, u32[]{:S(2)}, u32[]{:S(2)}) collective-permute-start(bf16[4,128,256]{2,1,0:T(8,128)(2,1)S(1)} %get-tuple-element.63), channel_id=1, source_target_pairs={{0,8},{8,0},{16,24},{24,16},{1,9},{9,1},{17,25},{25,17},{2,10},{10... | collective-permute-start | bytes 786440 | tf_op jit(solution)/shard_map/ppermute | solution.py:372
  28.4 14.8 %collective-permute-start.15 = (bf16[4,128,256]{2,1,0:T(8,128)(2,1)S(1)}, bf16[4,128,256]{2,1,0:T(8,128)(2,1)S(1)}, u32[]{:S(2)}, u32[]{:S(2)}) collective-permute-start(bf16[4,128,256]{2,1,0:T(8,128)(2,1)S(1)} %get-tuple-element.64), channel_id=1, source_target_pairs={{0,16},{8,24},{16,0},{24,8},{1,17},{9,25},{17,1},{25,9},{2,18},{10... | collective-permute-start | bytes 786440 | tf_op jit(solution)/shard_map/ppermute | solution.py:372
  32.0 12.3 %collective-permute-start.16 = (bf16[4,128,256]{2,1,0:T(8,128)(2,1)S(1)}, bf16[4,128,256]{2,1,0:T(8,128)(2,1)S(1)}, u32[]{:S(2)}, u32[]{:S(2)}) collective-permute-start(bf16[4,128,256]{2,1,0:T(8,128)(2,1)S(1)} %get-tuple-element.65), channel_id=1, source_target_pairs={{0,24},{8,16},{16,8},{24,0},{1,25},{9,17},{17,9},{25,1},{2,26},{10... | collective-permute-start | bytes 786440 | tf_op jit(solution)/shard_map/ppermute | solution.py:372
  32.5 5.0 %collective-permute-start.11 = (bf16[4,64,256]{2,1,0:T(8,128)(2,1)S(1)}, bf16[4,64,256]{2,1,0:T(8,128)(2,1)S(1)}, u32[]{:S(2)}, u32[]{:S(2)}) collective-permute-start(bf16[4,64,256]{2,1,0:T(8,128)(2,1)S(1)} %get-tuple-element.58), channel_id=1, source_target_pairs={{0,2},{1,3},{2,0},{3,1},{4,6},{5,7},{6,4},{7,5},{8,10},{9,11},{10,... | collective-permute-start | bytes 393224 | tf_op jit(solution)/shard_map/ppermute | solution.py:372
  37.6 8.7 %collective-permute-start.13 = (bf16[4,64,256]{2,1,0:T(8,128)(2,1)S(1)}, bf16[4,64,256]{2,1,0:T(8,128)(2,1)S(1)}, u32[]{:S(2)}, u32[]{:S(2)}) collective-permute-start(bf16[4,64,256]{2,1,0:T(8,128)(2,1)S(1)} %get-tuple-element.61), channel_id=1, source_target_pairs={{0,4},{1,5},{2,6},{3,7},{4,0},{5,1},{6,2},{7,3},{8,12},{9,13},{10,... | collective-permute-start | bytes 393224 | tf_op jit(solution)/shard_map/ppermute | solution.py:372
  40.1 6.3 %collective-permute-start.12 = (bf16[4,64,256]{2,1,0:T(8,128)(2,1)S(1)}, bf16[4,64,256]{2,1,0:T(8,128)(2,1)S(1)}, u32[]{:S(2)}, u32[]{:S(2)}) collective-permute-start(bf16[4,64,256]{2,1,0:T(8,128)(2,1)S(1)} %get-tuple-element.60.refs_4_), channel_id=1, source_target_pairs={{0,2},{1,3},{2,0},{3,1},{4,6},{5,7},{6,4},{7,5},{8,10},{9,11},{10,... | collective-permute-start | bytes 393224 | tf_op jit(solution)/shard_map/ppermute | solution.py:372
  44.5 9.9 %collective-permute-start.19 = (bf16[512,256]{1,0:T(8,128)(2,1)S(1)}, bf16[512,256]{1,0:T(8,128)(2,1)S(1)}, u32[]{:S(2)}, u32[]{:S(2)}) collective-permute-start(bf16[512,256]{1,0:T(8,128)(2,1)S(1)} %get-tuple-element.66.refs_3_.refs_10_), channel_id=1, source_target_pairs={{0,24},{8,16},{16,8},{24,0},{1,25},{9,17},{17,9},{25,1},{2,26},{10... | collective-permute-start | bytes 786440 | tf_op jit(solution)/shard_map/ppermute | solution.py:372
  46.4 8.0 %collective-permute-start.18 = (bf16[256,256]{1,0:T(8,128)(2,1)S(1)}, bf16[256,256]{1,0:T(8,128)(2,1)S(1)}, u32[]{:S(2)}, u32[]{:S(2)}) collective-permute-start(bf16[256,256]{1,0:T(8,128)(2,1)S(1)} %get-tuple-element.68.refs_0_), channel_id=1, source_target_pairs={{0,4},{1,5},{2,6},{3,7},{4,0},{5,1},{6,2},{7,3},{8,12},{9,13},{10,... | collective-permute-start | bytes 393224 | tf_op jit(solution)/shard_map/ppermute | solution.py:372
  48.8 8.4 %collective-permute-start.17 = (bf16[256,256]{1,0:T(8,128)(2,1)S(1)}, bf16[256,256]{1,0:T(8,128)(2,1)S(1)}, u32[]{:S(2)}, u32[]{:S(2)}) collective-permute-start(bf16[256,256]{1,0:T(8,128)(2,1)S(1)} %get-tuple-element.68.refs_0_), channel_id=1, source_target_pairs={{0,2},{1,3},{2,0},{3,1},{4,6},{5,7},{6,4},{7,5},{8,10},{9,11},{10,... | collective-permute-start | bytes 393224 | tf_op jit(solution)/shard_map/ppermute | solution.py:372
  54.4 5.0 %collective-permute-start.20 = (bf16[1,256,256]{2,1,0:T(8,128)(2,1)S(1)}, bf16[1,256,256]{2,1,0:T(8,128)(2,1)S(1)}, u32[]{:S(2)}, u32[]{:S(2)}) collective-permute-start(bf16[1,256,256]{2,1,0:T(8,128)(2,1)S(1)} %shard_map.95.refs_2_), channel_id=1, source_target_pairs={{0,2},{1,3},{2,0},{3,1},{4,6},{5,7},{6,4},{7,5},{8,10},{9,11},{10,... | collective-permute-start | bytes 393224 | tf_op jit(solution)/shard_map/ppermute | solution.py:372
  55.2 7.2 %collective-permute-start.25 = (bf16[512,256]{1,0:T(8,128)(2,1)S(1)}, bf16[512,256]{1,0:T(8,128)(2,1)S(1)}, u32[]{:S(2)}, u32[]{:S(2)}) collective-permute-start(bf16[512,256]{1,0:T(8,128)(2,1)S(1)} %get-tuple-element.66.refs_3_.refs_10_), channel_id=1, source_target_pairs={{0,16},{8,24},{16,0},{24,8},{1,17},{9,25},{17,1},{25,9},{2,18},{10... | collective-permute-start | bytes 786440 | tf_op jit(solution)/shard_map/ppermute | solution.py:372
  55.8 6.8 %collective-permute-start.24 = (bf16[512,256]{1,0:T(8,128)(2,1)S(1)}, bf16[512,256]{1,0:T(8,128)(2,1)S(1)}, u32[]{:S(2)}, u32[]{:S(2)}) collective-permute-start(bf16[512,256]{1,0:T(8,128)(2,1)S(1)} %get-tuple-element.66.refs_3_.refs_10_), channel_id=1, source_target_pairs={{0,8},{8,0},{16,24},{24,16},{1,9},{9,1},{17,25},{25,17},{2,10},{10... | collective-permute-start | bytes 786440 | tf_op jit(solution)/shard_map/ppermute | solution.py:372
  65.2 14.5 %collective-permute-start.30 = (bf16[4,128,256]{2,1,0:T(8,128)(2,1)S(1)}, bf16[4,128,256]{2,1,0:T(8,128)(2,1)S(1)}, u32[]{:S(2)}, u32[]{:S(2)}) collective-permute-start(bf16[4,128,256]{2,1,0:T(8,128)(2,1)S(1)} %get-tuple-element.85), channel_id=1, source_target_pairs={{0,8},{8,0},{16,24},{24,16},{1,9},{9,1},{17,25},{25,17},{2,10},{10... | collective-permute-start | bytes 786440 | tf_op jit(solution)/shard_map/ppermute | solution.py:372
  67.0 14.1 %collective-permute-start.31 = (bf16[4,128,256]{2,1,0:T(8,128)(2,1)S(1)}, bf16[4,128,256]{2,1,0:T(8,128)(2,1)S(1)}, u32[]{:S(2)}, u32[]{:S(2)}) collective-permute-start(bf16[4,128,256]{2,1,0:T(8,128)(2,1)S(1)} %get-tuple-element.86), channel_id=1, source_target_pairs={{0,16},{8,24},{16,0},{24,8},{1,17},{9,25},{17,1},{25,9},{2,18},{10... | collective-permute-start | bytes 786440 | tf_op jit(solution)/shard_map/ppermute | solution.py:372
  70.3 12.0 %collective-permute-start.32 = (bf16[4,128,256]{2,1,0:T(8,128)(2,1)S(1)}, bf16[4,128,256]{2,1,0:T(8,128)(2,1)S(1)}, u32[]{:S(2)}, u32[]{:S(2)}) collective-permute-start(bf16[4,128,256]{2,1,0:T(8,128)(2,1)S(1)} %get-tuple-element.87), channel_id=1, source_target_pairs={{0,24},{8,16},{16,8},{24,0},{1,25},{9,17},{17,9},{25,1},{2,26},{10... | collective-permute-start | bytes 786440 | tf_op jit(solution)/shard_map/ppermute | solution.py:372
  75.2 8.7 %collective-permute-start.29 = (bf16[4,64,256]{2,1,0:T(8,128)(2,1)S(1)}, bf16[4,64,256]{2,1,0:T(8,128)(2,1)S(1)}, u32[]{:S(2)}, u32[]{:S(2)}) collective-permute-start(bf16[4,64,256]{2,1,0:T(8,128)(2,1)S(1)} %get-tuple-element.82), channel_id=1, source_target_pairs={{0,4},{1,5},{2,6},{3,7},{4,0},{5,1},{6,2},{7,3},{8,12},{9,13},{10,... | collective-permute-start | bytes 393224 | tf_op jit(solution)/shard_map/ppermute | solution.py:372
  78.0 6.3 %collective-permute-start.28 = (bf16[4,64,256]{2,1,0:T(8,128)(2,1)S(1)}, bf16[4,64,256]{2,1,0:T(8,128)(2,1)S(1)}, u32[]{:S(2)}, u32[]{:S(2)}) collective-permute-start(bf16[4,64,256]{2,1,0:T(8,128)(2,1)S(1)} %get-tuple-element.81.refs_3_.refs_4_), channel_id=1, source_target_pairs={{0,2},{1,3},{2,0},{3,1},{4,6},{5,7},{6,4},{7,5},{8,10},{9,11},{10,... | collective-permute-start | bytes 393224 | tf_op jit(solution)/shard_map/ppermute | solution.py:372
  (14 other events, 129.4 us)

commit v9 on v5

--- a/solution.py
+++ b/solution.py
@@ -256,11 +256,17 @@
             swap[place] = piece.astype(bf16)
         else:
             keep[place] = piece
-    for b in range(col_blocks):
-        grad_col[b] = grad_turned[b].astype(bf16).T
+    aligned = col_part % 128 == 0
+    if not aligned:
+        for b in range(col_blocks):
+            grad_col[b] = grad_turned[b].astype(bf16).T
     for n in range(n_col):
         start = pl.multiple_of(col_owners[n] * col_part, col_part)
-        col_out[n][...] = grad_col[:, pl.ds(start, col_part), :]
+        if aligned:
+            for b in range(col_blocks):
+                col_out[n][b] = grad_turned[b, :, pl.ds(start, col_part)].astype(bf16).T
+        else:
+            col_out[n][...] = grad_col[:, pl.ds(start, col_part), :]
 
 
 def work(listing, used, tabs, row_in, col_in, tables, row_owner, col_owner, dims):

time: 86.3 us -> 86.1 us (level)
  starting transfers between devices: 46.8 us -> 29.7 us
  Pallas kernels: 11.1 us -> 19.8 us
  waiting for transfers between devices: 26.7 us -> 34.8 us
    ppermute x33, starting transfers between devices: 46.8 us -> 29.7 us  [send(): return lax.ppermute(x, axis, [(k, k ^ mask) for k in range(count)])]
    ppermute x33, waiting for transfers between devices: 26.7 us -> 34.8 us  [send(): return lax.ppermute(x, axis, [(k, k ^ mask) for k in range(count)])]
    pallas_call x2, Pallas kernels: 5.14 us -> 11.3 us  [work(): pl.pallas_call(functools.partial(work_kernel, first, len(row_in), n_row,...]
    pallas_call x1, Pallas kernels: 1.71 us -> 4.21 us  [levels(): pl.pallas_call(levels_kernel, out_shape=[shape(tiles.shape, f32), shape(t...]
  transfers between devices with their start and end apart: 33 -> 33, of which waited for: 14 -> 14; matrix products, arithmetic and copies ran while one was open for 0% -> 0% of each run, Pallas kernels for 4% -> 7%
where the time goes in v9:
time: 86.1 us; the launch traced here: 85.9 us
  waiting for transfers between devices  34.8 us (40%)
  starting transfers between devices  29.7 us (34%)
  Pallas kernels  19.8 us (23%)
  between operations  1.52 us (2%)
    ppermute x33, waiting for transfers between devices, send(): return lax.ppermute(x, axis, [(k, k ^ mask) for k in range(count)])  34.8 us
    ppermute x33, starting transfers between devices, send(): return lax.ppermute(x, axis, [(k, k ^ mask) for k in range(count)])  29.7 us
    pallas_call x2, Pallas kernels, work(): pl.pallas_call(functools.partial(work_kernel, first, len(row_in), n_row,...  11.3 us
    pallas_call x1, Pallas kernels, levels(): pl.pallas_call(levels_kernel, out_shape=[shape(tiles.shape, f32), shape(t...  4.21 us
    pallas_call x4, Pallas kernels, update(): pl.pallas_call(functools.partial(update_kernel, len(parts), len(outs)), o...  1.98 us
    pallas_call x1, Pallas kernels, pack(): pl.pallas_call(pack_kernel, out_shape=[shape((e.shape[0] * e.shape[1] + M...  1.93 us
  transfers between devices with their start and end apart: 33, of which 14 were waited for; matrix products, arithmetic and copies ran while one was open for 0% of the time, Pallas kernels for 7%

profile of v9, /device:TPU:0, one launch (start us, length us, event | category | flops | bytes accessed | tf_op | source)
XLA Modules:
  0.0 85.9 jit_solution(11909159027346381705)
XLA Ops:
  0.6 1.9 %shard_map.87 = (bf16[272,256]{1,0:T(8,128)(2,1)}, bf16[528,256]{1,0:T(8,128)(2,1)}) custom-call(f32[4,64,256]{2,1,0:T(8,128)} %emb.3, bf16[4,64]{1,0:T(4,128)(2,1)} %row_marg.1, f32[4,128,256]{2,1,0:T(8,128)} %emb.2, bf16[4,128]{1,0:T(4,128)(2,1)} %col_marg.1), custom_call_target="tpu_custom_call" | custom-call | bytes 1048576 | tf_op jit(solution)/shard_map/pallas_call | solution.py:50
  2.6 4.1 %collective-permute-start.1 = (bf16[272,256]{1,0:T(8,128)(2,1)}, bf16[272,256]{1,0:T(8,128)(2,1)S(1)}, u32[]{:S(2)}, u32[]{:S(2)}) collective-permute-start(bf16[272,256]{1,0:T(8,128)(2,1)} %get-tuple-element.47.refs_0_), channel_id=1, source_target_pairs={{0,4},{1,5},{2,6},{3,7},{4,0},{5,1},{6,2},{7,3},{8,12},{9,13},{10,... | collective-permute-start | bytes 417800 | tf_op jit(solution)/shard_map/ppermute | solution.py:377
  6.7 1.5 %collective-permute-start.4 = (bf16[528,256]{1,0:T(8,128)(2,1)}, bf16[528,256]{1,0:T(8,128)(2,1)S(1)}, u32[]{:S(2)}, u32[]{:S(2)}) collective-permute-start(bf16[528,256]{1,0:T(8,128)(2,1)} %get-tuple-element.49.refs_12_), channel_id=1, source_target_pairs={{0,16},{8,24},{16,0},{24,8},{1,17},{9,25},{17,1},{25,9},{2,18},{10... | collective-permute-start | bytes 811016 | tf_op jit(solution)/shard_map/ppermute | solution.py:377
  8.2 1.5 %collective-permute-start.3 = (bf16[528,256]{1,0:T(8,128)(2,1)}, bf16[528,256]{1,0:T(8,128)(2,1)S(1)}, u32[]{:S(2)}, u32[]{:S(2)}) collective-permute-start(bf16[528,256]{1,0:T(8,128)(2,1)} %get-tuple-element.49.refs_12_), channel_id=1, source_target_pairs={{0,8},{8,0},{16,24},{24,16},{1,9},{9,1},{17,25},{25,17},{2,10},{10... | collective-permute-start | bytes 811016 | tf_op jit(solution)/shard_map/ppermute | solution.py:377
  9.7 1.6 %collective-permute-start = (bf16[272,256]{1,0:T(8,128)(2,1)}, bf16[272,256]{1,0:T(8,128)(2,1)S(1)}, u32[]{:S(2)}, u32[]{:S(2)}) collective-permute-start(bf16[272,256]{1,0:T(8,128)(2,1)} %get-tuple-element.47.refs_0_), channel_id=1, source_target_pairs={{0,2},{1,3},{2,0},{3,1},{4,6},{5,7},{6,4},{7,5},{8,10},{9,11},{10,... | collective-permute-start | bytes 417800 | tf_op jit(solution)/shard_map/ppermute | solution.py:377
  11.9 4.2 %shard_map.86 = (f32[8,512,512]{2,1,0:T(8,128)S(1)}, bf16[8,512,512]{2,1,0:T(8,128)(2,1)S(1)}, f32[8,128]{1,0:T(8,128)S(1)}) custom-call(s32[1]{0:T(128)} %bitcast.5.used, s32[8,512,512]{2,1,0:T(8,128)} %bitcast.10), custom_call_target="tpu_custom_call" | custom-call | bytes 12582912 | tf_op jit(solution)/shard_map/pallas_call | solution.py:99
  17.0 4.3 %collective-permute-done.2.refs_3_ = bf16[1,272,256]{2,1,0:T(8,128)(2,1)S(1)} collective-permute-done((bf16[1,272,256]{2,1,0:T(8,128)(2,1)S(1)}, bf16[1,272,256]{2,1,0:T(8,128)(2,1)S(1)}, u32[]{:S(2)}, u32[]{:S(2)}) %collective-permute-start.2) | collective-permute-done | bytes 139296 | tf_op jit(solution)/shard_map/ppermute | solution.py:377
  22.4 1.5 %collective-permute-done.9.refs_15_ = bf16[528,256]{1,0:T(8,128)(2,1)S(1)} collective-permute-done((bf16[528,256]{1,0:T(8,128)(2,1)S(1)}, bf16[528,256]{1,0:T(8,128)(2,1)S(1)}, u32[]{:S(2)}, u32[]{:S(2)}) %collective-permute-start.9) | collective-permute-done | bytes 270368 | tf_op jit(solution)/shard_map/ppermute | solution.py:377
  24.0 5.8 %shard_map.90 = (f32[4,4,64,256]{3,2,1,0:T(8,128)S(1)}, bf16[4,4,64,256]{3,2,1,0:T(8,128)(2,1)S(1)}, bf16[4,128,256]{2,1,0:T(8,128)(2,1)S(1)}, bf16[4,128,256]{2...) custom-call(s32[2,8]{1,0:T(2,128)S(1)} %bitcast.8, ...), custom_call_target="tpu_custom_call" | custom-call | flops 3221225472 | bytes 16777216 | tf_op jit(solution)/shard_map/pallas_call | solution.py:285
  30.7 2.7 %collective-permute-start.16 = (bf16[4,128,256]{2,1,0:T(8,128)(2,1)S(1)}, bf16[4,128,256]{2,1,0:T(8,128)(2,1)S(1)}, u32[]{:S(2)}, u32[]{:S(2)}) collective-permute-start(bf16[4,128,256]{2,1,0:T(8,128)(2,1)S(1)} %get-tuple-element.65), channel_id=1, source_target_pairs={{0,24},{8,16},{16,8},{24,0},{1,25},{9,17},{17,9},{25,1},{2,26},{10... | collective-permute-start | bytes 786440 | tf_op jit(solution)/shard_map/ppermute | solution.py:377
  34.1 4.5 %collective-permute-done.11.refs_0_ = bf16[4,64,256]{2,1,0:T(8,128)(2,1)S(1)} collective-permute-done((bf16[4,64,256]{2,1,0:T(8,128)(2,1)S(1)}, bf16[4,64,256]{2,1,0:T(8,128)(2,1)S(1)}, u32[]{:S(2)}, u32[]{:S(2)}) %collective-permute-start.11) | collective-permute-done | bytes 131104 | tf_op jit(solution)/shard_map/ppermute | solution.py:377
  38.6 1.7 %collective-permute-start.13 = (bf16[4,64,256]{2,1,0:T(8,128)(2,1)S(1)}, bf16[4,64,256]{2,1,0:T(8,128)(2,1)S(1)}, u32[]{:S(2)}, u32[]{:S(2)}) collective-permute-start(bf16[4,64,256]{2,1,0:T(8,128)(2,1)S(1)} %get-tuple-element.61), channel_id=1, source_target_pairs={{0,4},{1,5},{2,6},{3,7},{4,0},{5,1},{6,2},{7,3},{8,12},{9,13},{10,... | collective-permute-start | bytes 393224 | tf_op jit(solution)/shard_map/ppermute | solution.py:377
  41.1 3.1 %collective-permute-done.15.refs_2_ = bf16[4,128,256]{2,1,0:T(8,128)(2,1)S(1)} collective-permute-done((bf16[4,128,256]{2,1,0:T(8,128)(2,1)S(1)}, bf16[4,128,256]{2,1,0:T(8,128)(2,1)S(1)}, u32[]{:S(2)}, u32[]{:S(2)}) %collective-permute-start.15) | collective-permute-done | bytes 262176 | tf_op jit(solution)/shard_map/ppermute | solution.py:377
  44.4 1.7 %collective-permute-start.19 = (bf16[512,256]{1,0:T(8,128)(2,1)S(1)}, bf16[512,256]{1,0:T(8,128)(2,1)S(1)}, u32[]{:S(2)}, u32[]{:S(2)}) collective-permute-start(bf16[512,256]{1,0:T(8,128)(2,1)S(1)} %get-tuple-element.66.refs_3_.refs_10_), channel_id=1, source_target_pairs={{0,24},{8,16},{16,8},{24,0},{1,25},{9,17},{17,9},{25,1},{2,26},{10... | collective-permute-start | bytes 786440 | tf_op jit(solution)/shard_map/ppermute | solution.py:377
  46.9 2.1 %collective-permute-start.18 = (bf16[256,256]{1,0:T(8,128)(2,1)S(1)}, bf16[256,256]{1,0:T(8,128)(2,1)S(1)}, u32[]{:S(2)}, u32[]{:S(2)}) collective-permute-start(bf16[256,256]{1,0:T(8,128)(2,1)S(1)} %get-tuple-element.68.refs_0_), channel_id=1, source_target_pairs={{0,4},{1,5},{2,6},{3,7},{4,0},{5,1},{6,2},{7,3},{8,12},{9,13},{10,... | collective-permute-start | bytes 393224 | tf_op jit(solution)/shard_map/ppermute | solution.py:377
  49.7 5.3 %collective-permute-done.18.refs_0_ = bf16[256,256]{1,0:T(8,128)(2,1)S(1)} collective-permute-done((bf16[256,256]{1,0:T(8,128)(2,1)S(1)}, bf16[256,256]{1,0:T(8,128)(2,1)S(1)}, u32[]{:S(2)}, u32[]{:S(2)}) %collective-permute-start.18) | collective-permute-done | bytes 131104 | tf_op jit(solution)/shard_map/ppermute | solution.py:377
  57.4 2.6 %collective-permute-done.20.refs_3_ = bf16[1,256,256]{2,1,0:T(8,128)(2,1)S(1)} collective-permute-done((bf16[1,256,256]{2,1,0:T(8,128)(2,1)S(1)}, bf16[1,256,256]{2,1,0:T(8,128)(2,1)S(1)}, u32[]{:S(2)}, u32[]{:S(2)}) %collective-permute-start.20) | collective-permute-done | bytes 131104 | tf_op jit(solution)/shard_map/ppermute | solution.py:377
  61.9 1.5 %collective-permute-done.24.refs_11_ = bf16[512,256]{1,0:T(8,128)(2,1)S(1)} collective-permute-done((bf16[512,256]{1,0:T(8,128)(2,1)S(1)}, bf16[512,256]{1,0:T(8,128)(2,1)S(1)}, u32[]{:S(2)}, u32[]{:S(2)}) %collective-permute-start.24) | collective-permute-done | bytes 262176 | tf_op jit(solution)/shard_map/ppermute | solution.py:377
  63.4 5.5 %shard_map.97 = (f32[4,4,64,256]{3,2,1,0:T(8,128)S(1)}, bf16[4,4,64,256]{3,2,1,0:T(8,128)(2,1)S(1)}, bf16[4,128,256]{2,1,0:T(8,128)(2,1)S(1)}, bf16[4,128,256]{2...) custom-call(s32[2,8]{1,0:T(2,128)S(1)} %bitcast.9, s32[1]{0:T(128)} %bitcast.7.refs_1_, ...), custom_call_target="tpu_custom_call" | custom-call | flops 3221225472 | bytes 16777216 | tf_op jit(solution)/shard_map/pallas_call | solution.py:285
  69.5 1.4 %collective-permute-done.26.got = bf16[4,4,64,256]{3,2,1,0:T(8,128)(2,1)S(1)} collective-permute-done((bf16[4,4,64,256]{3,2,1,0:T(8,128)(2,1)S(1)}, bf16[4,4,64,256]{3,2,1,0:T(8,128)(2,1)S(1)}, u32[]{:S(2)}, u32[]{:S(2)}) %collective-permute-start.26) | collective-permute-done | bytes 524320 | tf_op jit(solution)/shard_map/ppermute | solution.py:377
  71.0 1.2 %collective-permute-start.27 = (bf16[4,64,256]{2,1,0:T(8,128)(2,1)S(1)}, bf16[4,64,256]{2,1,0:T(8,128)(2,1)S(1)}, u32[]{:S(2)}, u32[]{:S(2)}) collective-permute-start(bf16[4,64,256]{2,1,0:T(8,128)(2,1)S(1)} %get-tuple-element.79), channel_id=1, source_target_pairs={{0,2},{1,3},{2,0},{3,1},{4,6},{5,7},{6,4},{7,5},{8,10},{9,11},{10,... | collective-permute-start | bytes 393224 | tf_op jit(solution)/shard_map/ppermute | solution.py:377
  72.2 1.5 %collective-permute-start.32 = (bf16[4,128,256]{2,1,0:T(8,128)(2,1)S(1)}, bf16[4,128,256]{2,1,0:T(8,128)(2,1)S(1)}, u32[]{:S(2)}, u32[]{:S(2)}) collective-permute-start(bf16[4,128,256]{2,1,0:T(8,128)(2,1)S(1)} %get-tuple-element.87), channel_id=1, source_target_pairs={{0,24},{8,16},{16,8},{24,0},{1,25},{9,17},{17,9},{25,1},{2,26},{10... | collective-permute-start | bytes 786440 | tf_op jit(solution)/shard_map/ppermute | solution.py:377
  73.8 2.9 %collective-permute-done.27.refs_0_ = bf16[4,64,256]{2,1,0:T(8,128)(2,1)S(1)} collective-permute-done((bf16[4,64,256]{2,1,0:T(8,128)(2,1)S(1)}, bf16[4,64,256]{2,1,0:T(8,128)(2,1)S(1)}, u32[]{:S(2)}, u32[]{:S(2)}) %collective-permute-start.27) | collective-permute-done | bytes 131104 | tf_op jit(solution)/shard_map/ppermute | solution.py:377
  78.5 4.8 %collective-permute-done.31.refs_2_ = bf16[4,128,256]{2,1,0:T(8,128)(2,1)S(1)} collective-permute-done((bf16[4,128,256]{2,1,0:T(8,128)(2,1)S(1)}, bf16[4,128,256]{2,1,0:T(8,128)(2,1)S(1)}, u32[]{:S(2)}, u32[]{:S(2)}) %collective-permute-start.31) | collective-permute-done | bytes 262176 | tf_op jit(solution)/shard_map/ppermute | solution.py:377
  (68 shorter events, 15.3 us)
Async XLA Ops:
  2.6 13.6 %collective-permute-start.1 = (bf16[272,256]{1,0:T(8,128)(2,1)}, bf16[272,256]{1,0:T(8,128)(2,1)S(1)}, u32[]{:S(2)}, u32[]{:S(2)}) collective-permute-start(bf16[272,256]{1,0:T(8,128)(2,1)} %get-tuple-element.47.refs_0_), channel_id=1, source_target_pairs={{0,4},{1,5},{2,6},{3,7},{4,0},{5,1},{6,2},{7,3},{8,12},{9,13},{10,... | collective-permute-start | bytes 417800 | tf_op jit(solution)/shard_map/ppermute | solution.py:377
  6.7 10.3 %collective-permute-start.4 = (bf16[528,256]{1,0:T(8,128)(2,1)}, bf16[528,256]{1,0:T(8,128)(2,1)S(1)}, u32[]{:S(2)}, u32[]{:S(2)}) collective-permute-start(bf16[528,256]{1,0:T(8,128)(2,1)} %get-tuple-element.49.refs_12_), channel_id=1, source_target_pairs={{0,16},{8,24},{16,0},{24,8},{1,17},{9,25},{17,1},{25,9},{2,18},{10... | collective-permute-start | bytes 811016 | tf_op jit(solution)/shard_map/ppermute | solution.py:377
  8.2 8.8 %collective-permute-start.3 = (bf16[528,256]{1,0:T(8,128)(2,1)}, bf16[528,256]{1,0:T(8,128)(2,1)S(1)}, u32[]{:S(2)}, u32[]{:S(2)}) collective-permute-start(bf16[528,256]{1,0:T(8,128)(2,1)} %get-tuple-element.49.refs_12_), channel_id=1, source_target_pairs={{0,8},{8,0},{16,24},{24,16},{1,9},{9,1},{17,25},{25,17},{2,10},{10... | collective-permute-start | bytes 811016 | tf_op jit(solution)/shard_map/ppermute | solution.py:377
  9.7 7.3 %collective-permute-start = (bf16[272,256]{1,0:T(8,128)(2,1)}, bf16[272,256]{1,0:T(8,128)(2,1)S(1)}, u32[]{:S(2)}, u32[]{:S(2)}) collective-permute-start(bf16[272,256]{1,0:T(8,128)(2,1)} %get-tuple-element.47.refs_0_), channel_id=1, source_target_pairs={{0,2},{1,3},{2,0},{3,1},{4,6},{5,7},{6,4},{7,5},{8,10},{9,11},{10,... | collective-permute-start | bytes 417800 | tf_op jit(solution)/shard_map/ppermute | solution.py:377
  16.2 5.1 %collective-permute-start.2 = (bf16[1,272,256]{2,1,0:T(8,128)(2,1)S(1)}, bf16[1,272,256]{2,1,0:T(8,128)(2,1)S(1)}, u32[]{:S(2)}, u32[]{:S(2)}) collective-permute-start(bf16[1,272,256]{2,1,0:T(8,128)(2,1)S(1)} %shard_map.88.refs_2_), channel_id=1, source_target_pairs={{0,2},{1,3},{2,0},{3,1},{4,6},{5,7},{6,4},{7,5},{8,10},{9,11},{10,... | collective-permute-start | bytes 417800 | tf_op jit(solution)/shard_map/ppermute | solution.py:377
  16.3 7.6 %collective-permute-start.9 = (bf16[528,256]{1,0:T(8,128)(2,1)S(1)}, bf16[528,256]{1,0:T(8,128)(2,1)S(1)}, u32[]{:S(2)}, u32[]{:S(2)}) collective-permute-start(bf16[528,256]{1,0:T(8,128)(2,1)S(1)} %copy-done.2), channel_id=1, source_target_pairs={{0,24},{8,16},{16,8},{24,0},{1,25},{9,17},{17,9},{25,1},{2,26},{10... | collective-permute-start | bytes 811016 | tf_op jit(solution)/shard_map/ppermute | solution.py:377
  29.9 11.2 %collective-permute-start.14 = (bf16[4,128,256]{2,1,0:T(8,128)(2,1)S(1)}, bf16[4,128,256]{2,1,0:T(8,128)(2,1)S(1)}, u32[]{:S(2)}, u32[]{:S(2)}) collective-permute-start(bf16[4,128,256]{2,1,0:T(8,128)(2,1)S(1)} %get-tuple-element.63), channel_id=1, source_target_pairs={{0,8},{8,0},{16,24},{24,16},{1,9},{9,1},{17,25},{25,17},{2,10},{10... | collective-permute-start | bytes 786440 | tf_op jit(solution)/shard_map/ppermute | solution.py:377
  29.9 14.2 %collective-permute-start.15 = (bf16[4,128,256]{2,1,0:T(8,128)(2,1)S(1)}, bf16[4,128,256]{2,1,0:T(8,128)(2,1)S(1)}, u32[]{:S(2)}, u32[]{:S(2)}) collective-permute-start(bf16[4,128,256]{2,1,0:T(8,128)(2,1)S(1)} %get-tuple-element.64), channel_id=1, source_target_pairs={{0,16},{8,24},{16,0},{24,8},{1,17},{9,25},{17,1},{25,9},{2,18},{10... | collective-permute-start | bytes 786440 | tf_op jit(solution)/shard_map/ppermute | solution.py:377
  30.7 13.5 %collective-permute-start.16 = (bf16[4,128,256]{2,1,0:T(8,128)(2,1)S(1)}, bf16[4,128,256]{2,1,0:T(8,128)(2,1)S(1)}, u32[]{:S(2)}, u32[]{:S(2)}) collective-permute-start(bf16[4,128,256]{2,1,0:T(8,128)(2,1)S(1)} %get-tuple-element.65), channel_id=1, source_target_pairs={{0,24},{8,16},{16,8},{24,0},{1,25},{9,17},{17,9},{25,1},{2,26},{10... | collective-permute-start | bytes 786440 | tf_op jit(solution)/shard_map/ppermute | solution.py:377
  33.5 5.1 %collective-permute-start.11 = (bf16[4,64,256]{2,1,0:T(8,128)(2,1)S(1)}, bf16[4,64,256]{2,1,0:T(8,128)(2,1)S(1)}, u32[]{:S(2)}, u32[]{:S(2)}) collective-permute-start(bf16[4,64,256]{2,1,0:T(8,128)(2,1)S(1)} %get-tuple-element.58), channel_id=1, source_target_pairs={{0,2},{1,3},{2,0},{3,1},{4,6},{5,7},{6,4},{7,5},{8,10},{9,11},{10,... | collective-permute-start | bytes 393224 | tf_op jit(solution)/shard_map/ppermute | solution.py:377
  38.6 8.0 %collective-permute-start.13 = (bf16[4,64,256]{2,1,0:T(8,128)(2,1)S(1)}, bf16[4,64,256]{2,1,0:T(8,128)(2,1)S(1)}, u32[]{:S(2)}, u32[]{:S(2)}) collective-permute-start(bf16[4,64,256]{2,1,0:T(8,128)(2,1)S(1)} %get-tuple-element.61), channel_id=1, source_target_pairs={{0,4},{1,5},{2,6},{3,7},{4,0},{5,1},{6,2},{7,3},{8,12},{9,13},{10,... | collective-permute-start | bytes 393224 | tf_op jit(solution)/shard_map/ppermute | solution.py:377
  40.4 6.4 %collective-permute-start.12 = (bf16[4,64,256]{2,1,0:T(8,128)(2,1)S(1)}, bf16[4,64,256]{2,1,0:T(8,128)(2,1)S(1)}, u32[]{:S(2)}, u32[]{:S(2)}) collective-permute-start(bf16[4,64,256]{2,1,0:T(8,128)(2,1)S(1)} %get-tuple-element.60.refs_4_), channel_id=1, source_target_pairs={{0,2},{1,3},{2,0},{3,1},{4,6},{5,7},{6,4},{7,5},{8,10},{9,11},{10,... | collective-permute-start | bytes 393224 | tf_op jit(solution)/shard_map/ppermute | solution.py:377
  44.4 10.6 %collective-permute-start.19 = (bf16[512,256]{1,0:T(8,128)(2,1)S(1)}, bf16[512,256]{1,0:T(8,128)(2,1)S(1)}, u32[]{:S(2)}, u32[]{:S(2)}) collective-permute-start(bf16[512,256]{1,0:T(8,128)(2,1)S(1)} %get-tuple-element.66.refs_3_.refs_10_), channel_id=1, source_target_pairs={{0,24},{8,16},{16,8},{24,0},{1,25},{9,17},{17,9},{25,1},{2,26},{10... | collective-permute-start | bytes 786440 | tf_op jit(solution)/shard_map/ppermute | solution.py:377
  46.9 8.1 %collective-permute-start.18 = (bf16[256,256]{1,0:T(8,128)(2,1)S(1)}, bf16[256,256]{1,0:T(8,128)(2,1)S(1)}, u32[]{:S(2)}, u32[]{:S(2)}) collective-permute-start(bf16[256,256]{1,0:T(8,128)(2,1)S(1)} %get-tuple-element.68.refs_0_), channel_id=1, source_target_pairs={{0,4},{1,5},{2,6},{3,7},{4,0},{5,1},{6,2},{7,3},{8,12},{9,13},{10,... | collective-permute-start | bytes 393224 | tf_op jit(solution)/shard_map/ppermute | solution.py:377
  49.0 8.4 %collective-permute-start.17 = (bf16[256,256]{1,0:T(8,128)(2,1)S(1)}, bf16[256,256]{1,0:T(8,128)(2,1)S(1)}, u32[]{:S(2)}, u32[]{:S(2)}) collective-permute-start(bf16[256,256]{1,0:T(8,128)(2,1)S(1)} %get-tuple-element.68.refs_0_), channel_id=1, source_target_pairs={{0,2},{1,3},{2,0},{3,1},{4,6},{5,7},{6,4},{7,5},{8,10},{9,11},{10,... | collective-permute-start | bytes 393224 | tf_op jit(solution)/shard_map/ppermute | solution.py:377
  55.0 5.0 %collective-permute-start.20 = (bf16[1,256,256]{2,1,0:T(8,128)(2,1)S(1)}, bf16[1,256,256]{2,1,0:T(8,128)(2,1)S(1)}, u32[]{:S(2)}, u32[]{:S(2)}) collective-permute-start(bf16[1,256,256]{2,1,0:T(8,128)(2,1)S(1)} %shard_map.95.refs_2_), channel_id=1, source_target_pairs={{0,2},{1,3},{2,0},{3,1},{4,6},{5,7},{6,4},{7,5},{8,10},{9,11},{10,... | collective-permute-start | bytes 393224 | tf_op jit(solution)/shard_map/ppermute | solution.py:377
  55.2 6.7 %collective-permute-start.25 = (bf16[512,256]{1,0:T(8,128)(2,1)S(1)}, bf16[512,256]{1,0:T(8,128)(2,1)S(1)}, u32[]{:S(2)}, u32[]{:S(2)}) collective-permute-start(bf16[512,256]{1,0:T(8,128)(2,1)S(1)} %get-tuple-element.66.refs_3_.refs_10_), channel_id=1, source_target_pairs={{0,16},{8,24},{16,0},{24,8},{1,17},{9,25},{17,1},{25,9},{2,18},{10... | collective-permute-start | bytes 786440 | tf_op jit(solution)/shard_map/ppermute | solution.py:377
  56.3 7.1 %collective-permute-start.24 = (bf16[512,256]{1,0:T(8,128)(2,1)S(1)}, bf16[512,256]{1,0:T(8,128)(2,1)S(1)}, u32[]{:S(2)}, u32[]{:S(2)}) collective-permute-start(bf16[512,256]{1,0:T(8,128)(2,1)S(1)} %get-tuple-element.66.refs_3_.refs_10_), channel_id=1, source_target_pairs={{0,8},{8,0},{16,24},{24,16},{1,9},{9,1},{17,25},{25,17},{2,10},{10... | collective-permute-start | bytes 786440 | tf_op jit(solution)/shard_map/ppermute | solution.py:377
  69.0 9.5 %collective-permute-start.30 = (bf16[4,128,256]{2,1,0:T(8,128)(2,1)S(1)}, bf16[4,128,256]{2,1,0:T(8,128)(2,1)S(1)}, u32[]{:S(2)}, u32[]{:S(2)}) collective-permute-start(bf16[4,128,256]{2,1,0:T(8,128)(2,1)S(1)} %get-tuple-element.85), channel_id=1, source_target_pairs={{0,8},{8,0},{16,24},{24,16},{1,9},{9,1},{17,25},{25,17},{2,10},{10... | collective-permute-start | bytes 786440 | tf_op jit(solution)/shard_map/ppermute | solution.py:377
  69.1 14.2 %collective-permute-start.31 = (bf16[4,128,256]{2,1,0:T(8,128)(2,1)S(1)}, bf16[4,128,256]{2,1,0:T(8,128)(2,1)S(1)}, u32[]{:S(2)}, u32[]{:S(2)}) collective-permute-start(bf16[4,128,256]{2,1,0:T(8,128)(2,1)S(1)} %get-tuple-element.86), channel_id=1, source_target_pairs={{0,16},{8,24},{16,0},{24,8},{1,17},{9,25},{17,1},{25,9},{2,18},{10... | collective-permute-start | bytes 786440 | tf_op jit(solution)/shard_map/ppermute | solution.py:377
  71.0 5.6 %collective-permute-start.27 = (bf16[4,64,256]{2,1,0:T(8,128)(2,1)S(1)}, bf16[4,64,256]{2,1,0:T(8,128)(2,1)S(1)}, u32[]{:S(2)}, u32[]{:S(2)}) collective-permute-start(bf16[4,64,256]{2,1,0:T(8,128)(2,1)S(1)} %get-tuple-element.79), channel_id=1, source_target_pairs={{0,2},{1,3},{2,0},{3,1},{4,6},{5,7},{6,4},{7,5},{8,10},{9,11},{10,... | collective-permute-start | bytes 393224 | tf_op jit(solution)/shard_map/ppermute | solution.py:377
  72.2 11.1 %collective-permute-start.32 = (bf16[4,128,256]{2,1,0:T(8,128)(2,1)S(1)}, bf16[4,128,256]{2,1,0:T(8,128)(2,1)S(1)}, u32[]{:S(2)}, u32[]{:S(2)}) collective-permute-start(bf16[4,128,256]{2,1,0:T(8,128)(2,1)S(1)} %get-tuple-element.87), channel_id=1, source_target_pairs={{0,24},{8,16},{16,8},{24,0},{1,25},{9,17},{17,9},{25,1},{2,26},{10... | collective-permute-start | bytes 786440 | tf_op jit(solution)/shard_map/ppermute | solution.py:377
  76.7 8.5 %collective-permute-start.29 = (bf16[4,64,256]{2,1,0:T(8,128)(2,1)S(1)}, bf16[4,64,256]{2,1,0:T(8,128)(2,1)S(1)}, u32[]{:S(2)}, u32[]{:S(2)}) collective-permute-start(bf16[4,64,256]{2,1,0:T(8,128)(2,1)S(1)} %get-tuple-element.82), channel_id=1, source_target_pairs={{0,4},{1,5},{2,6},{3,7},{4,0},{5,1},{6,2},{7,3},{8,12},{9,13},{10,... | collective-permute-start | bytes 393224 | tf_op jit(solution)/shard_map/ppermute | solution.py:377
  77.3 7.8 %collective-permute-start.28 = (bf16[4,64,256]{2,1,0:T(8,128)(2,1)S(1)}, bf16[4,64,256]{2,1,0:T(8,128)(2,1)S(1)}, u32[]{:S(2)}, u32[]{:S(2)}) collective-permute-start(bf16[4,64,256]{2,1,0:T(8,128)(2,1)S(1)} %get-tuple-element.81.refs_3_.refs_4_), channel_id=1, source_target_pairs={{0,2},{1,3},{2,0},{3,1},{4,6},{5,7},{6,4},{7,5},{8,10},{9,11},{10,... | collective-permute-start | bytes 393224 | tf_op jit(solution)/shard_map/ppermute | solution.py:377
  (14 other events, 122.6 us)

commit v10 on v9

--- a/solution.py
+++ b/solution.py
@@ -201,7 +201,8 @@
             row_panel[i, rows, :], col_panel[j], (((1,), (1,)), ((), ())), preferred_element_type=f32
         )
         marg_left = jnp.concatenate([left[i, rows, :]] * (size // 128), axis=1)
-        diff = (scores + marg_left + right[j, 0:1, :] - logs[slot, rows, :]).astype(bf16)
+        shift = marg_left + right[j, 0:1, :] - logs[slot, rows, :]
+        diff = (scores + shift).astype(bf16)
         weight = weights[slot, rows, :]
         half_one = jnp.asarray(0.5, bf16)
         flat = half_one * jnp.tanh(half_one * diff) + half_one

time: 86.1 us -> 87.3 us (1.014); the launches traced: 85.9 us -> 85.9 us
  starting transfers between devices: 29.7 us -> 40 us
  Pallas kernels: 19.8 us -> 14 us
  waiting for transfers between devices: 34.8 us -> 30.4 us
    ppermute x33, starting transfers between devices: 29.7 us -> 40 us  [send(): return lax.ppermute(x, axis, [(k, k ^ mask) for k in range(count)])]
    ppermute x33, waiting for transfers between devices: 34.8 us -> 30.4 us  [send(): return lax.ppermute(x, axis, [(k, k ^ mask) for k in range(count)])]
    pallas_call x2, Pallas kernels: 11.3 us -> 7.2 us  [work(): pl.pallas_call(functools.partial(work_kernel, first, len(row_in), n_row,...]
    pallas_call x1, Pallas kernels: 4.21 us -> 2.54 us  [levels(): pl.pallas_call(levels_kernel, out_shape=[shape(tiles.shape, f32), shape(t...]
  transfers between devices with their start and end apart: 33 -> 33, of which waited for: 14 -> 13; matrix products, arithmetic and copies ran while one was open for 0% -> 0% of each run, Pallas kernels for 7% -> 5%
where the time goes in v10:
time: 87.3 us; the launch traced here: 85.9 us
  starting transfers between devices  40 us (46%)
  waiting for transfers between devices  30.4 us (35%)
  Pallas kernels  14 us (16%)
  between operations  1.52 us (2%)
    ppermute x33, starting transfers between devices, send(): return lax.ppermute(x, axis, [(k, k ^ mask) for k in range(count)])  40 us
    ppermute x33, waiting for transfers between devices, send(): return lax.ppermute(x, axis, [(k, k ^ mask) for k in range(count)])  30.4 us
    pallas_call x2, Pallas kernels, work(): pl.pallas_call(functools.partial(work_kernel, first, len(row_in), n_row,...  7.2 us
    pallas_call x1, Pallas kernels, levels(): pl.pallas_call(levels_kernel, out_shape=[shape(tiles.shape, f32), shape(t...  2.54 us
    pallas_call x4, Pallas kernels, update(): pl.pallas_call(functools.partial(update_kernel, len(parts), len(outs)), o...  1.98 us
    pallas_call x1, Pallas kernels, pack(): pl.pallas_call(pack_kernel, out_shape=[shape((e.shape[0] * e.shape[1] + M...  1.93 us
  transfers between devices with their start and end apart: 33, of which 13 were waited for; matrix products, arithmetic and copies ran while one was open for 0% of the time, Pallas kernels for 5%

profile of v10, /device:TPU:0, one launch (start us, length us, event | category | flops | bytes accessed | tf_op | source)
XLA Modules:
  0.0 85.9 jit_solution(7406575675126548207)
XLA Ops:
  0.6 1.9 %shard_map.87 = (bf16[272,256]{1,0:T(8,128)(2,1)}, bf16[528,256]{1,0:T(8,128)(2,1)}) custom-call(f32[4,64,256]{2,1,0:T(8,128)} %emb.3, bf16[4,64]{1,0:T(4,128)(2,1)} %row_marg.1, f32[4,128,256]{2,1,0:T(8,128)} %emb.2, bf16[4,128]{1,0:T(4,128)(2,1)} %col_marg.1), custom_call_target="tpu_custom_call" | custom-call | bytes 1048576 | tf_op jit(solution)/shard_map/pallas_call | solution.py:50
  2.6 4.1 %collective-permute-start.1 = (bf16[272,256]{1,0:T(8,128)(2,1)}, bf16[272,256]{1,0:T(8,128)(2,1)S(1)}, u32[]{:S(2)}, u32[]{:S(2)}) collective-permute-start(bf16[272,256]{1,0:T(8,128)(2,1)} %get-tuple-element.47.refs_0_), channel_id=1, source_target_pairs={{0,4},{1,5},{2,6},{3,7},{4,0},{5,1},{6,2},{7,3},{8,12},{9,13},{10,... | collective-permute-start | bytes 417800 | tf_op jit(solution)/shard_map/ppermute | solution.py:378
  11.9 2.5 %shard_map.86 = (f32[8,512,512]{2,1,0:T(8,128)S(1)}, bf16[8,512,512]{2,1,0:T(8,128)(2,1)S(1)}, f32[8,128]{1,0:T(8,128)S(1)}) custom-call(s32[1]{0:T(128)} %bitcast.5.used, s32[8,512,512]{2,1,0:T(8,128)} %bitcast.10), custom_call_target="tpu_custom_call" | custom-call | bytes 12582912 | tf_op jit(solution)/shard_map/pallas_call | solution.py:99
  14.5 2.6 %collective-permute-start.2 = (bf16[1,272,256]{2,1,0:T(8,128)(2,1)S(1)}, bf16[1,272,256]{2,1,0:T(8,128)(2,1)S(1)}, u32[]{:S(2)}, u32[]{:S(2)}) collective-permute-start(bf16[1,272,256]{2,1,0:T(8,128)(2,1)S(1)} %shard_map.88.refs_2_), channel_id=1, source_target_pairs={{0,2},{1,3},{2,0},{3,1},{4,6},{5,7},{6,4},{7,5},{8,10},{9,11},{10,... | collective-permute-start | bytes 417800 | tf_op jit(solution)/shard_map/ppermute | solution.py:378
  17.2 3.0 %collective-permute-done.2.refs_3_ = bf16[1,272,256]{2,1,0:T(8,128)(2,1)S(1)} collective-permute-done((bf16[1,272,256]{2,1,0:T(8,128)(2,1)S(1)}, bf16[1,272,256]{2,1,0:T(8,128)(2,1)S(1)}, u32[]{:S(2)}, u32[]{:S(2)}) %collective-permute-start.2) | collective-permute-done | bytes 139296 | tf_op jit(solution)/shard_map/ppermute | solution.py:378
  21.3 3.2 %collective-permute-done.9.refs_15_ = bf16[528,256]{1,0:T(8,128)(2,1)S(1)} collective-permute-done((bf16[528,256]{1,0:T(8,128)(2,1)S(1)}, bf16[528,256]{1,0:T(8,128)(2,1)S(1)}, u32[]{:S(2)}, u32[]{:S(2)}) %collective-permute-start.9) | collective-permute-done | bytes 270368 | tf_op jit(solution)/shard_map/ppermute | solution.py:378
  24.5 3.7 %shard_map.90 = (f32[4,4,64,256]{3,2,1,0:T(8,128)S(1)}, bf16[4,4,64,256]{3,2,1,0:T(8,128)(2,1)S(1)}, bf16[4,128,256]{2,1,0:T(8,128)(2,1)S(1)}, bf16[4,128,256]{2...) custom-call(s32[2,8]{1,0:T(2,128)S(1)} %bitcast.8, ...), custom_call_target="tpu_custom_call" | custom-call | flops 3221225472 | bytes 16777216 | tf_op jit(solution)/shard_map/pallas_call | solution.py:286
  28.4 1.8 %collective-permute-start.15 = (bf16[4,128,256]{2,1,0:T(8,128)(2,1)S(1)}, bf16[4,128,256]{2,1,0:T(8,128)(2,1)S(1)}, u32[]{:S(2)}, u32[]{:S(2)}) collective-permute-start(bf16[4,128,256]{2,1,0:T(8,128)(2,1)S(1)} %get-tuple-element.64), channel_id=1, source_target_pairs={{0,16},{8,24},{16,0},{24,8},{1,17},{9,25},{17,1},{25,9},{2,18},{10... | collective-permute-start | bytes 786440 | tf_op jit(solution)/shard_map/ppermute | solution.py:378
  30.2 1.7 %collective-permute-start.16 = (bf16[4,128,256]{2,1,0:T(8,128)(2,1)S(1)}, bf16[4,128,256]{2,1,0:T(8,128)(2,1)S(1)}, u32[]{:S(2)}, u32[]{:S(2)}) collective-permute-start(bf16[4,128,256]{2,1,0:T(8,128)(2,1)S(1)} %get-tuple-element.65), channel_id=1, source_target_pairs={{0,24},{8,16},{16,8},{24,0},{1,25},{9,17},{17,9},{25,1},{2,26},{10... | collective-permute-start | bytes 786440 | tf_op jit(solution)/shard_map/ppermute | solution.py:378
  32.0 3.6 %collective-permute-start.11 = (bf16[4,64,256]{2,1,0:T(8,128)(2,1)S(1)}, bf16[4,64,256]{2,1,0:T(8,128)(2,1)S(1)}, u32[]{:S(2)}, u32[]{:S(2)}) collective-permute-start(bf16[4,64,256]{2,1,0:T(8,128)(2,1)S(1)} %get-tuple-element.58), channel_id=1, source_target_pairs={{0,2},{1,3},{2,0},{3,1},{4,6},{5,7},{6,4},{7,5},{8,10},{9,11},{10,... | collective-permute-start | bytes 393224 | tf_op jit(solution)/shard_map/ppermute | solution.py:378
  35.7 3.3 %collective-permute-done.11.refs_0_ = bf16[4,64,256]{2,1,0:T(8,128)(2,1)S(1)} collective-permute-done((bf16[4,64,256]{2,1,0:T(8,128)(2,1)S(1)}, bf16[4,64,256]{2,1,0:T(8,128)(2,1)S(1)}, u32[]{:S(2)}, u32[]{:S(2)}) %collective-permute-start.11) | collective-permute-done | bytes 131104 | tf_op jit(solution)/shard_map/ppermute | solution.py:378
  39.7 1.7 %collective-permute-start.12 = (bf16[4,64,256]{2,1,0:T(8,128)(2,1)S(1)}, bf16[4,64,256]{2,1,0:T(8,128)(2,1)S(1)}, u32[]{:S(2)}, u32[]{:S(2)}) collective-permute-start(bf16[4,64,256]{2,1,0:T(8,128)(2,1)S(1)} %get-tuple-element.60.refs_4_), channel_id=1, source_target_pairs={{0,2},{1,3},{2,0},{3,1},{4,6},{5,7},{6,4},{7,5},{8,10},{9,11},{10,... | collective-permute-start | bytes 393224 | tf_op jit(solution)/shard_map/ppermute | solution.py:378
  41.5 2.4 %collective-permute-done.16.refs_3_ = bf16[4,128,256]{2,1,0:T(8,128)(2,1)S(1)} collective-permute-done((bf16[4,128,256]{2,1,0:T(8,128)(2,1)S(1)}, bf16[4,128,256]{2,1,0:T(8,128)(2,1)S(1)}, u32[]{:S(2)}, u32[]{:S(2)}) %collective-permute-start.16) | collective-permute-done | bytes 262176 | tf_op jit(solution)/shard_map/ppermute | solution.py:378
  44.0 1.8 %collective-permute-start.19 = (bf16[512,256]{1,0:T(8,128)(2,1)S(1)}, bf16[512,256]{1,0:T(8,128)(2,1)S(1)}, u32[]{:S(2)}, u32[]{:S(2)}) collective-permute-start(bf16[512,256]{1,0:T(8,128)(2,1)S(1)} %get-tuple-element.66.refs_3_.refs_10_), channel_id=1, source_target_pairs={{0,24},{8,16},{16,8},{24,0},{1,25},{9,17},{17,9},{25,1},{2,26},{10... | collective-permute-start | bytes 786440 | tf_op jit(solution)/shard_map/ppermute | solution.py:378
  50.4 3.9 %collective-permute-done.18.refs_0_ = bf16[256,256]{1,0:T(8,128)(2,1)S(1)} collective-permute-done((bf16[256,256]{1,0:T(8,128)(2,1)S(1)}, bf16[256,256]{1,0:T(8,128)(2,1)S(1)}, u32[]{:S(2)}, u32[]{:S(2)}) %collective-permute-start.18) | collective-permute-done | bytes 131104 | tf_op jit(solution)/shard_map/ppermute | solution.py:378
  57.4 2.0 %collective-permute-done.20.refs_3_ = bf16[1,256,256]{2,1,0:T(8,128)(2,1)S(1)} collective-permute-done((bf16[1,256,256]{2,1,0:T(8,128)(2,1)S(1)}, bf16[1,256,256]{2,1,0:T(8,128)(2,1)S(1)}, u32[]{:S(2)}, u32[]{:S(2)}) %collective-permute-start.20) | collective-permute-done | bytes 131104 | tf_op jit(solution)/shard_map/ppermute | solution.py:378
  60.0 1.8 %collective-permute-done.25.refs_12_ = bf16[512,256]{1,0:T(8,128)(2,1)S(1)} collective-permute-done((bf16[512,256]{1,0:T(8,128)(2,1)S(1)}, bf16[512,256]{1,0:T(8,128)(2,1)S(1)}, u32[]{:S(2)}, u32[]{:S(2)}) %collective-permute-start.25) | collective-permute-done | bytes 262176 | tf_op jit(solution)/shard_map/ppermute | solution.py:378
  63.3 3.5 %shard_map.97 = (f32[4,4,64,256]{3,2,1,0:T(8,128)S(1)}, bf16[4,4,64,256]{3,2,1,0:T(8,128)(2,1)S(1)}, bf16[4,128,256]{2,1,0:T(8,128)(2,1)S(1)}, bf16[4,128,256]{2...) custom-call(s32[2,8]{1,0:T(2,128)S(1)} %bitcast.9, s32[1]{0:T(128)} %bitcast.7.refs_1_, ...), custom_call_target="tpu_custom_call" | custom-call | flops 3221225472 | bytes 16777216 | tf_op jit(solution)/shard_map/pallas_call | solution.py:286
  68.9 3.7 %collective-permute-start.27 = (bf16[4,64,256]{2,1,0:T(8,128)(2,1)S(1)}, bf16[4,64,256]{2,1,0:T(8,128)(2,1)S(1)}, u32[]{:S(2)}, u32[]{:S(2)}) collective-permute-start(bf16[4,64,256]{2,1,0:T(8,128)(2,1)S(1)} %get-tuple-element.79), channel_id=1, source_target_pairs={{0,2},{1,3},{2,0},{3,1},{4,6},{5,7},{6,4},{7,5},{8,10},{9,11},{10,... | collective-permute-start | bytes 393224 | tf_op jit(solution)/shard_map/ppermute | solution.py:378
  72.5 1.7 %collective-permute-start.32 = (bf16[4,128,256]{2,1,0:T(8,128)(2,1)S(1)}, bf16[4,128,256]{2,1,0:T(8,128)(2,1)S(1)}, u32[]{:S(2)}, u32[]{:S(2)}) collective-permute-start(bf16[4,128,256]{2,1,0:T(8,128)(2,1)S(1)} %get-tuple-element.87), channel_id=1, source_target_pairs={{0,24},{8,16},{16,8},{24,0},{1,25},{9,17},{17,9},{25,1},{2,26},{10... | collective-permute-start | bytes 786440 | tf_op jit(solution)/shard_map/ppermute | solution.py:378
  74.2 2.1 %collective-permute-done.27.refs_0_ = bf16[4,64,256]{2,1,0:T(8,128)(2,1)S(1)} collective-permute-done((bf16[4,64,256]{2,1,0:T(8,128)(2,1)S(1)}, bf16[4,64,256]{2,1,0:T(8,128)(2,1)S(1)}, u32[]{:S(2)}, u32[]{:S(2)}) %collective-permute-start.27) | collective-permute-done | bytes 131104 | tf_op jit(solution)/shard_map/ppermute | solution.py:378
  76.8 1.7 %collective-permute-start.28 = (bf16[4,64,256]{2,1,0:T(8,128)(2,1)S(1)}, bf16[4,64,256]{2,1,0:T(8,128)(2,1)S(1)}, u32[]{:S(2)}, u32[]{:S(2)}) collective-permute-start(bf16[4,64,256]{2,1,0:T(8,128)(2,1)S(1)} %get-tuple-element.81.refs_3_.refs_4_), channel_id=1, source_target_pairs={{0,2},{1,3},{2,0},{3,1},{4,6},{5,7},{6,4},{7,5},{8,10},{9,11},{10,... | collective-permute-start | bytes 393224 | tf_op jit(solution)/shard_map/ppermute | solution.py:378
  78.5 3.6 %collective-permute-done.32.refs_3_ = bf16[4,128,256]{2,1,0:T(8,128)(2,1)S(1)} collective-permute-done((bf16[4,128,256]{2,1,0:T(8,128)(2,1)S(1)}, bf16[4,128,256]{2,1,0:T(8,128)(2,1)S(1)}, u32[]{:S(2)}, u32[]{:S(2)}) %collective-permute-start.32) | collective-permute-done | bytes 262176 | tf_op jit(solution)/shard_map/ppermute | solution.py:378
  83.1 2.1 %collective-permute-done.29.refs_2_ = bf16[4,64,256]{2,1,0:T(8,128)(2,1)S(1)} collective-permute-done((bf16[4,64,256]{2,1,0:T(8,128)(2,1)S(1)}, bf16[4,64,256]{2,1,0:T(8,128)(2,1)S(1)}, u32[]{:S(2)}, u32[]{:S(2)}) %collective-permute-start.29) | collective-permute-done | bytes 131104 | tf_op jit(solution)/shard_map/ppermute | solution.py:378
  (68 shorter events, 20.9 us)
Async XLA Ops:
  2.6 11.9 %collective-permute-start.1 = (bf16[272,256]{1,0:T(8,128)(2,1)}, bf16[272,256]{1,0:T(8,128)(2,1)S(1)}, u32[]{:S(2)}, u32[]{:S(2)}) collective-permute-start(bf16[272,256]{1,0:T(8,128)(2,1)} %get-tuple-element.47.refs_0_), channel_id=1, source_target_pairs={{0,4},{1,5},{2,6},{3,7},{4,0},{5,1},{6,2},{7,3},{8,12},{9,13},{10,... | collective-permute-start | bytes 417800 | tf_op jit(solution)/shard_map/ppermute | solution.py:378
  6.7 10.4 %collective-permute-start.4 = (bf16[528,256]{1,0:T(8,128)(2,1)}, bf16[528,256]{1,0:T(8,128)(2,1)S(1)}, u32[]{:S(2)}, u32[]{:S(2)}) collective-permute-start(bf16[528,256]{1,0:T(8,128)(2,1)} %get-tuple-element.49.refs_12_), channel_id=1, source_target_pairs={{0,16},{8,24},{16,0},{24,8},{1,17},{9,25},{17,1},{25,9},{2,18},{10... | collective-permute-start | bytes 811016 | tf_op jit(solution)/shard_map/ppermute | solution.py:378
  8.2 8.9 %collective-permute-start.3 = (bf16[528,256]{1,0:T(8,128)(2,1)}, bf16[528,256]{1,0:T(8,128)(2,1)S(1)}, u32[]{:S(2)}, u32[]{:S(2)}) collective-permute-start(bf16[528,256]{1,0:T(8,128)(2,1)} %get-tuple-element.49.refs_12_), channel_id=1, source_target_pairs={{0,8},{8,0},{16,24},{24,16},{1,9},{9,1},{17,25},{25,17},{2,10},{10... | collective-permute-start | bytes 811016 | tf_op jit(solution)/shard_map/ppermute | solution.py:378
  9.7 7.4 %collective-permute-start = (bf16[272,256]{1,0:T(8,128)(2,1)}, bf16[272,256]{1,0:T(8,128)(2,1)S(1)}, u32[]{:S(2)}, u32[]{:S(2)}) collective-permute-start(bf16[272,256]{1,0:T(8,128)(2,1)} %get-tuple-element.47.refs_0_), channel_id=1, source_target_pairs={{0,2},{1,3},{2,0},{3,1},{4,6},{5,7},{6,4},{7,5},{8,10},{9,11},{10,... | collective-permute-start | bytes 417800 | tf_op jit(solution)/shard_map/ppermute | solution.py:378
  14.5 5.6 %collective-permute-start.2 = (bf16[1,272,256]{2,1,0:T(8,128)(2,1)S(1)}, bf16[1,272,256]{2,1,0:T(8,128)(2,1)S(1)}, u32[]{:S(2)}, u32[]{:S(2)}) collective-permute-start(bf16[1,272,256]{2,1,0:T(8,128)(2,1)S(1)} %shard_map.88.refs_2_), channel_id=1, source_target_pairs={{0,2},{1,3},{2,0},{3,1},{4,6},{5,7},{6,4},{7,5},{8,10},{9,11},{10,... | collective-permute-start | bytes 417800 | tf_op jit(solution)/shard_map/ppermute | solution.py:378
  17.1 7.4 %collective-permute-start.9 = (bf16[528,256]{1,0:T(8,128)(2,1)S(1)}, bf16[528,256]{1,0:T(8,128)(2,1)S(1)}, u32[]{:S(2)}, u32[]{:S(2)}) collective-permute-start(bf16[528,256]{1,0:T(8,128)(2,1)S(1)} %copy-done.2), channel_id=1, source_target_pairs={{0,24},{8,16},{16,8},{24,0},{1,25},{9,17},{17,9},{25,1},{2,26},{10... | collective-permute-start | bytes 811016 | tf_op jit(solution)/shard_map/ppermute | solution.py:378
  28.4 13.1 %collective-permute-start.14 = (bf16[4,128,256]{2,1,0:T(8,128)(2,1)S(1)}, bf16[4,128,256]{2,1,0:T(8,128)(2,1)S(1)}, u32[]{:S(2)}, u32[]{:S(2)}) collective-permute-start(bf16[4,128,256]{2,1,0:T(8,128)(2,1)S(1)} %get-tuple-element.63), channel_id=1, source_target_pairs={{0,8},{8,0},{16,24},{24,16},{1,9},{9,1},{17,25},{25,17},{2,10},{10... | collective-permute-start | bytes 786440 | tf_op jit(solution)/shard_map/ppermute | solution.py:378
  28.4 13.0 %collective-permute-start.15 = (bf16[4,128,256]{2,1,0:T(8,128)(2,1)S(1)}, bf16[4,128,256]{2,1,0:T(8,128)(2,1)S(1)}, u32[]{:S(2)}, u32[]{:S(2)}) collective-permute-start(bf16[4,128,256]{2,1,0:T(8,128)(2,1)S(1)} %get-tuple-element.64), channel_id=1, source_target_pairs={{0,16},{8,24},{16,0},{24,8},{1,17},{9,25},{17,1},{25,9},{2,18},{10... | collective-permute-start | bytes 786440 | tf_op jit(solution)/shard_map/ppermute | solution.py:378
  30.2 13.6 %collective-permute-start.16 = (bf16[4,128,256]{2,1,0:T(8,128)(2,1)S(1)}, bf16[4,128,256]{2,1,0:T(8,128)(2,1)S(1)}, u32[]{:S(2)}, u32[]{:S(2)}) collective-permute-start(bf16[4,128,256]{2,1,0:T(8,128)(2,1)S(1)} %get-tuple-element.65), channel_id=1, source_target_pairs={{0,24},{8,16},{16,8},{24,0},{1,25},{9,17},{17,9},{25,1},{2,26},{10... | collective-permute-start | bytes 786440 | tf_op jit(solution)/shard_map/ppermute | solution.py:378
  32.0 6.9 %collective-permute-start.11 = (bf16[4,64,256]{2,1,0:T(8,128)(2,1)S(1)}, bf16[4,64,256]{2,1,0:T(8,128)(2,1)S(1)}, u32[]{:S(2)}, u32[]{:S(2)}) collective-permute-start(bf16[4,64,256]{2,1,0:T(8,128)(2,1)S(1)} %get-tuple-element.58), channel_id=1, source_target_pairs={{0,2},{1,3},{2,0},{3,1},{4,6},{5,7},{6,4},{7,5},{8,10},{9,11},{10,... | collective-permute-start | bytes 393224 | tf_op jit(solution)/shard_map/ppermute | solution.py:378
  39.0 8.2 %collective-permute-start.13 = (bf16[4,64,256]{2,1,0:T(8,128)(2,1)S(1)}, bf16[4,64,256]{2,1,0:T(8,128)(2,1)S(1)}, u32[]{:S(2)}, u32[]{:S(2)}) collective-permute-start(bf16[4,64,256]{2,1,0:T(8,128)(2,1)S(1)} %get-tuple-element.61), channel_id=1, source_target_pairs={{0,4},{1,5},{2,6},{3,7},{4,0},{5,1},{6,2},{7,3},{8,12},{9,13},{10,... | collective-permute-start | bytes 393224 | tf_op jit(solution)/shard_map/ppermute | solution.py:378
  39.7 7.4 %collective-permute-start.12 = (bf16[4,64,256]{2,1,0:T(8,128)(2,1)S(1)}, bf16[4,64,256]{2,1,0:T(8,128)(2,1)S(1)}, u32[]{:S(2)}, u32[]{:S(2)}) collective-permute-start(bf16[4,64,256]{2,1,0:T(8,128)(2,1)S(1)} %get-tuple-element.60.refs_4_), channel_id=1, source_target_pairs={{0,2},{1,3},{2,0},{3,1},{4,6},{5,7},{6,4},{7,5},{8,10},{9,11},{10,... | collective-permute-start | bytes 393224 | tf_op jit(solution)/shard_map/ppermute | solution.py:378
  44.0 10.3 %collective-permute-start.19 = (bf16[512,256]{1,0:T(8,128)(2,1)S(1)}, bf16[512,256]{1,0:T(8,128)(2,1)S(1)}, u32[]{:S(2)}, u32[]{:S(2)}) collective-permute-start(bf16[512,256]{1,0:T(8,128)(2,1)S(1)} %get-tuple-element.66.refs_3_.refs_10_), channel_id=1, source_target_pairs={{0,24},{8,16},{16,8},{24,0},{1,25},{9,17},{17,9},{25,1},{2,26},{10... | collective-permute-start | bytes 786440 | tf_op jit(solution)/shard_map/ppermute | solution.py:378
  47.2 7.1 %collective-permute-start.18 = (bf16[256,256]{1,0:T(8,128)(2,1)S(1)}, bf16[256,256]{1,0:T(8,128)(2,1)S(1)}, u32[]{:S(2)}, u32[]{:S(2)}) collective-permute-start(bf16[256,256]{1,0:T(8,128)(2,1)S(1)} %get-tuple-element.68.refs_0_), channel_id=1, source_target_pairs={{0,4},{1,5},{2,6},{3,7},{4,0},{5,1},{6,2},{7,3},{8,12},{9,13},{10,... | collective-permute-start | bytes 393224 | tf_op jit(solution)/shard_map/ppermute | solution.py:378
  48.8 8.6 %collective-permute-start.17 = (bf16[256,256]{1,0:T(8,128)(2,1)S(1)}, bf16[256,256]{1,0:T(8,128)(2,1)S(1)}, u32[]{:S(2)}, u32[]{:S(2)}) collective-permute-start(bf16[256,256]{1,0:T(8,128)(2,1)S(1)} %get-tuple-element.68.refs_0_), channel_id=1, source_target_pairs={{0,2},{1,3},{2,0},{3,1},{4,6},{5,7},{6,4},{7,5},{8,10},{9,11},{10,... | collective-permute-start | bytes 393224 | tf_op jit(solution)/shard_map/ppermute | solution.py:378
  54.3 5.0 %collective-permute-start.20 = (bf16[1,256,256]{2,1,0:T(8,128)(2,1)S(1)}, bf16[1,256,256]{2,1,0:T(8,128)(2,1)S(1)}, u32[]{:S(2)}, u32[]{:S(2)}) collective-permute-start(bf16[1,256,256]{2,1,0:T(8,128)(2,1)S(1)} %shard_map.95.refs_2_), channel_id=1, source_target_pairs={{0,2},{1,3},{2,0},{3,1},{4,6},{5,7},{6,4},{7,5},{8,10},{9,11},{10,... | collective-permute-start | bytes 393224 | tf_op jit(solution)/shard_map/ppermute | solution.py:378
  55.3 6.6 %collective-permute-start.25 = (bf16[512,256]{1,0:T(8,128)(2,1)S(1)}, bf16[512,256]{1,0:T(8,128)(2,1)S(1)}, u32[]{:S(2)}, u32[]{:S(2)}) collective-permute-start(bf16[512,256]{1,0:T(8,128)(2,1)S(1)} %get-tuple-element.66.refs_3_.refs_10_), channel_id=1, source_target_pairs={{0,16},{8,24},{16,0},{24,8},{1,17},{9,25},{17,1},{25,9},{2,18},{10... | collective-permute-start | bytes 786440 | tf_op jit(solution)/shard_map/ppermute | solution.py:378
  56.8 6.4 %collective-permute-start.24 = (bf16[512,256]{1,0:T(8,128)(2,1)S(1)}, bf16[512,256]{1,0:T(8,128)(2,1)S(1)}, u32[]{:S(2)}, u32[]{:S(2)}) collective-permute-start(bf16[512,256]{1,0:T(8,128)(2,1)S(1)} %get-tuple-element.66.refs_3_.refs_10_), channel_id=1, source_target_pairs={{0,8},{8,0},{16,24},{24,16},{1,9},{9,1},{17,25},{25,17},{2,10},{10... | collective-permute-start | bytes 786440 | tf_op jit(solution)/shard_map/ppermute | solution.py:378
  66.8 11.7 %collective-permute-start.30 = (bf16[4,128,256]{2,1,0:T(8,128)(2,1)S(1)}, bf16[4,128,256]{2,1,0:T(8,128)(2,1)S(1)}, u32[]{:S(2)}, u32[]{:S(2)}) collective-permute-start(bf16[4,128,256]{2,1,0:T(8,128)(2,1)S(1)} %get-tuple-element.85), channel_id=1, source_target_pairs={{0,8},{8,0},{16,24},{24,16},{1,9},{9,1},{17,25},{25,17},{2,10},{10... | collective-permute-start | bytes 786440 | tf_op jit(solution)/shard_map/ppermute | solution.py:378
  66.9 11.6 %collective-permute-start.31 = (bf16[4,128,256]{2,1,0:T(8,128)(2,1)S(1)}, bf16[4,128,256]{2,1,0:T(8,128)(2,1)S(1)}, u32[]{:S(2)}, u32[]{:S(2)}) collective-permute-start(bf16[4,128,256]{2,1,0:T(8,128)(2,1)S(1)} %get-tuple-element.86), channel_id=1, source_target_pairs={{0,16},{8,24},{16,0},{24,8},{1,17},{9,25},{17,1},{25,9},{2,18},{10... | collective-permute-start | bytes 786440 | tf_op jit(solution)/shard_map/ppermute | solution.py:378
  68.9 7.5 %collective-permute-start.27 = (bf16[4,64,256]{2,1,0:T(8,128)(2,1)S(1)}, bf16[4,64,256]{2,1,0:T(8,128)(2,1)S(1)}, u32[]{:S(2)}, u32[]{:S(2)}) collective-permute-start(bf16[4,64,256]{2,1,0:T(8,128)(2,1)S(1)} %get-tuple-element.79), channel_id=1, source_target_pairs={{0,2},{1,3},{2,0},{3,1},{4,6},{5,7},{6,4},{7,5},{8,10},{9,11},{10,... | collective-permute-start | bytes 393224 | tf_op jit(solution)/shard_map/ppermute | solution.py:378
  72.5 9.6 %collective-permute-start.32 = (bf16[4,128,256]{2,1,0:T(8,128)(2,1)S(1)}, bf16[4,128,256]{2,1,0:T(8,128)(2,1)S(1)}, u32[]{:S(2)}, u32[]{:S(2)}) collective-permute-start(bf16[4,128,256]{2,1,0:T(8,128)(2,1)S(1)} %get-tuple-element.87), channel_id=1, source_target_pairs={{0,24},{8,16},{16,8},{24,0},{1,25},{9,17},{17,9},{25,1},{2,26},{10... | collective-permute-start | bytes 786440 | tf_op jit(solution)/shard_map/ppermute | solution.py:378
  76.4 8.8 %collective-permute-start.29 = (bf16[4,64,256]{2,1,0:T(8,128)(2,1)S(1)}, bf16[4,64,256]{2,1,0:T(8,128)(2,1)S(1)}, u32[]{:S(2)}, u32[]{:S(2)}) collective-permute-start(bf16[4,64,256]{2,1,0:T(8,128)(2,1)S(1)} %get-tuple-element.82), channel_id=1, source_target_pairs={{0,4},{1,5},{2,6},{3,7},{4,0},{5,1},{6,2},{7,3},{8,12},{9,13},{10,... | collective-permute-start | bytes 393224 | tf_op jit(solution)/shard_map/ppermute | solution.py:378
  76.8 8.4 %collective-permute-start.28 = (bf16[4,64,256]{2,1,0:T(8,128)(2,1)S(1)}, bf16[4,64,256]{2,1,0:T(8,128)(2,1)S(1)}, u32[]{:S(2)}, u32[]{:S(2)}) collective-permute-start(bf16[4,64,256]{2,1,0:T(8,128)(2,1)S(1)} %get-tuple-element.81.refs_3_.refs_4_), channel_id=1, source_target_pairs={{0,2},{1,3},{2,0},{3,1},{4,6},{5,7},{6,4},{7,5},{8,10},{9,11},{10,... | collective-permute-start | bytes 393224 | tf_op jit(solution)/shard_map/ppermute | solution.py:378
  (14 other events, 130.4 us)
